TPU v7x, 32 devices: a whole 2x2x4 slice. The times are simulated.
32 devices in a mesh: dp: 4 (over y, core), tensor: 8 (over z, x).
Axes of the slice: x: 2, y: 2, z: 4, core: 2. Of those that a mesh axis runs over, the one named last changes fastest.
Arguments:
- frames: bfloat16 [16, 1536, 1280], P('dp', 'tensor'), may hold values from -6 to 6
- upstream: bfloat16 [16, 1536, 1280], P('dp', 'tensor'), may hold values from -6 to 6
- clip_frame_length: int32 [16], P('dp'), may hold values from 512 to 1536, as said below
- clip_adapter_index: int32 [16, 6], P('dp'), may hold values from 0 to 7
- attention_norm_gain: float32 [1280], replicated, may hold values from 0.1 to 1.9
- feedforward_norm_gain: float32 [1280], replicated, may hold values from 0.1 to 1.9
- query_key_value_frozen_weight: bfloat16 [3, 1280, 1280], P(None, 'dp', 'tensor'), may hold values from -0.15625 to 0.15625
- output_frozen_weight: bfloat16 [1280, 1280], P('tensor', 'dp'), may hold values from -0.5 to 0.5
- first_ffn_frozen_weight: bfloat16 [1280, 5120], P('dp', 'tensor'), may hold values from -0.15625 to 0.15625
- second_ffn_frozen_weight: bfloat16 [5120, 1280], P('tensor', 'dp'), may hold values from -0.078125 to 0.078125
- query_key_value_adapter_down: bfloat16 [3, 8, 1280, 16], replicated, may hold values from -0.15625 to 0.15625
- query_key_value_adapter_up: bfloat16 [3, 8, 16, 1280], P(None, None, None, 'tensor'), may hold values from -1.5 to 1.5
- output_adapter_down: bfloat16 [8, 1280, 16], P(None, 'tensor'), may hold values from -0.5 to 0.5
- output_adapter_up: bfloat16 [8, 16, 1280], replicated, may hold values from -1.5 to 1.5
- first_ffn_adapter_down: bfloat16 [8, 1280, 16], replicated, may hold values from -0.15625 to 0.15625
- first_ffn_adapter_up: bfloat16 [8, 16, 5120], P(None, None, 'tensor'), may hold values from -1.5 to 1.5
- second_ffn_adapter_down: bfloat16 [8, 5120, 16], P(None, 'tensor'), may hold values from -0.078125 to 0.078125
- second_ffn_adapter_up: bfloat16 [8, 16, 1280], replicated, may hold values from -1.5 to 1.5
Outputs:
- layer_output: bfloat16 [16, 1536, 1280], P('dp', 'tensor')
- frames_grad: float32 [16, 1536, 1280], P('dp', 'tensor')
- qkv_grad_a: float32 [3, 8, 1280, 16], P(None, None, 'tensor', 'dp')
- qkv_grad_b: float32 [3, 8, 16, 1280], P(None, None, 'dp', 'tensor')
- out_grad_a: float32 [8, 1280, 16], P(None, 'tensor', 'dp')
- out_grad_b: float32 [8, 16, 1280], P(None, 'dp', 'tensor')
- fc1_grad_a: float32 [8, 1280, 16], P(None, 'tensor', 'dp')
- fc1_grad_b: float32 [8, 16, 5120], P(None, 'dp', 'tensor')
- fc2_grad_a: float32 [8, 5120, 16], P(None, 'tensor', 'dp')
- fc2_grad_b: float32 [8, 16, 1280], P(None, 'dp', 'tensor')
Inputs may be any that keep to these rules, and one draw needn't show every extreme that they name: `clip_frame_length`: each clip's valid frames are the first of its buffer; some clip in every draw has all 1536.
All inputs are finite; a program needn't handle non-finite values.
Results may differ from a plain program's by a relative error of at most 0.04.
Values may be sent and summed in bfloat16 or wider, within the bound.
No kernel may reach another device: no remote copies, remote signals or barrier semaphores. Data moves between devices by JAX's collectives and lax.ppermute only.
A program may use at most 320 MiB of HBM per device.

v0:
```python
from functools import partial

import jax
import jax.numpy as jnp
from jax import lax
from jax.sharding import PartitionSpec as P

HEAD = 80
MB_CLIPS = 2


def coarse_product(left, right):
    return jnp.dot(left, right, preferred_element_type=jnp.float32)


def coarse_backward(left, right):
    return lax.dot_general(
        left, right, (((1,), (1,)), ((), ())), preferred_element_type=jnp.float32
    )


def coarse_outer(left, right):
    return lax.dot_general(
        left, right, (((0,), (0,)), ((), ())), preferred_element_type=jnp.float32
    )


def halves(values):
    leading = values.astype(jnp.bfloat16)
    trailing = (values - leading.astype(jnp.float32)).astype(jnp.bfloat16)
    return (leading, trailing)


def wide_product(wide, right_low):
    leading, trailing = halves(wide)
    return coarse_product(leading, right_low) + coarse_product(trailing, right_low)


def wide_back(wide, right_low):
    leading, trailing = halves(wide)
    return coarse_backward(leading, right_low) + coarse_backward(trailing, right_low)


def outer_low(left_low, wide):
    leading, trailing = halves(wide)
    return coarse_outer(left_low, leading) + coarse_outer(left_low, trailing)


def outer_wide(wide, right_low):
    leading, trailing = halves(wide)
    return coarse_outer(leading, right_low) + coarse_outer(trailing, right_low)


def layer_norm(values, gain):
    center = values - jnp.mean(values, axis=-1, keepdims=True)
    spread = jnp.mean(center * center, axis=-1, keepdims=True)
    return center * lax.rsqrt(spread + 1e-05) * gain


def select_adapter(stack, index):
    return lax.dynamic_index_in_dim(stack, index, 0, keepdims=False)


def place(stack, index, value_rows):
    marks = (jnp.arange(stack.shape[0]) == index).astype(jnp.float32)
    return stack + marks.reshape((-1,) + (1,) * value_rows.ndim) * value_rows[None]


def exact_gelu(values):
    return jax.nn.gelu(values, approximate=False)


def attend_block(query_blk, keys_all, values_all, length, extent):
    keys_used = keys_all[:extent]
    values_used = values_all[:extent]
    scores = jnp.einsum(
        "qhd,khd->hqk", query_blk, keys_used, preferred_element_type=jnp.float32
    ) * HEAD ** (-0.5)
    live = jnp.arange(extent) < length
    scores = jnp.where(live[None, None, :], scores, -1e30)
    top = jnp.max(scores, axis=-1, keepdims=True)
    expo = jnp.exp(scores - top)
    total = jnp.sum(expo, axis=-1, keepdims=True)
    weights_low = (expo / total).astype(jnp.bfloat16)
    mixed_heads = jnp.einsum(
        "hqk,khd->qhd", weights_low, values_used, preferred_element_type=jnp.float32
    )
    return (mixed_heads.astype(jnp.bfloat16), top + jnp.log(total))


def attend_back_block(query_blk, keys_all, values_all, dmixed_blk, lse_blk, length, extent):
    frames_total = keys_all.shape[0]
    keys_used = keys_all[:extent]
    values_used = values_all[:extent]
    scores = jnp.einsum(
        "qhd,khd->hqk", query_blk, keys_used, preferred_element_type=jnp.float32
    ) * HEAD ** (-0.5)
    live = jnp.arange(extent) < length
    scores = jnp.where(live[None, None, :], scores, -1e30)
    weights_full = jnp.exp(scores - lse_blk)
    weights_low = weights_full.astype(jnp.bfloat16)
    dvalues = jnp.einsum(
        "hqk,qhd->khd", weights_low, dmixed_blk, preferred_element_type=jnp.float32
    )
    dweights = jnp.einsum(
        "qhd,khd->hqk", dmixed_blk, values_used, preferred_element_type=jnp.float32
    )
    delta = jnp.sum(weights_full * dweights, axis=-1, keepdims=True)
    dscores = (weights_full * (dweights - delta)).astype(jnp.bfloat16)
    dquery = jnp.einsum(
        "hqk,khd->qhd", dscores, keys_used, preferred_element_type=jnp.float32
    ) * HEAD ** (-0.5)
    dkeys = jnp.einsum(
        "hqk,qhd->khd", dscores, query_blk, preferred_element_type=jnp.float32
    ) * HEAD ** (-0.5)
    padding = ((0, frames_total - extent), (0, 0), (0, 0))
    return (dquery, jnp.pad(dkeys, padding), jnp.pad(dvalues, padding))


def attend_clip(query, keys_all, values_all, length):
    frames_total = query.shape[0]
    span = min(512, frames_total)
    count = frames_total // span
    mixed_list = []
    lse_list = []
    for number in range(count):
        query_blk = query[number * span : (number + 1) * span]
        mixed_blk, lse_blk = attend_block(query_blk, keys_all, values_all, length, frames_total)
        mixed_list.append(mixed_blk)
        lse_list.append(lse_blk)
    return (jnp.concatenate(mixed_list, axis=0), lse_list)


def attend_clip_back(query, keys_all, values_all, dmixed, lse_list, length):
    frames_total = query.shape[0]
    span = min(512, frames_total)
    count = frames_total // span
    dquery_list = []
    dkeys = jnp.zeros(keys_all.shape, jnp.float32)
    dvalues = jnp.zeros(values_all.shape, jnp.float32)
    for number in range(count):
        query_blk = query[number * span : (number + 1) * span]
        dmixed_blk = dmixed[number * span : (number + 1) * span]
        dquery_blk, dkeys_blk, dvalues_blk = attend_back_block(
            query_blk, keys_all, values_all, dmixed_blk, lse_list[number], length, frames_total
        )
        dquery_list.append(dquery_blk)
        dkeys = dkeys + dkeys_blk
        dvalues = dvalues + dvalues_blk
    return (jnp.concatenate(dquery_list, axis=0), dkeys, dvalues)


def fetch_frozen(
    query_key_value_frozen_weight,
    output_frozen_weight,
    first_ffn_frozen_weight,
    second_ffn_frozen_weight,
):
    return (
        lax.all_gather(query_key_value_frozen_weight, "dp", axis=1, tiled=True),
        lax.all_gather(output_frozen_weight, "dp", axis=1, tiled=True),
        lax.all_gather(first_ffn_frozen_weight, "dp", axis=0, tiled=True),
        lax.all_gather(second_ffn_frozen_weight, "dp", axis=1, tiled=True),
    )


def spread_rows(first_normalized):
    return lax.all_gather(first_normalized, "tensor", axis=1, tiled=True)


def collect_rows(terms):
    return lax.psum_scatter(terms, "tensor", scatter_dimension=1, tiled=True)


def spread_grads(grads_low):
    return lax.all_gather(grads_low, "tensor", axis=1, tiled=True)


def collect_grads(terms):
    return lax.psum_scatter(terms, "tensor", scatter_dimension=1, tiled=True)


def body(
    frames,
    upstream,
    clip_frame_length,
    clip_adapter_index,
    attention_norm_gain,
    feedforward_norm_gain,
    query_key_value_frozen_weight,
    output_frozen_weight,
    first_ffn_frozen_weight,
    second_ffn_frozen_weight,
    query_key_value_adapter_down,
    query_key_value_adapter_up,
    output_adapter_down,
    output_adapter_up,
    first_ffn_adapter_down,
    first_ffn_adapter_up,
    second_ffn_adapter_down,
    second_ffn_adapter_up,
):
    clips_here, local_frames, width = frames.shape
    frames_total = local_frames * lax.axis_size("tensor")
    head_cols = query_key_value_frozen_weight.shape[2]
    local_heads = head_cols // HEAD
    micro_count = clips_here // MB_CLIPS
    positions = lax.axis_index("tensor") * local_frames + jnp.arange(local_frames)

    def prepare(frozen_now):
        qkv_full, out_full, first_ffn_weight_full, second_ffn_weight_full = frozen_now
        (
            first_ffn_weight_used,
            second_ffn_weight_used,
            first_ffn_second_factor_used,
            second_ffn_first_factor_used,
        ) = (
            first_ffn_weight_full,
            second_ffn_weight_full,
            first_ffn_adapter_up,
            second_ffn_adapter_down,
        )
        return (
            qkv_full,
            out_full,
            first_ffn_weight_used,
            second_ffn_weight_used,
            first_ffn_second_factor_used,
            second_ffn_first_factor_used,
        )

    def micro_step(grads, clip_item):
        frames_mb, upstream_mb, lengths_mb, picks_mb = clip_item
        qkv_a_acc, qkv_b_acc, out_a_acc, out_b_acc, fc1_a_acc, fc1_b_acc, fc2_a_acc, fc2_b_acc = (
            grads
        )
        qkv_a_parts = [qkv_a_acc[part] for part in range(3)]
        qkv_b_parts = [qkv_b_acc[part] for part in range(3)]
        frozen_now = prepare(
            fetch_frozen(
                query_key_value_frozen_weight,
                output_frozen_weight,
                first_ffn_frozen_weight,
                second_ffn_frozen_weight,
            )
        )
        (
            qkv_full,
            out_full,
            first_ffn_weight_used,
            second_ffn_weight_used,
            first_ffn_second_factor_used,
            second_ffn_first_factor_used,
        ) = frozen_now
        valid = (positions[None, :] < lengths_mb[:, None])[:, :, None]
        rows_in = frames_mb.astype(jnp.float32)
        normed_all = spread_rows(layer_norm(rows_in, attention_norm_gain).astype(jnp.bfloat16))
        attn_saved = []
        attn_terms = []
        for slot in range(MB_CLIPS):
            length = lengths_mb[slot]
            adapter_picks = picks_mb[slot]
            source = normed_all[slot]
            projected = []
            inners = []
            for part in range(3):
                entry_input = select_adapter(
                    query_key_value_adapter_down[part], adapter_picks[part]
                )
                exit_input = select_adapter(query_key_value_adapter_up[part], adapter_picks[part])
                inner = coarse_product(source, entry_input)
                value_rows = coarse_product(source, qkv_full[part]) + wide_product(
                    inner, exit_input
                )
                projected.append(
                    value_rows.astype(jnp.bfloat16).reshape(frames_total, local_heads, HEAD)
                )
                inners.append(inner)
            mixed_heads, lse_list = attend_clip(projected[0], projected[1], projected[2], length)
            mixed_heads = mixed_heads.reshape(frames_total, head_cols)
            entry_output = select_adapter(output_adapter_down, adapter_picks[3])
            exit_output = select_adapter(output_adapter_up, adapter_picks[3])
            inner_out = coarse_product(mixed_heads, entry_output)
            attn_terms.append(
                coarse_product(mixed_heads, out_full) + wide_product(inner_out, exit_output)
            )
            attn_saved.append((projected, inners, mixed_heads, lse_list, inner_out))
        hidden = rows_in + collect_rows(jnp.stack(attn_terms))
        normed2_low = layer_norm(hidden, feedforward_norm_gain).astype(jnp.bfloat16)
        normed2_all = spread_rows(normed2_low)
        ffn_saved = []
        ffn_terms = []
        for slot in range(MB_CLIPS):
            adapter_picks = picks_mb[slot]
            second_source = normed2_all[slot]
            inner_up_projection = coarse_product(
                second_source, select_adapter(first_ffn_adapter_down, adapter_picks[4])
            )
            upper_hidden = coarse_product(second_source, first_ffn_weight_used) + wide_product(
                inner_up_projection, select_adapter(first_ffn_second_factor_used, adapter_picks[4])
            )
            active_rows = exact_gelu(upper_hidden).astype(jnp.bfloat16)
            inner_down_projection = coarse_product(
                active_rows, select_adapter(second_ffn_first_factor_used, adapter_picks[5])
            )
            ffn_terms.append(
                coarse_product(active_rows, second_ffn_weight_used)
                + wide_product(
                    inner_down_projection, select_adapter(second_ffn_adapter_up, adapter_picks[5])
                )
            )
            ffn_saved.append(
                (inner_up_projection, upper_hidden, active_rows, inner_down_projection)
            )
        branch_output = collect_rows(jnp.stack(ffn_terms))
        layer_rows = jnp.where(valid, hidden + branch_output, 0.0).astype(jnp.bfloat16)
        (
            qkv_full,
            out_full,
            first_ffn_weight_used,
            second_ffn_weight_used,
            first_ffn_second_factor_used,
            second_ffn_first_factor_used,
        ) = prepare(
            fetch_frozen(
                query_key_value_frozen_weight,
                output_frozen_weight,
                first_ffn_frozen_weight,
                second_ffn_frozen_weight,
            )
        )
        seed = jnp.where(valid, upstream_mb.astype(jnp.float32), 0.0)
        seed_all = spread_grads(seed.astype(jnp.bfloat16))
        normed2_terms = []
        for slot in range(MB_CLIPS):
            adapter_picks = picks_mb[slot]
            inner_up_projection, upper_hidden, active_rows, inner_down_projection = ffn_saved[slot]
            clip_random_seed = seed_all[slot]
            enter_down = select_adapter(second_ffn_first_factor_used, adapter_picks[5])
            inner_down_gradient = coarse_backward(
                clip_random_seed, select_adapter(second_ffn_adapter_up, adapter_picks[5])
            )
            dactive = coarse_backward(clip_random_seed, second_ffn_weight_used) + wide_back(
                inner_down_gradient, enter_down
            )
            fc2_a_acc = place(
                fc2_a_acc, adapter_picks[5], outer_low(active_rows, inner_down_gradient)
            )
            fc2_b_acc = place(
                fc2_b_acc, adapter_picks[5], outer_wide(inner_down_projection, clip_random_seed)
            )
            gelu_back = jax.vjp(exact_gelu, upper_hidden)[1]
            dupper = gelu_back(dactive)[0].astype(jnp.bfloat16)
            entry_up_weight = select_adapter(first_ffn_adapter_down, adapter_picks[4])
            dinner_up = coarse_backward(
                dupper, select_adapter(first_ffn_second_factor_used, adapter_picks[4])
            )
            normed2_terms.append(
                coarse_backward(dupper, first_ffn_weight_used)
                + wide_back(dinner_up, entry_up_weight)
            )
            fc1_a_acc = place(fc1_a_acc, adapter_picks[4], outer_low(normed2_all[slot], dinner_up))
            fc1_b_acc = place(fc1_b_acc, adapter_picks[4], outer_wide(inner_up_projection, dupper))
        dnormed2 = collect_grads(jnp.stack(normed2_terms))
        second_back = jax.vjp(partial(layer_norm, gain=feedforward_norm_gain), hidden)[1]
        dhidden = seed + second_back(dnormed2)[0]
        dattn_all = spread_grads(dhidden.astype(jnp.bfloat16))
        normed_terms = []
        for slot in range(MB_CLIPS):
            length = lengths_mb[slot]
            adapter_picks = picks_mb[slot]
            projected, inners, mixed_heads, lse_list, inner_out = attn_saved[slot]
            attention_gradient = dattn_all[slot]
            entry_output = select_adapter(output_adapter_down, adapter_picks[3])
            inner_output_gradient = coarse_backward(
                attention_gradient, select_adapter(output_adapter_up, adapter_picks[3])
            )
            dmixed = (
                coarse_backward(attention_gradient, out_full)
                + wide_back(inner_output_gradient, entry_output)
            ).astype(jnp.bfloat16)
            out_a_acc = place(
                out_a_acc, adapter_picks[3], outer_low(mixed_heads, inner_output_gradient)
            )
            out_b_acc = place(
                out_b_acc, adapter_picks[3], outer_wide(inner_out, attention_gradient)
            )
            dprojected = attend_clip_back(
                projected[0],
                projected[1],
                projected[2],
                dmixed.reshape(frames_total, local_heads, HEAD),
                lse_list,
                length,
            )
            source_low = normed_all[slot]
            normed_term = jnp.zeros((frames_total, width), jnp.float32)
            for part in range(3):
                projection_gradient = (
                    dprojected[part].astype(jnp.bfloat16).reshape(frames_total, head_cols)
                )
                entry_input = select_adapter(
                    query_key_value_adapter_down[part], adapter_picks[part]
                )
                inner_gradient = coarse_backward(
                    projection_gradient,
                    select_adapter(query_key_value_adapter_up[part], adapter_picks[part]),
                )
                normed_term = (
                    normed_term
                    + coarse_backward(projection_gradient, qkv_full[part])
                    + wide_back(inner_gradient, entry_input)
                )
                qkv_a_parts[part] = place(
                    qkv_a_parts[part], adapter_picks[part], outer_low(source_low, inner_gradient)
                )
                qkv_b_parts[part] = place(
                    qkv_b_parts[part],
                    adapter_picks[part],
                    outer_wide(inners[part], projection_gradient),
                )
            normed_terms.append(normed_term)
        dnormed = collect_grads(jnp.stack(normed_terms))
        first_back = jax.vjp(partial(layer_norm, gain=attention_norm_gain), rows_in)[1]
        dframes = dhidden + first_back(dnormed)[0]
        new_grads = (
            jnp.stack(qkv_a_parts),
            jnp.stack(qkv_b_parts),
            out_a_acc,
            out_b_acc,
            fc1_a_acc,
            fc1_b_acc,
            fc2_a_acc,
            fc2_b_acc,
        )
        return (new_grads, (layer_rows, dframes))

    first_ffn_second_factor_begin = jnp.zeros(first_ffn_adapter_up.shape, jnp.float32)
    second_ffn_first_factor_begin = jnp.zeros(second_ffn_adapter_down.shape, jnp.float32)
    start_grads = (
        jnp.zeros(query_key_value_adapter_down.shape, jnp.float32),
        jnp.zeros(query_key_value_adapter_up.shape, jnp.float32),
        jnp.zeros(output_adapter_down.shape, jnp.float32),
        jnp.zeros(output_adapter_up.shape, jnp.float32),
        jnp.zeros(first_ffn_adapter_down.shape, jnp.float32),
        first_ffn_second_factor_begin,
        second_ffn_first_factor_begin,
        jnp.zeros(second_ffn_adapter_up.shape, jnp.float32),
    )
    micro_items = (
        frames.reshape(micro_count, MB_CLIPS, local_frames, width),
        upstream.reshape(micro_count, MB_CLIPS, local_frames, width),
        clip_frame_length.reshape(micro_count, MB_CLIPS),
        clip_adapter_index.reshape(micro_count, MB_CLIPS, 6),
    )
    final_grads, stacked = lax.scan(micro_step, start_grads, micro_items)
    layer_output = stacked[0].reshape(clips_here, local_frames, width)
    frames_grad = stacked[1].reshape(clips_here, local_frames, width)
    qkv_a_sum, out_b_sum, fc1_a_sum, fc2_b_sum = (
        lax.psum_scatter(final_grads[0], "tensor", scatter_dimension=2, tiled=True),
        lax.psum_scatter(final_grads[3], "tensor", scatter_dimension=2, tiled=True),
        lax.psum_scatter(final_grads[4], "tensor", scatter_dimension=1, tiled=True),
        lax.psum_scatter(final_grads[7], "tensor", scatter_dimension=2, tiled=True),
    )
    fc1_b_sum = final_grads[5]
    fc2_a_sum = final_grads[6]
    owned = (
        lax.psum_scatter(qkv_a_sum, "dp", scatter_dimension=3, tiled=True),
        lax.psum_scatter(final_grads[1], "dp", scatter_dimension=2, tiled=True),
        lax.psum_scatter(final_grads[2], "dp", scatter_dimension=2, tiled=True),
        lax.psum_scatter(out_b_sum, "dp", scatter_dimension=1, tiled=True),
        lax.psum_scatter(fc1_a_sum, "dp", scatter_dimension=2, tiled=True),
        lax.psum_scatter(fc1_b_sum, "dp", scatter_dimension=1, tiled=True),
        lax.psum_scatter(fc2_a_sum, "dp", scatter_dimension=2, tiled=True),
        lax.psum_scatter(fc2_b_sum, "dp", scatter_dimension=1, tiled=True),
    )
    return (
        layer_output,
        frames_grad,
        owned[0],
        owned[1],
        owned[2],
        owned[3],
        owned[4],
        owned[5],
        owned[6],
        owned[7],
    )


def solution(mesh):
    placed = (
        P("dp", "tensor", None),
        P("dp", "tensor", None),
        P("dp"),
        P("dp", None),
        P(),
        P(),
        P(None, "dp", "tensor"),
        P("tensor", "dp"),
        P("dp", "tensor"),
        P("tensor", "dp"),
        P(),
        P(None, None, None, "tensor"),
        P(None, "tensor", None),
        P(),
        P(),
        P(None, None, "tensor"),
        P(None, "tensor", None),
        P(),
    )
    return jax.shard_map(
        body,
        mesh=mesh,
        in_specs=placed,
        out_specs=(
            P("dp", "tensor", None),
            P("dp", "tensor", None),
            P(None, None, "tensor", "dp"),
            P(None, None, "dp", "tensor"),
            P(None, "tensor", "dp"),
            P(None, "dp", "tensor"),
            P(None, "tensor", "dp"),
            P(None, "dp", "tensor"),
            P(None, "tensor", "dp"),
            P(None, "dp", "tensor"),
        ),
        check_vma=False,
    )
```

profile of v0, /device:TPU:0, one launch (start us, length us, event | category | flops | bytes accessed | tf_op | source)
XLA Modules:
  0.0 3923.1 jit_solution(4692441482681352161)
XLA Ops:
  13.8 3451.2 %while.29 = (s32[]{:T(128)}, f32[3,8,1280,16]{2,3,1,0:T(8,128)}, f32[3,8,16,160]{3,2,1,0:T(8,128)}, f32[8,160,16]{1,2,0:T(8,128)}, f32[8,16,1280]{2,1,0:T(8,128)...) while((s32[]{:T(128)}, f32[3,8,1280,16]{2,3,1,0:T(8,128)}, ...), condition=%wide.region_31.32_spmd.clone, body=%wide.region_0.31_spmd.clone.sunk | while | flops 44444041216 | bytes 2853088000 | solution.py:456
  67.7 100.1 %all-gather.12.cloned.1.call-done = bf16[2,1536,1280]{2,1,0:T(8,128)(2,1)} async-done(((bf16[2,192,1280]{2,1,0:T(8,128)(2,1)}), bf16[2,1536,1280]{2,1,0:T(8,128)(2,1)}) %all-gather.12.cloned.1.call-update) | async-done | bytes 7864336 | tf_op jit(solution)/shard_map/while/body/eval_jaxpr/all_gather | solution.py:168
  255.2 246.0 %reduce-scatter.49.cloned.1.call-done = f32[2,192,1280]{2,1,0:T(8,128)} async-done(((f32[2,1536,1280]{2,1,0:T(8,128)}), f32[2,192,1280]{2,1,0:T(8,128)}) %reduce-scatter.49.cloned.1.call-update) | async-done | bytes 1966096 | tf_op jit(solution)/shard_map/while/body/eval_jaxpr/reduce_scatter | solution.py:172
  514.0 106.8 %all-gather.22.cloned.1.call-done = bf16[2,1536,1280]{2,1,0:T(8,128)(2,1)} async-done(((bf16[2,192,1280]{2,1,0:T(8,128)(2,1)}), bf16[2,1536,1280]{2,1,0:T(8,128)(2,1)}) %all-gather.22.cloned.1.call-update) | async-done | bytes 7864336 | tf_op jit(solution)/shard_map/while/body/eval_jaxpr/all_gather | solution.py:176
  626.3 14.1 all-gather.20.cloned.1.call-done
  660.7 100.2 %all-gather.18.cloned.1.call-done = bf16[2,1536,1280]{2,1,0:T(8,128)(2,1)} async-done(((bf16[2,192,1280]{2,1,0:T(8,128)(2,1)}), bf16[2,1536,1280]{2,1,0:T(8,128)(2,1)}) %all-gather.18.cloned.1.call-update) | async-done | bytes 7864336 | tf_op jit(solution)/shard_map/while/body/eval_jaxpr/all_gather | solution.py:168
  849.6 251.2 %reduce-scatter.51.cloned.1.call-done = f32[2,192,1280]{2,1,0:T(8,128)} async-done(((f32[2,1536,1280]{2,1,0:T(8,128)}), f32[2,192,1280]{2,1,0:T(8,128)}) %reduce-scatter.51.cloned.1.call-update) | async-done | bytes 1966096 | tf_op jit(solution)/shard_map/while/body/eval_jaxpr/reduce_scatter | solution.py:180
  1134.1 12.1 pad_maximum_fusion.48
  1146.3 77.6 %all-gather.24.cloned.1.call-done = bf16[2,1536,1280]{2,1,0:T(8,128)(2,1)} async-done(((bf16[2,192,1280]{2,1,0:T(8,128)(2,1)}), bf16[2,1536,1280]{2,1,0:T(8,128)(2,1)}) %all-gather.24.cloned.1.call-update) | async-done | bytes 7864336 | tf_op jit(solution)/shard_map/while/body/eval_jaxpr/all_gather | solution.py:176
  1455.1 21.4 reduce-scatter.53.cloned.1.call-done
  1502.2 228.3 %reduce-scatter.55.cloned.1.call-done = f32[2,192,1280]{2,1,0:T(8,128)} async-done(((f32[2,1536,1280]{2,1,0:T(8,128)}), f32[2,192,1280]{2,1,0:T(8,128)}) %reduce-scatter.55.cloned.1.call-update) | async-done | bytes 1966096 | tf_op jit(solution)/shard_map/while/body/eval_jaxpr/reduce_scatter | solution.py:180
  1789.6 98.1 %all-gather.12.cloned.1.call-done = bf16[2,1536,1280]{2,1,0:T(8,128)(2,1)} async-done(((bf16[2,192,1280]{2,1,0:T(8,128)(2,1)}), bf16[2,1536,1280]{2,1,0:T(8,128)(2,1)}) %all-gather.12.cloned.1.call-update) | async-done | bytes 7864336 | tf_op jit(solution)/shard_map/while/body/eval_jaxpr/all_gather | solution.py:168
  1975.2 246.0 %reduce-scatter.49.cloned.1.call-done = f32[2,192,1280]{2,1,0:T(8,128)} async-done(((f32[2,1536,1280]{2,1,0:T(8,128)}), f32[2,192,1280]{2,1,0:T(8,128)}) %reduce-scatter.49.cloned.1.call-update) | async-done | bytes 1966096 | tf_op jit(solution)/shard_map/while/body/eval_jaxpr/reduce_scatter | solution.py:172
  2233.6 107.2 %all-gather.22.cloned.1.call-done = bf16[2,1536,1280]{2,1,0:T(8,128)(2,1)} async-done(((bf16[2,192,1280]{2,1,0:T(8,128)(2,1)}), bf16[2,1536,1280]{2,1,0:T(8,128)(2,1)}) %all-gather.22.cloned.1.call-update) | async-done | bytes 7864336 | tf_op jit(solution)/shard_map/while/body/eval_jaxpr/all_gather | solution.py:176
  2346.4 14.1 all-gather.20.cloned.1.call-done
  2380.8 100.2 %all-gather.18.cloned.1.call-done = bf16[2,1536,1280]{2,1,0:T(8,128)(2,1)} async-done(((bf16[2,192,1280]{2,1,0:T(8,128)(2,1)}), bf16[2,1536,1280]{2,1,0:T(8,128)(2,1)}) %all-gather.18.cloned.1.call-update) | async-done | bytes 7864336 | tf_op jit(solution)/shard_map/while/body/eval_jaxpr/all_gather | solution.py:168
  2569.8 251.2 %reduce-scatter.51.cloned.1.call-done = f32[2,192,1280]{2,1,0:T(8,128)} async-done(((f32[2,1536,1280]{2,1,0:T(8,128)}), f32[2,192,1280]{2,1,0:T(8,128)}) %reduce-scatter.51.cloned.1.call-update) | async-done | bytes 1966096 | tf_op jit(solution)/shard_map/while/body/eval_jaxpr/reduce_scatter | solution.py:180
  2866.1 77.9 %all-gather.24.cloned.1.call-done = bf16[2,1536,1280]{2,1,0:T(8,128)(2,1)} async-done(((bf16[2,192,1280]{2,1,0:T(8,128)(2,1)}), bf16[2,1536,1280]{2,1,0:T(8,128)(2,1)}) %all-gather.24.cloned.1.call-update) | async-done | bytes 7864336 | tf_op jit(solution)/shard_map/while/body/eval_jaxpr/all_gather | solution.py:176
  3175.3 21.5 reduce-scatter.53.cloned.1.call-done
  3223.3 227.4 %reduce-scatter.55.cloned.1.call-done = f32[2,192,1280]{2,1,0:T(8,128)} async-done(((f32[2,1536,1280]{2,1,0:T(8,128)}), f32[2,192,1280]{2,1,0:T(8,128)}) %reduce-scatter.55.cloned.1.call-update) | async-done | bytes 1966096 | tf_op jit(solution)/shard_map/while/body/eval_jaxpr/reduce_scatter | solution.py:180
  3513.9 21.3 reduce-scatter.43.cloned.1.call-done
  3537.4 62.5 %reduce-scatter.45.cloned.1.call-done = f32[160,128]{1,0:T(8,128)} async-done(((f32[1280,128]{1,0:T(8,128)}), f32[160,128]{1,0:T(8,128)}) %reduce-scatter.45.cloned.1.call-update) | async-done | bytes 81936
  3602.1 62.2 %reduce-scatter.47.cloned.1.call-done = f32[160,128]{1,0:T(8,128)} async-done(((f32[1280,128]{1,0:T(8,128)}), f32[160,128]{1,0:T(8,128)}) %reduce-scatter.47.cloned.1.call-update) | async-done | bytes 81936
  3666.5 67.6 %reduce-scatter.41.cloned.1.call-done = f32[160,384]{1,0:T(8,128)} async-done(((f32[1280,384]{1,0:T(8,128)}), f32[160,384]{1,0:T(8,128)}) %reduce-scatter.41.cloned.1.call-update) | async-done | bytes 245776
  3737.5 17.8 reduce-scatter.29.cloned.1.call-done
  3756.7 22.1 reduce-scatter.27.cloned.1.call-done
  3780.3 21.3 reduce-scatter.35.cloned.1.call-done
  3803.2 21.2 reduce-scatter.37.cloned.1.call-done
  3826.0 20.5 reduce-scatter.31.cloned.1.call-done
  3847.8 20.7 reduce-scatter.33.cloned.1.call-done
  3869.9 20.7 reduce-scatter.39.cloned.1.call-done
  3891.9 21.9 reduce-scatter.25.cloned.1.call-done
  (1611 shorter events, 1166.4 us)
Async XLA Ops:
  14.6 153.2 %all-gather.12.cloned.1.call-start = ((), (), s32[]{:S(2)}) async-start(), calls=%async_computation.28 | async-start | bytes 8847360 | tf_op jit(solution)/shard_map/while/body/eval_jaxpr/all_gather | solution.py:168
  20.5 480.7 %reduce-scatter.49.cloned.1.call-start = ((), (), s32[]{:S(2)}) async-start(), calls=%async_computation.31 | async-start | bytes 17694720 | tf_op jit(solution)/shard_map/while/body/eval_jaxpr/reduce_scatter | solution.py:172
  251.8 369.0 %all-gather.22.cloned.1.call-start = ((), (), s32[]{:S(2)}) async-start(), calls=%async_computation.34 | async-start | bytes 8847360 | tf_op jit(solution)/shard_map/while/body/eval_jaxpr/all_gather | solution.py:176
  254.5 385.9 %all-gather.20.cloned.1.call-start = ((), (), s32[]{:S(2)}) async-start(), calls=%async_computation.33 | async-start | bytes 2048000 | tf_op jit(solution)/shard_map/while/body/eval_jaxpr/all_gather | solution.py:163
  255.1 505.8 %all-gather.18.cloned.1.call-start = ((), (), s32[]{:S(2)}) async-start(), calls=%async_computation.32 | async-start | bytes 8847360 | tf_op jit(solution)/shard_map/while/body/eval_jaxpr/all_gather | solution.py:168
  505.0 275.7 %all-gather.16.cloned.1.call-start = ((), (), s32[]{:S(2)}) async-start(), calls=%async_computation.30 | async-start | bytes 2048000 | tf_op jit(solution)/shard_map/while/body/eval_jaxpr/all_gather | solution.py:162
  505.8 595.0 %reduce-scatter.51.cloned.1.call-start = ((), (), s32[]{:S(2)}) async-start(), calls=%async_computation.35 | async-start | bytes 17694720 | tf_op jit(solution)/shard_map/while/body/eval_jaxpr/reduce_scatter | solution.py:180
  849.5 374.3 %all-gather.24.cloned.1.call-start = ((), (), s32[]{:S(2)}) async-start(), calls=%async_computation.36 | async-start | bytes 8847360 | tf_op jit(solution)/shard_map/while/body/eval_jaxpr/all_gather | solution.py:176
  1106.2 370.4 %reduce-scatter.53.cloned.1.call-start = ((), (), s32[]{:S(2)}) async-start(), calls=%async_computation.37 | async-start | bytes 17694720 | tf_op jit(solution)/shard_map/while/body/eval_jaxpr/reduce_scatter | solution.py:172
  1146.2 584.3 %reduce-scatter.55.cloned.1.call-start = ((), (), s32[]{:S(2)}) async-start(), calls=%async_computation.38 | async-start | bytes 17694720 | tf_op jit(solution)/shard_map/while/body/eval_jaxpr/reduce_scatter | solution.py:180
  1738.2 149.5 %all-gather.12.cloned.1.call-start = ((), (), s32[]{:S(2)}) async-start(), calls=%async_computation.28 | async-start | bytes 8847360 | tf_op jit(solution)/shard_map/while/body/eval_jaxpr/all_gather | solution.py:168
  1744.0 477.2 %reduce-scatter.49.cloned.1.call-start = ((), (), s32[]{:S(2)}) async-start(), calls=%async_computation.31 | async-start | bytes 17694720 | tf_op jit(solution)/shard_map/while/body/eval_jaxpr/reduce_scatter | solution.py:172
  1971.8 369.0 %all-gather.22.cloned.1.call-start = ((), (), s32[]{:S(2)}) async-start(), calls=%async_computation.34 | async-start | bytes 8847360 | tf_op jit(solution)/shard_map/while/body/eval_jaxpr/all_gather | solution.py:176
  1974.6 385.9 %all-gather.20.cloned.1.call-start = ((), (), s32[]{:S(2)}) async-start(), calls=%async_computation.33 | async-start | bytes 2048000 | tf_op jit(solution)/shard_map/while/body/eval_jaxpr/all_gather | solution.py:163
  1975.2 505.8 %all-gather.18.cloned.1.call-start = ((), (), s32[]{:S(2)}) async-start(), calls=%async_computation.32 | async-start | bytes 8847360 | tf_op jit(solution)/shard_map/while/body/eval_jaxpr/all_gather | solution.py:168
  2225.1 275.5 %all-gather.16.cloned.1.call-start = ((), (), s32[]{:S(2)}) async-start(), calls=%async_computation.30 | async-start | bytes 2048000 | tf_op jit(solution)/shard_map/while/body/eval_jaxpr/all_gather | solution.py:162
  2225.7 595.3 %reduce-scatter.51.cloned.1.call-start = ((), (), s32[]{:S(2)}) async-start(), calls=%async_computation.35 | async-start | bytes 17694720 | tf_op jit(solution)/shard_map/while/body/eval_jaxpr/reduce_scatter | solution.py:180
  2569.7 374.2 %all-gather.24.cloned.1.call-start = ((), (), s32[]{:S(2)}) async-start(), calls=%async_computation.36 | async-start | bytes 8847360 | tf_op jit(solution)/shard_map/while/body/eval_jaxpr/all_gather | solution.py:176
  2826.3 370.5 %reduce-scatter.53.cloned.1.call-start = ((), (), s32[]{:S(2)}) async-start(), calls=%async_computation.37 | async-start | bytes 17694720 | tf_op jit(solution)/shard_map/while/body/eval_jaxpr/reduce_scatter | solution.py:172
  2866.0 584.7 %reduce-scatter.55.cloned.1.call-start = ((), (), s32[]{:S(2)}) async-start(), calls=%async_computation.38 | async-start | bytes 17694720 | tf_op jit(solution)/shard_map/while/body/eval_jaxpr/reduce_scatter | solution.py:180
  3465.0 70.2 %reduce-scatter.43.cloned.1.call-start = ((), (), s32[]{:S(2)}) async-start(), calls=%async_computation.25 | async-start | bytes 737280
  3473.9 126.1 %reduce-scatter.45.cloned.1.call-start = ((), (), s32[]{:S(2)}) async-start(), calls=%async_computation.26 | async-start | bytes 737280
  3481.9 182.5 %reduce-scatter.47.cloned.1.call-start = ((), (), s32[]{:S(2)}) async-start(), calls=%async_computation.27 | async-start | bytes 737280
  3489.9 244.3 %reduce-scatter.41.cloned.1.call-start = ((), (), s32[]{:S(2)}) async-start(), calls=%async_computation.24 | async-start | bytes 2211840
  3509.2 246.1 %reduce-scatter.29.cloned.1.call-start = ((), (), s32[]{:S(2)}) async-start(), calls=%async_computation.18 | async-start | bytes 163840 | tf_op jit(solution)/shard_map/reduce_scatter | solution.py:470
  3511.0 267.8 %reduce-scatter.27.cloned.1.call-start = ((), (), s32[]{:S(2)}) async-start(), calls=%async_computation.17 | async-start | bytes 491520 | tf_op jit(solution)/shard_map/reduce_scatter | solution.py:469
  3512.0 289.7 %reduce-scatter.35.cloned.1.call-start = ((), (), s32[]{:S(2)}) async-start(), calls=%async_computation.21 | async-start | bytes 409600 | tf_op jit(solution)/shard_map/reduce_scatter | solution.py:473
  3513.0 311.5 %reduce-scatter.37.cloned.1.call-start = ((), (), s32[]{:S(2)}) async-start(), calls=%async_computation.22 | async-start | bytes 409600 | tf_op jit(solution)/shard_map/reduce_scatter | solution.py:474
  3513.9 332.6 %reduce-scatter.31.cloned.1.call-start = ((), (), s32[]{:S(2)}) async-start(), calls=%async_computation.19 | async-start | bytes 163840 | tf_op jit(solution)/shard_map/reduce_scatter | solution.py:471
  3537.4 331.1 %reduce-scatter.33.cloned.1.call-start = ((), (), s32[]{:S(2)}) async-start(), calls=%async_computation.20 | async-start | bytes 163840 | tf_op jit(solution)/shard_map/reduce_scatter | solution.py:472
  3602.1 288.5 %reduce-scatter.39.cloned.1.call-start = ((), (), s32[]{:S(2)}) async-start(), calls=%async_computation.23 | async-start | bytes 163840 | tf_op jit(solution)/shard_map/reduce_scatter | solution.py:475
  3666.5 247.3 %reduce-scatter.25.cloned.1.call-start = ((), (), s32[]{:S(2)}) async-start(), calls=%async_computation.16 | async-start | bytes 491520 | tf_op jit(solution)/shard_map/reduce_scatter | solution.py:468
  (476 other events, 12341.4 us)
Sparse Core Ops, SparseCore 0:
  16.2 30.8 all-gather.13
  49.4 118.3 all-gather.11
  251.9 249.2 reduce-scatter.48
  503.2 117.5 all-gather.21
  622.2 18.1 all-gather.19
  642.5 118.3 all-gather.17
  762.5 18.1 all-gather.15
  849.7 251.1 reduce-scatter.50
  1106.3 117.4 all-gather.23
  1227.3 249.2 reduce-scatter.52
  1480.2 250.2 reduce-scatter.54
  1739.7 27.3 all-gather.13
  1769.2 118.3 all-gather.11
  1972.0 249.2 reduce-scatter.48
  2223.3 117.5 all-gather.21
  2342.3 18.1 all-gather.19
  2362.6 118.3 all-gather.17
  2482.4 18.1 all-gather.15
  2569.8 251.0 reduce-scatter.50
  2826.4 117.4 all-gather.23
  2947.5 249.2 reduce-scatter.52
  3200.4 250.2 reduce-scatter.54
Sparse Core Ops, SparseCore 1:
  3473.9 61.2 reduce-scatter.42
  3538.7 61.2 reduce-scatter.44
  3603.1 61.2 reduce-scatter.46
  3668.3 65.8 reduce-scatter.40
  3736.6 18.7 reduce-scatter.28
  3758.0 20.7 reduce-scatter.26
  3781.3 20.3 reduce-scatter.34
  3804.0 20.3 reduce-scatter.36
  3826.8 19.6 reduce-scatter.30
  3848.9 19.6 reduce-scatter.32
  3870.9 19.6 reduce-scatter.38
  3893.1 20.7 reduce-scatter.24
where the time goes:
time: 3930 us; the launch traced here: 3920 us
  waiting for transfers between devices  2690 us (68%)
  matrix products  746 us (19%)
  other arithmetic  237 us (6%)
  local copies, waits for them, and re-layouts  147 us (4%)
  loops' own time  59.3 us (2%)
    reduce_scatter x4, waiting for transfers between devices, collect_grads(): return lax.psum_scatter(terms, 'tensor', scatter_dimension=1, tiled=True)  958 us
    reduce_scatter x4, waiting for transfers between devices, collect_rows(): return lax.psum_scatter(terms, 'tensor', scatter_dimension=1, tiled=True)  535 us
    all_gather x4, waiting for transfers between devices, spread_rows(): return lax.all_gather(first_normalized, 'tensor', axis=1, tiled=True)  399 us
    all_gather x4, waiting for transfers between devices, spread_grads(): return lax.all_gather(grads_low, 'tensor', axis=1, tiled=True)  370 us
    dot_general x96, matrix products, coarse_backward(): lax.dot_general(left, right, (((1,), (1,)), ((), ())), preferred_element_...  329 us
    dot_general x96, matrix products, coarse_product(): return jnp.dot(left, right, preferred_element_type=jnp.float32)  222 us
    unnamed x16, waiting for transfers between devices  214 us
  transfers between devices with their start and end apart: 34, of which 32 were waited for; matrix products, arithmetic and copies ran while one was open for 19% of the time, Pallas kernels for 0%

commit v1 on v0

v1 whole, which is shorter than its diff:
```python
import functools

import jax
import jax.numpy as jnp
from jax import lax
from jax.sharding import PartitionSpec as P

HEAD = 80
BF = jnp.bfloat16
F32 = jnp.float32


def mm(a, b):
    return jnp.dot(a, b, preferred_element_type=F32)


def mm_nt(a, b):
    return lax.dot_general(a, b, (((1,), (1,)), ((), ())), preferred_element_type=F32)


def mm_tn(a, b):
    return lax.dot_general(a, b, (((0,), (0,)), ((), ())), preferred_element_type=F32)


def norm_parts(values):
    center = values - jnp.mean(values, axis=-1, keepdims=True)
    rate = lax.rsqrt(jnp.mean(center * center, axis=-1, keepdims=True) + 1e-5)
    return center * rate, rate


def norm_back(z, rate, grad):
    return rate * (
        grad
        - jnp.mean(grad, axis=-1, keepdims=True)
        - z * jnp.mean(grad * z, axis=-1, keepdims=True)
    )


class Place:
    def __init__(self, clips, local_frames):
        self.D, self.T = lax.axis_size("dp"), lax.axis_size("tensor")
        self.d, self.t = lax.axis_index("dp"), lax.axis_index("tensor")
        self.core = self.d % 2
        self.C, self.LF = clips, local_frames
        self.Q = self.T // (2 * clips)
        self.S = local_frames // (2 * self.Q)
        self.rows = self.T * self.S
        self.swap = [(i, i ^ 1) for i in range(self.D)]

    def swap_core(self, x):
        return lax.ppermute(x, "dp", self.swap)

    def positions(self, core, q):
        source = jnp.arange(self.T, dtype=jnp.int32)[:, None] * self.LF
        inner = (q * 2 + core) * self.S + jnp.arange(self.S, dtype=jnp.int32)[None, :]
        return (source + inner).reshape(self.rows)


def to_clip(pl_, x):
    C, LF, W = x.shape
    parts = x.reshape(C, pl_.Q, 2, pl_.S, W)
    even, odd = parts[:, :, 0], parts[:, :, 1]
    first = pl_.core == 0
    mine, theirs = jnp.where(first, even, odd), jnp.where(first, odd, even)
    got = pl_.swap_core(theirs)
    both = jnp.stack([jnp.where(first, mine, got), jnp.where(first, got, mine)])
    both = both.reshape(pl_.T, pl_.S, W)
    return lax.all_to_all(both, "tensor", 0, 0).reshape(pl_.rows, W)


def from_clip(pl_, y):
    W = y.shape[-1]
    both = lax.all_to_all(y.reshape(pl_.T, pl_.S, W), "tensor", 0, 0)
    both = both.reshape(2, pl_.C, pl_.Q, pl_.S, W)
    first = pl_.core == 0
    mine, theirs = jnp.where(first, both[0], both[1]), jnp.where(first, both[1], both[0])
    got = pl_.swap_core(theirs)
    even, odd = jnp.where(first, mine, got), jnp.where(first, got, mine)
    return jnp.stack([even, odd], axis=2).reshape(pl_.C, pl_.LF, W)


def gather_rows(x):
    return lax.all_gather(x, ("tensor", "dp"))


def group_values(pl_, x):
    out = [x, pl_.swap_core(x)]
    for step in range(1, pl_.Q):
        perm = [
            (i, i - i % pl_.Q + (i + step) % pl_.Q) for i in range(pl_.T)
        ]
        out.append(lax.ppermute(out[0], "tensor", perm))
        out.append(lax.ppermute(out[1], "tensor", perm))
    return out


def group_places(pl_):
    q = pl_.t % pl_.Q
    out = []
    for step in range(pl_.Q):
        sender = (q - step) % pl_.Q
        out.append((pl_.core, sender))
        out.append((1 - pl_.core, sender))
    return out


def group_sums(pl_, blocks):
    total = blocks[0]
    total = total + pl_.swap_core(blocks[1].astype(BF)).astype(F32)
    for step in range(1, pl_.Q):
        perm = [
            (i - i % pl_.Q + (i + step) % pl_.Q, i) for i in range(pl_.T)
        ]
        own = lax.ppermute(blocks[2 * step].astype(BF), "tensor", perm)
        other = lax.ppermute(pl_.swap_core(blocks[2 * step + 1].astype(BF)), "tensor", perm)
        total = total + own.astype(F32) + other.astype(F32)
    return total


def attend(q, k, v, bias):
    def head(item):
        qh, kh, vh = item
        scores = mm_nt(qh, kh) * HEAD**-0.5 + bias[None, :]
        top = jnp.max(scores, axis=-1, keepdims=True)
        expo = jnp.exp(scores - top)
        total = jnp.sum(expo, axis=-1, keepdims=True)
        mixed = mm((expo / total).astype(BF), vh)
        return mixed.astype(BF), top + jnp.log(total)

    return lax.map(head, (q, k, v))


def attend_back(q, k, v, bias, lse, dmixed):
    def head(item):
        qh, kh, vh, lh, dh = item
        scores = mm_nt(qh, kh) * HEAD**-0.5 + bias[None, :]
        probs = jnp.exp(scores - lh)
        dprobs = mm_nt(dh, vh)
        delta = jnp.sum(probs * dprobs, axis=-1, keepdims=True)
        dscores = (probs * (dprobs - delta)).astype(BF)
        dq = mm(dscores, kh) * HEAD**-0.5
        dk = mm_tn(dscores, qh) * HEAD**-0.5
        dv = mm_tn(probs.astype(BF), dh)
        return dq, dk, dv

    return lax.map(head, (q, k, v, lse, dmixed))


def body(
    frames,
    upstream,
    clip_frame_length,
    clip_adapter_index,
    gain1,
    gain2,
    w_qkv,
    w_out,
    w_up,
    w_down,
    qkv_a,
    qkv_b,
    out_a,
    out_b,
    fc1_a,
    fc1_b,
    fc2_a,
    fc2_b,
):
    C, LF, W = frames.shape
    pl_ = Place(C, LF)
    D, T, d, t = pl_.D, pl_.T, pl_.d, pl_.t
    Hc = w_qkv.shape[2]
    U = w_up.shape[1]
    A, R = fc1_a.shape[0], fc1_a.shape[2]
    AR = A * R
    rows = pl_.rows
    heads = W // HEAD

    meta = jnp.concatenate([clip_frame_length[:, None], clip_adapter_index], axis=1)
    metas = lax.all_gather(meta, "dp")
    g = t // pl_.Q
    here = metas[d - pl_.core + g // C, g % C]
    length, picks = here[0], here[1:]
    marks = (jnp.arange(AR)[None, :] // R == picks[:, None]).astype(F32)

    qkvo = jnp.concatenate([w_qkv.transpose(0, 2, 1), w_out[None]]).reshape(4 * Hc, W // D)
    qkvo = lax.all_to_all(qkvo, "dp", 0, 1, tiled=True)
    qkvo_low = jnp.concatenate(
        [qkv_b.transpose(0, 3, 1, 2).reshape(3, Hc, AR), out_a.transpose(1, 0, 2).reshape(1, Hc, AR)]
    ).reshape(D, 4 * Hc // D, AR)
    qkvo = jnp.concatenate([qkvo, lax.dynamic_index_in_dim(qkvo_low, d, 0, False)], axis=1)
    ffn = jnp.stack([w_up.T, w_down])
    ffn = lax.all_to_all(ffn, "dp", 1, 2, tiled=True)
    ffn_low = jnp.stack(
        [fc1_b.transpose(2, 0, 1).reshape(U, AR), fc2_a.transpose(1, 0, 2).reshape(U, AR)]
    ).reshape(2, D, U // D, AR)
    ffn = jnp.concatenate([ffn, lax.dynamic_index_in_dim(ffn_low, d, 1, False)], axis=2)
    all_qkvo = gather_rows(qkvo).reshape(T, 4, Hc, W + AR).transpose(1, 0, 2, 3).reshape(4, W, W + AR)
    all_ffn = gather_rows(ffn).transpose(1, 0, 2, 3).reshape(2, T * U, W + AR)

    flat_a = lambda a: a.transpose(1, 0, 2).reshape(W, AR)
    flat_b = lambda b: b.reshape(AR, W)

    x_in = to_clip(pl_, frames).astype(F32)
    live = (pl_.positions(pl_.core, t % pl_.Q) < length)[:, None]
    z1, rate1 = norm_parts(x_in)
    n1 = (z1 * gain1).astype(BF)
    proj, inner = [], []
    for j in range(3):
        low = (mm(n1, flat_a(qkv_a[j])) * marks[j]).astype(BF)
        proj.append(mm_nt(jnp.concatenate([n1, low], axis=1), all_qkvo[j]).astype(BF))
        inner.append(low)
    split = lambda a: a.reshape(-1, heads, HEAD).transpose(1, 0, 2)
    join = lambda a: a.transpose(1, 0, 2).reshape(-1, W)
    q = split(proj[0])
    kv = group_values(pl_, jnp.stack([split(proj[1]), split(proj[2])]))
    kv_all = jnp.concatenate(kv, axis=2)
    keys_live = jnp.concatenate([pl_.positions(c, s) for c, s in group_places(pl_)]) < length
    bias = jnp.where(keys_live, 0.0, -1e30).astype(F32)
    mixed_heads, lse = attend(q, kv_all[0], kv_all[1], bias)
    mixed = join(mixed_heads)
    both = mm(mixed, all_qkvo[3])
    inner_out = (both[:, W:] * marks[3]).astype(BF)
    hidden = x_in + both[:, :W] + mm(inner_out, flat_b(out_b))
    z2, rate2 = norm_parts(hidden)
    n2 = (z2 * gain2).astype(BF)
    inner_up = (mm(n2, flat_a(fc1_a)) * marks[4]).astype(BF)
    upper = mm_nt(jnp.concatenate([n2, inner_up], axis=1), all_ffn[0])
    cdf = 0.5 * (1.0 + lax.erf(upper * (0.5**0.5)))
    active = (upper * cdf).astype(BF)
    both = mm(active, all_ffn[1])
    inner_down = (both[:, W:] * marks[5]).astype(BF)
    branch = both[:, :W] + mm(inner_down, flat_b(fc2_b))
    layer_rows = jnp.where(live, hidden + branch, 0.0).astype(BF)
    layer_output = from_clip(pl_, layer_rows)

    seed = jnp.where(live, to_clip(pl_, upstream), 0).astype(BF)
    dinner_down = (mm_nt(seed, flat_b(fc2_b)) * marks[5]).astype(BF)
    dactive = mm_nt(jnp.concatenate([seed, dinner_down], axis=1), all_ffn[1])
    slope = cdf + upper * jnp.exp(-0.5 * upper * upper) * (1.0 / (2.0 * jnp.pi) ** 0.5)
    dupper = (dactive * slope).astype(BF)
    both = mm(dupper, all_ffn[0])
    dinner_up = (both[:, W:] * marks[4]).astype(BF)
    dn2 = both[:, :W] + mm_nt(dinner_up, flat_a(fc1_a))
    dhidden = seed.astype(F32) + norm_back(z2, rate2, dn2 * gain2)
    dattn = dhidden.astype(BF)
    dinner_out = (mm_nt(dattn, flat_b(out_b)) * marks[3]).astype(BF)
    dmixed = mm_nt(jnp.concatenate([dattn, dinner_out], axis=1), all_qkvo[3]).astype(BF)
    dq, dk, dv = attend_back(q, kv_all[0], kv_all[1], bias, lse, split(dmixed))
    dkv = jnp.stack([dk, dv])
    dkv = group_sums(pl_, [dkv[:, :, i * rows : (i + 1) * rows] for i in range(2 * pl_.Q)])
    dproj = [join(a).astype(BF) for a in (dq, dkv[0], dkv[1])]
    dn1 = jnp.zeros((rows, W), F32)
    dinner = []
    for j in range(3):
        both = mm(dproj[j], all_qkvo[j])
        low = (both[:, W:] * marks[j]).astype(BF)
        dn1 = dn1 + both[:, :W] + mm_nt(low, flat_a(qkv_a[j]))
        dinner.append(low)
    dframes = dhidden + norm_back(z1, rate1, dn1 * gain1)
    frames_grad = from_clip(pl_, dframes.astype(BF)).astype(F32)

    def pick(low, j):
        return lax.dynamic_slice_in_dim(low, picks[j] * R, R, 1)

    model_side = [
        mm_tn(pick(dinner[0], 0), n1),
        mm_tn(pick(dinner[1], 1), n1),
        mm_tn(pick(dinner[2], 2), n1),
        mm_tn(pick(inner_out, 3), dattn),
        mm_tn(pick(dinner_up, 4), n2),
        mm_tn(pick(inner_down, 5), seed),
    ]
    head_side = [
        mm_tn(pick(inner[0], 0), dproj[0]),
        mm_tn(pick(inner[1], 1), dproj[1]),
        mm_tn(pick(inner[2], 2), dproj[2]),
        mm_tn(pick(dinner_out, 3), mixed),
    ]
    unit_side = [mm_tn(pick(inner_up, 4), dupper), mm_tn(pick(dinner_down, 5), active)]
    terms = jnp.concatenate(
        [a.reshape(R, T, -1) for a in model_side + head_side + unit_side], axis=2
    )
    K = D // 2
    RD = R // D if R >= D else 1
    width = terms.shape[2]
    terms = terms.reshape(K, 2, RD, T, width)
    even, odd = terms[:, 0], terms[:, 1]
    first = pl_.core == 0
    mine, theirs = jnp.where(first, even, odd), jnp.where(first, odd, even)
    mine = mine + pl_.swap_core(theirs)
    mine = lax.all_to_all(mine.transpose(2, 0, 1, 3), "tensor", 0, 0)
    planes = [[2 * k + c for k in range(K)] for c in range(2)]
    mine = lax.all_to_all(mine.transpose(1, 0, 2, 3), "dp", 0, 0, axis_index_groups=planes)
    clips = metas.reshape(K, 2 * C, 7)[:, :, 1:]
    clips = jnp.repeat(clips, pl_.Q, axis=1)
    hot = (clips[..., None] == jnp.arange(A)).astype(F32)
    hot = hot.reshape(K * T, 6, A)
    mine = mine.reshape(K * T, RD, width)

    def owned(j, start, size):
        return jnp.einsum(
            "sa,srw->arw", hot[:, j], mine[:, :, start : start + size], precision=lax.Precision.HIGHEST
        )

    wm, wu = W // T, U
    model = [owned(j, j * wm, wm) for j in range(6)]
    head = [owned(j, (6 + j) * wm, wm) for j in range(4)]
    unit = [owned(4, 10 * wm, wu), owned(5, 10 * wm + wu, wu)]
    flip = lambda a: jnp.swapaxes(a, -1, -2)
    return (
        layer_output,
        frames_grad,
        flip(jnp.stack(model[:3])),
        jnp.stack(head[:3]),
        flip(head[3]),
        model[3],
        flip(model[4]),
        unit[0],
        flip(unit[1]),
        model[5],
    )


def solution(mesh):
    placed = (
        P("dp", "tensor", None),
        P("dp", "tensor", None),
        P("dp"),
        P("dp", None),
        P(),
        P(),
        P(None, "dp", "tensor"),
        P("tensor", "dp"),
        P("dp", "tensor"),
        P("tensor", "dp"),
        P(),
        P(None, None, None, "tensor"),
        P(None, "tensor", None),
        P(),
        P(),
        P(None, None, "tensor"),
        P(None, "tensor", None),
        P(),
    )
    return jax.shard_map(
        body,
        mesh=mesh,
        in_specs=placed,
        out_specs=(
            P("dp", "tensor", None),
            P("dp", "tensor", None),
            P(None, None, "tensor", "dp"),
            P(None, None, "dp", "tensor"),
            P(None, "tensor", "dp"),
            P(None, "dp", "tensor"),
            P(None, "tensor", "dp"),
            P(None, "dp", "tensor"),
            P(None, "tensor", "dp"),
            P(None, "dp", "tensor"),
        ),
        check_vma=False,
    )
```

time: 3930 us -> 924 us (0.24)
  waiting for transfers between devices: 2690 us -> 201 us
  matrix products: 746 us -> 433 us
  other arithmetic: 237 us -> 88.6 us
  loops' own time: 59.3 us -> 0.88 us
  starting transfers between devices: 2.59 us -> 45.4 us
    reduce_scatter x16 -> x0, waiting for transfers between devices: 1660 us -> none  [the longest x4 958 us: collect_grads(): return lax.psum_scatter(terms, 'tensor', scatter_dimension=1, tiled=True)]
    all_gather x14 -> x2, waiting for transfers between devices: 816 us -> 17.4 us  [gather_rows(): return lax.all_gather(x, ('tensor', 'dp'))]
    dot_general x360 -> x160, matrix products: 746 us -> 433 us  [the longest x60 173 us: mm_nt(): lax.dot_general(a, b, (((1,), (1,)), ((), ())), preferred_element_type=F32)]
    unnamed x16 -> x2, waiting for transfers between devices: 214 us -> 0.03 us
    all_to_all x0 -> x8, waiting for transfers between devices: none -> 176 us  [the longest x2 67.5 us: to_clip(): return lax.all_to_all(both, 'tensor', 0, 0).reshape(pl_.rows, W)]
    another operation x12 -> x14, other arithmetic: 101 us -> 18.4 us  [the longest x2 24.2 us: micro_step(): branch_output = collect_rows(jnp.stack(ffn_terms))]
    another operation x1 -> x2, loops' own time: 59.3 us -> 0.88 us  [the longest x1 0.54 us: attend_back(): return lax.map(head, (q, k, v, lse, dmixed))]
    convert_element_type x32 -> x28, other arithmetic: 80.5 us -> 22.6 us  [the longest x16 7.59 us: head(): dscores = (probs * (dprobs - delta)).astype(BF)]
  transfers between devices with their start and end apart: 34 -> 17, of which waited for: 32 -> 11; matrix products, arithmetic and copies ran while one was open for 19% -> 32% of each run, Pallas kernels for 0% -> 0%
where the time goes in v1:
time: 924 us; the launch traced here: 914 us
  matrix products  433 us (47%)
  waiting for transfers between devices  201 us (22%)
  local copies, waits for them, and re-layouts  121 us (13%)
  other arithmetic  88.6 us (10%)
  starting transfers between devices  45.4 us (5%)
  between operations  19.8 us (2%)
    dot_general x60, matrix products, mm_nt(): lax.dot_general(a, b, (((1,), (1,)), ((), ())), preferred_element_type=F32)  173 us
    dot_general x44, matrix products, mm(): return jnp.dot(a, b, preferred_element_type=F32)  161 us
    dot_general x44, matrix products, mm_tn(): lax.dot_general(a, b, (((0,), (0,)), ((), ())), preferred_element_type=F32)  96.4 us
    all_to_all x2, waiting for transfers between devices, to_clip(): return lax.all_to_all(both, 'tensor', 0, 0).reshape(pl_.rows, W)  67.5 us
    all_to_all x2, waiting for transfers between devices, from_clip(): both = lax.all_to_all(y.reshape(pl_.T, pl_.S, W), 'tensor', 0, 0)  66.8 us
    unnamed x175, local copies, waits for them, and re-layouts  21.3 us
    while x3, local copies, waits for them, and re-layouts, attend(): return lax.map(head, (q, k, v))  19.9 us
  transfers between devices with their start and end apart: 17, of which 11 were waited for; matrix products, arithmetic and copies ran while one was open for 32% of the time, Pallas kernels for 0%

profile of v1, /device:TPU:0, one launch (start us, length us, event | category | flops | bytes accessed | tf_op | source)
XLA Modules:
  0.0 914.0 jit_solution(41825496960269122)
XLA Ops:
  14.4 7.5 all-to-all-done.1
  31.6 15.0 %all-to-all-done.2 = bf16[2,640,320]{2,0,1:T(2,128)(2,1)S(1)} async-done(((bf16[2,640,320]{2,0,1:T(2,128)(2,1)}), bf16[2,640,320]{2,0,1:T(2,128)(2,1)S(1)}, u32[]{:S(2)}, u32[]{:S(2)}) %all-to-all-start.2) | async-done | bytes 819232 | tf_op jit(solution)/shard_map/all_to_all | solution.py:193
  55.5 6.6 all-to-all-start
  64.8 5.1 all-gather.3
  75.7 67.5 %all-to-all-done = bf16[8,96,1280]{2,1,0:T(8,128)(2,1)S(1)} async-done(((bf16[8,96,1280]{2,1,0:T(8,128)(2,1)}), bf16[8,96,1280]{2,1,0:T(8,128)(2,1)S(1)}, u32[]{:S(2)}, u32[]{:S(2)}) %all-to-all-start) | async-done | bytes 1966112 | tf_op jit(solution)/shard_map/all_to_all | solution.py:68
  143.2 4.7 all-to-all-start.4
  157.0 17.4 %all-gather.7.cloned.1.call-done = bf16[5120,1408]{1,0:T(8,128)(2,1)} async-done(((bf16[160,1408]{1,0:T(8,128)(2,1)}), bf16[5120,1408]{1,0:T(8,128)(2,1)}) %all-gather.7.cloned.1.call-update) | async-done | bytes 14417936 | tf_op jit(solution)/shard_map/all_gather | solution.py:83
  174.4 9.9 %fusion.152 = (bf16[1,8,160,1408]{3,2,0,1:T(8,128)(2,1)}, bf16[1,8,160,1408]{3,2,0,1:T(8,128)(2,1)}, bf16[1,8,160,1408]{3,2,0,1:T(8,128)(2,1)S(1)}, bf16[1,8,160,1408]{3,2,0,1:T(8,128)(2,1)}) fusion(bf16[4,8,160,1408]{3,2,0,1:T(8,128)(2,1)} %bitcast.526), kind=kLoop, calls=%fused_computation.305 | loop fusion | bytes 28835840 | tf_op jit(solution)/shard_map/slice | solution.py:222
  194.6 7.3 convolution_convert_fusion.1
  256.7 7.8 copy.326
  264.5 7.7 copy.327
  272.2 99.3 %while.26 = (s32[]{:T(128)}, bf16[16,768,80]{1,2,0:T(8,128)(2,1)}, f32[16,768,1]{1,2,0:T(1,128)S(1)}, bf16[16,768,80]{2,1,0:T(8,128)(2,1)}, bf16[16,1536,80]{2,1...) while((s32[]{:T(128)}, bf16[16,768,80]{1,2,0:T(8,128)(2,1)}, ...), condition=%wide.region_5.6_spmd, body=%wide.region_2.5_spmd.sunk | while | flops 391703808 | bytes 15314009 | solution.py:130
  371.5 6.0 fusion.157
  381.1 15.7 %fusion.151 = (bf16[1,32,160,1408]{3,2,0,1:T(8,128)(2,1)}, bf16[1,32,160,1408]{3,2,0,1:T(8,128)(2,1)S(1)}) fusion(bf16[2,32,160,1408]{3,2,0,1:T(8,128)(2,1)} %bitcast.517), kind=kLoop, calls=%fused_computation.304 | loop fusion | bytes 57671680 | tf_op jit(solution)/shard_map/slice | solution.py:231
  396.8 15.3 %multiply_convert_fusion.1 = (bf16[768,5120]{1,0:T(8,128)(2,1)S(1)}, f32[768,5120]{1,0:T(8,128)}) fusion(bf16[5120,1408]{1,0:T(8,128)(2,1)S(1)} %bitcast.522, bf16[768,128]{1,0:T(8,128)(2,1)S(1)} %fusion.81, bf16[768,1280]{1,0:T(8,128)(2,1)S(1)} %multiply_convert_fusion.2), kind=kOutput, calls=%fused_computation.63 | convolution fusion | flops 11096948736 | bytes 40173568 | tf_op jit(solution)/shard_map/dot_general | solution.py:18
  412.1 19.1 %fusion.158 = f32[768,1408]{1,0:T(8,128)S(1)} fusion(bf16[768,5120]{1,0:T(8,128)(2,1)S(1)} %get-tuple-element.334, bf16[5120,1408]{1,0:T(8,128)(2,1)} %bitcast.524), kind=kOutput, calls=%fused_computation.311 | convolution fusion | flops 11072962560 | bytes 26607616 | tf_op jit(solution)/shard_map/dot_general | solution.py:14
  431.3 20.6 %fusion.47 = bf16[768,5120]{1,0:T(8,128)(2,1)S(1)} fusion(f32[768,5120]{1,0:T(8,128)} %get-tuple-element.335, bf16[5120,1408]{1,0:T(8,128)(2,1)} %bitcast.525, bf16[768,128]{1,0:T(8,128)(2,1)S(1)} %fusion.82, bf16[768,1280]{1,0:T(8,128)(2,1)S(1)} %copy-done.15), kind=kOutput, calls=%fused_computation.60 | convolution fusion | flops 11116609536 | bytes 40173568 | tf_op jit(solution)/shard_map/dot_general | solution.py:18
  451.9 18.6 %fusion.159 = f32[768,1408]{1,0:T(8,128)S(1)} fusion(bf16[768,5120]{1,0:T(8,128)(2,1)S(1)} %fusion.47, bf16[5120,1408]{1,0:T(8,128)(2,1)} %bitcast.523), kind=kOutput, calls=%fused_computation.312 | convolution fusion | flops 11072962560 | bytes 26607616 | tf_op jit(solution)/shard_map/dot_general | solution.py:14
  485.6 192.1 %while.27 = (s32[]{:T(128)}, bf16[16,768,80]{1,2,0:T(8,128)(2,1)}, f32[16,1536,80]{1,2,0:T(8,128)}, f32[16,1536,80]{1,2,0:T(8,128)}, bf16[16,768,80]{2,1,0:T(8,1...) while((s32[]{:T(128)}, bf16[16,768,80]{1,2,0:T(8,128)(2,1)}, ...), condition=%wide.region_12.13_spmd, body=%wide.region_10.12_spmd.sunk | while | flops 954518784 | bytes 38463600 | solution.py:146
  677.8 5.8 fusion.50
  692.4 5.9 fusion.160
  701.1 4.6 fusion.97
  714.9 5.2 fusion.49
  732.2 5.9 fusion.161
  754.2 11.9 %all-to-all-start.6 = ((f32[8,2,4,2880]{3,2,1,0:T(4,128)}), f32[8,2,4,2880]{3,2,1,0:T(4,128)S(1)}, u32[]{:S(2)}, u32[]{:S(2)}) async-start(f32[8,2,4,2880]{3,2,1,0:T(4,128)} %fusion.92), calls=%async_computation.6 | async-start | bytes 1507328 | tf_op jit(solution)/shard_map/all_to_all | solution.py:292
  766.0 5.3 fusion.58
  771.3 14.7 %all-to-all-done.6 = f32[8,2,4,2880]{3,2,1,0:T(4,128)S(1)} async-done(((f32[8,2,4,2880]{3,2,1,0:T(4,128)}), f32[8,2,4,2880]{3,2,1,0:T(4,128)S(1)}, u32[]{:S(2)}, u32[]{:S(2)}) %all-to-all-start.6) | async-done | bytes 737312 | tf_op jit(solution)/shard_map/all_to_all | solution.py:292
  786.0 4.6 all-to-all-start.3
  802.2 33.5 %all-to-all-done.3 = bf16[8,96,1280]{2,1,0:T(8,128)(2,1)} async-done(((bf16[8,96,1280]{2,1,0:T(8,128)(2,1)}), bf16[8,96,1280]{2,1,0:T(8,128)(2,1)}, u32[]{:S(2)}, u32[]{:S(2)}) %all-to-all-start.3) | async-done | bytes 1966112 | tf_op jit(solution)/shard_map/all_to_all | solution.py:73
  839.2 4.9 add_convert_fusion
  848.5 5.3 all-to-all-start.5
  865.2 33.3 %all-to-all-done.5 = bf16[8,96,1280]{2,1,0:T(8,128)(2,1)S(1)} async-done(((bf16[8,96,1280]{2,1,0:T(8,128)(2,1)}), bf16[8,96,1280]{2,1,0:T(8,128)(2,1)S(1)}, u32[]{:S(2)}, u32[]{:S(2)}) %all-to-all-start.5) | async-done | bytes 1966112 | tf_op jit(solution)/shard_map/all_to_all | solution.py:73
  (557 shorter events, 500.5 us)
Async XLA Ops:
  7.2 373.2 %copy-start = (bf16[8,1280,16]{1,2,0:T(8,128)(2,1)S(1)}, bf16[8,1280,16]{1,2,0:T(8,128)(2,1)}, u32[]{:S(2)}) copy-start(bf16[8,1280,16]{1,2,0:T(8,128)(2,1)} %param.36) | copy-start | bytes 983044
  9.2 12.7 %all-to-all-start.1 = ((bf16[4,160,320]{2,1,0:T(8,128)(2,1)}), bf16[4,160,320]{2,1,0:T(8,128)(2,1)S(1)}, u32[]{:S(2)}, u32[]{:S(2)}) async-start(bf16[4,160,320]{2,1,0:T(8,128)(2,1)} %pad_maximum_fusion.8), calls=%async_computation.1 | async-start | bytes 983040 | tf_op jit(solution)/shard_map/all_to_all | solution.py:187
  13.5 161.0 %all-gather.7.cloned.1.call-start = ((), (), s32[]{:S(2)}) async-start(), calls=%async_computation.8 | async-start | bytes 14868480 | tf_op jit(solution)/shard_map/all_gather | solution.py:83
  26.2 20.5 %all-to-all-start.2 = ((bf16[2,640,320]{2,0,1:T(2,128)(2,1)}), bf16[2,640,320]{2,0,1:T(2,128)(2,1)S(1)}, u32[]{:S(2)}, u32[]{:S(2)}) async-start(bf16[2,640,320]{2,0,1:T(2,128)(2,1)} %copy.329), calls=%async_computation.2 | async-start | bytes 1966080 | tf_op jit(solution)/shard_map/all_to_all | solution.py:193
  29.7 351.4 %all-gather.9.cloned.1.call-start = ((), (), s32[]{:S(2)}) async-start(), calls=%async_computation.9 | async-start | bytes 29736960 | tf_op jit(solution)/shard_map/all_gather | solution.py:83
  31.6 19.5 %copy-start.9 = (bf16[4,192,1280]{2,1,0:T(8,128)(2,1)S(1)}, bf16[4,192,1280]{2,1,0:T(8,128)(2,1)}, u32[]{:S(2)}) copy-start(bf16[4,192,1280]{2,1,0:T(8,128)(2,1)} %param.22) | copy-start | bytes 5898244
  51.2 2.6 collective-permute-start
  55.5 87.7 %all-to-all-start = ((bf16[8,96,1280]{2,1,0:T(8,128)(2,1)}), bf16[8,96,1280]{2,1,0:T(8,128)(2,1)S(1)}, u32[]{:S(2)}, u32[]{:S(2)}) async-start(bf16[8,96,1280]{2,1,0:T(8,128)(2,1)} %bitcast.534), calls=%async_computation | async-start | bytes 3932160 | tf_op jit(solution)/shard_map/all_to_all | solution.py:68
  64.7 7.2 collective-permute-start.3
  70.6 79.1 %copy-start.74 = (f32[128]{0:T(128)}, f32[128]{0:T(128)S(1)}, u32[]{:S(2)}) copy-start(f32[128]{0:T(128)S(1)} %get-tuple-element.321) | copy-start | bytes 1540
  70.6 82.0 %copy-start.76 = (f32[128]{0:T(128)}, f32[128]{0:T(128)S(1)}, u32[]{:S(2)}) copy-start(f32[128]{0:T(128)S(1)} %get-tuple-element.320) | copy-start | bytes 1540
  70.6 147.0 %copy-start.78 = (f32[128]{0:T(128)}, f32[128]{0:T(128)S(1)}, u32[]{:S(2)}) copy-start(f32[128]{0:T(128)S(1)} %get-tuple-element.322) | copy-start | bytes 1540
  70.6 164.4 %copy-start.71 = (f32[128]{0:T(128)}, f32[128]{0:T(128)S(1)}, u32[]{:S(2)}) copy-start(f32[128]{0:T(128)S(1)} %get-tuple-element.317) | copy-start | bytes 1540
  71.9 77.9 %copy-start.35 = (bf16[1,8,1280,16]{2,3,1,0:T(8,128)(2,1)}, bf16[1,8,1280,16]{2,3,1,0:T(8,128)(2,1)S(1)}, u32[]{:S(2)}) copy-start(bf16[1,8,1280,16]{2,3,1,0:T(8,128)(2,1)S(1)} %get-tuple-element.314) | copy-start | bytes 983044
  71.9 80.7 %copy-start.33 = (bf16[1,8,1280,16]{2,3,1,0:T(8,128)(2,1)}, bf16[1,8,1280,16]{2,3,1,0:T(8,128)(2,1)S(1)}, u32[]{:S(2)}) copy-start(bf16[1,8,1280,16]{2,3,1,0:T(8,128)(2,1)S(1)} %get-tuple-element.316) | copy-start | bytes 983044
  71.9 145.7 %copy-start.37 = (bf16[1,8,1280,16]{2,3,1,0:T(8,128)(2,1)}, bf16[1,8,1280,16]{2,3,1,0:T(8,128)(2,1)S(1)}, u32[]{:S(2)}) copy-start(bf16[1,8,1280,16]{2,3,1,0:T(8,128)(2,1)S(1)} %get-tuple-element.315) | copy-start | bytes 983044
  143.2 234.3 %copy-start.3 = (bf16[8,96,1280]{2,1,0:T(8,128)(2,1)}, bf16[8,96,1280]{2,1,0:T(8,128)(2,1)S(1)}, u32[]{:S(2)}) copy-start(bf16[8,96,1280]{2,1,0:T(8,128)(2,1)S(1)} %all-to-all-done) | copy-start | bytes 5898244
  143.2 82.8 %all-to-all-start.4 = ((bf16[8,96,1280]{2,1,0:T(8,128)(2,1)}), bf16[8,96,1280]{2,1,0:T(8,128)(2,1)}, u32[]{:S(2)}, u32[]{:S(2)}) async-start(bf16[8,96,1280]{2,1,0:T(8,128)(2,1)} %bitcast.532), calls=%async_computation.4 | async-start | bytes 3932160 | tf_op jit(solution)/shard_map/all_to_all | solution.py:68
  210.4 38.8 %collective-permute-start.1 = (bf16[2,16,768,80]{2,3,1,0:T(8,128)(2,1)}, bf16[2,16,768,80]{2,3,1,0:T(8,128)(2,1)}, u32[]{:S(2)}, u32[]{:S(2)}) collective-permute-start(bf16[2,16,768,80]{2,3,1,0:T(8,128)(2,1)} %pad_maximum_fusion.2), channel_id=1, source_target_pairs={{0,8},{8,0},{16,24},{24,16},{1,9},{9,1},{17,25},{25,17},{2,10},{10... | collective-permute-start | bytes 11796488 | tf_op jit(solution)/shard_map/ppermute | solution.py:51
  235.7 195.5 %copy-start.52 = (bf16[768,128]{1,0:T(8,128)(2,1)}, bf16[768,128]{1,0:T(8,128)(2,1)S(1)}, u32[]{:S(2)}) copy-start(bf16[768,128]{1,0:T(8,128)(2,1)S(1)} %fusion.82) | copy-start | bytes 589828
  412.1 19.1 %copy-start.6 = (bf16[768,5120]{1,0:T(8,128)(2,1)}, bf16[768,5120]{1,0:T(8,128)(2,1)S(1)}, u32[]{:S(2)}) copy-start(bf16[768,5120]{1,0:T(8,128)(2,1)S(1)} %get-tuple-element.334) | copy-start | bytes 23592964
  412.1 19.2 %copy-start.15 = (bf16[768,1280]{1,0:T(8,128)(2,1)S(1)}, bf16[768,1280]{1,0:T(8,128)(2,1)}, u32[]{:S(2)}) copy-start(bf16[768,1280]{1,0:T(8,128)(2,1)} %bitcast_select_fusion) | copy-start | bytes 5898244
  431.2 39.3 %copy-start.18 = (f32[768,1408]{1,0:T(8,128)}, f32[768,1408]{1,0:T(8,128)S(1)}, u32[]{:S(2)}) copy-start(f32[768,1408]{1,0:T(8,128)S(1)} %fusion.158) | copy-start | bytes 12976132
  683.6 31.3 %collective-permute-start.4 = (bf16[2,16,768,80]{2,3,1,0:T(8,128)(2,1)}, bf16[2,16,768,80]{2,3,1,0:T(8,128)(2,1)}, u32[]{:S(2)}, u32[]{:S(2)}) collective-permute-start(bf16[2,16,768,80]{2,3,1,0:T(8,128)(2,1)} %fusion.50), channel_id=1, source_target_pairs={{0,8},{8,0},{16,24},{24,16},{1,9},{9,1},{17,25},{25,17},{2,10},{10... | collective-permute-start | bytes 11796488 | tf_op jit(solution)/shard_map/ppermute | solution.py:51
  750.6 2.3 collective-permute-start.6
  754.2 31.8 %all-to-all-start.6 = ((f32[8,2,4,2880]{3,2,1,0:T(4,128)}), f32[8,2,4,2880]{3,2,1,0:T(4,128)S(1)}, u32[]{:S(2)}, u32[]{:S(2)}) async-start(f32[8,2,4,2880]{3,2,1,0:T(4,128)} %fusion.92), calls=%async_computation.6 | async-start | bytes 1507328 | tf_op jit(solution)/shard_map/all_to_all | solution.py:292
  771.3 19.3 %copy-start.38 = (bf16[1,8,1280,16]{2,3,1,0:T(8,128)(2,1)S(1)}, bf16[1,8,1280,16]{2,3,1,0:T(8,128)(2,1)}, u32[]{:S(2)}) copy-start(bf16[1,8,1280,16]{2,3,1,0:T(8,128)(2,1)} %copy-done.37) | copy-start | bytes 983044
  786.0 49.7 %all-to-all-start.3 = ((bf16[8,96,1280]{2,1,0:T(8,128)(2,1)}), bf16[8,96,1280]{2,1,0:T(8,128)(2,1)}, u32[]{:S(2)}, u32[]{:S(2)}) async-start(bf16[8,96,1280]{2,1,0:T(8,128)(2,1)} %bitcast.82), calls=%async_computation.3 | async-start | bytes 3932160 | tf_op jit(solution)/shard_map/all_to_all | solution.py:73
  835.7 12.8 %all-to-all-start.7 = ((f32[2,8,4,2880]{3,2,1,0:T(4,128)}), f32[2,8,4,2880]{3,2,1,0:T(4,128)S(1)}, u32[]{:S(2)}, u32[]{:S(2)}) async-start(f32[2,8,4,2880]{3,2,1,0:T(4,128)} %copy.364), calls=%async_computation.7 | async-start | bytes 1507328 | tf_op jit(solution)/shard_map/all_to_all | solution.py:294
  848.5 50.1 %all-to-all-start.5 = ((bf16[8,96,1280]{2,1,0:T(8,128)(2,1)}), bf16[8,96,1280]{2,1,0:T(8,128)(2,1)S(1)}, u32[]{:S(2)}, u32[]{:S(2)}) async-start(bf16[8,96,1280]{2,1,0:T(8,128)(2,1)} %bitcast.536), calls=%async_computation.5 | async-start | bytes 3932160 | tf_op jit(solution)/shard_map/all_to_all | solution.py:73
  856.3 2.9 collective-permute-start.2
  898.6 5.4 collective-permute-start.5
  (66 other events, 439.1 us)
Sparse Core Ops, SparseCore 0:
  23.6 150.8 all-gather.6
  177.3 182.9 all-gather.8

commit v2 on v1

v2 whole, which is shorter than its diff:
```python
import functools

import jax
import jax.numpy as jnp
from jax import lax
from jax.experimental import pallas as pl
from jax.experimental.pallas import tpu as pltpu
from jax.sharding import PartitionSpec as P

HEAD = 80
BF = jnp.bfloat16
F32 = jnp.float32


def mm(a, b):
    return jnp.dot(a, b, preferred_element_type=F32)


def mm_nt(a, b):
    return lax.dot_general(a, b, (((1,), (1,)), ((), ())), preferred_element_type=F32)


def mm_tn(a, b):
    return lax.dot_general(a, b, (((0,), (0,)), ((), ())), preferred_element_type=F32)


def norm_parts(values):
    center = values - jnp.mean(values, axis=-1, keepdims=True)
    rate = lax.rsqrt(jnp.mean(center * center, axis=-1, keepdims=True) + 1e-5)
    return center * rate, rate


def norm_back(z, rate, grad):
    return rate * (
        grad
        - jnp.mean(grad, axis=-1, keepdims=True)
        - z * jnp.mean(grad * z, axis=-1, keepdims=True)
    )


class Place:
    def __init__(self, clips, local_frames):
        self.D, self.T = lax.axis_size("dp"), lax.axis_size("tensor")
        self.d, self.t = lax.axis_index("dp"), lax.axis_index("tensor")
        self.core = self.d % 2
        self.C, self.LF = clips, local_frames
        self.Q = self.T // (2 * clips)
        self.S = local_frames // (2 * self.Q)
        self.rows = self.T * self.S
        self.swap = [(i, i ^ 1) for i in range(self.D)]

    def swap_core(self, x):
        return lax.ppermute(x, "dp", self.swap)

    def positions(self, core, q):
        source = jnp.arange(self.T, dtype=jnp.int32)[:, None] * self.LF
        inner = (q * 2 + core) * self.S + jnp.arange(self.S, dtype=jnp.int32)[None, :]
        return (source + inner).reshape(self.rows)


def by_chip(pl_, x):
    C, LF, W = x.shape
    parts = x.reshape(C, pl_.Q, 2, pl_.S, W)
    even, odd = parts[:, :, 0], parts[:, :, 1]
    first = pl_.core == 0
    mine, theirs = jnp.where(first, even, odd), jnp.where(first, odd, even)
    got = pl_.swap_core(theirs)
    both = jnp.stack([jnp.where(first, mine, got), jnp.where(first, got, mine)])
    return both.reshape(pl_.T, pl_.S, W)


def to_clip(pl_, both):
    return lax.all_to_all(both, "tensor", 0, 0).reshape(pl_.rows, both.shape[2])


def from_clip(pl_, y):
    W = y.shape[-1]
    both = lax.all_to_all(y.reshape(pl_.T, pl_.S, W), "tensor", 0, 0)
    both = both.reshape(2, pl_.C, pl_.Q, pl_.S, W)
    first = pl_.core == 0
    mine, theirs = jnp.where(first, both[0], both[1]), jnp.where(first, both[1], both[0])
    got = pl_.swap_core(theirs)
    even, odd = jnp.where(first, mine, got), jnp.where(first, got, mine)
    return jnp.stack([even, odd], axis=2).reshape(pl_.C, pl_.LF, W)


def ring(x, axis, stride, size):
    perm = [(i, (i + stride) % size) for i in range(size)]
    out = [x]
    for _ in range(size // stride - 1):
        out.append(lax.ppermute(out[-1], axis, perm))
    return jnp.stack(out)


class Gather:
    def __init__(self, place, first, second):
        self.place = place
        self.parts = (first, second)

    def line(self):
        self.parts = [ring(v, "tensor", 2, self.place.T) for v in self.parts]

    def pair(self, v):
        perm = [(i, i ^ 1) for i in range(self.place.T)]
        return jnp.stack([v, lax.ppermute(v, "tensor", perm)])

    def plane(self, v):
        return ring(v, "dp", 2, self.place.D)

    def middle(self):
        self.parts = [self.pair(self.parts[0]), self.plane(self.parts[1])]

    def last(self):
        self.parts = [self.plane(self.parts[0]), self.pair(self.parts[1])]

    def core(self):
        self.parts = [*self.parts, *[self.place.swap_core(v) for v in self.parts]]


def tie(gathers, *values):
    moved = [g.parts for g in gathers]
    moved, values = lax.optimization_barrier((moved, values))
    for g, parts in zip(gathers, moved):
        g.parts = list(parts)
    return values


def places(pl_, pair_first):
    T, D = pl_.T, pl_.D
    tt, dd = jnp.meshgrid(jnp.arange(T), jnp.arange(D), indexing="ij")
    fx = (pl_.t ^ tt) & 1
    s = ((pl_.t ^ fx) - tt) // 2 % (T // 2)
    fc = (pl_.d ^ dd) & 1
    u = ((pl_.d ^ fc) - dd) // 2 % (D // 2)
    if pair_first:
        index = ((fc * (D // 2) + u) * 2 + fx) * (T // 2) + s
    else:
        index = ((fc * 2 + fx) * (D // 2) + u) * (T // 2) + s
    return index.reshape(-1)


def plane_places(pl_):
    dd = jnp.arange(pl_.D)
    fc = (pl_.d ^ dd) & 1
    return fc * (pl_.D // 2) + ((pl_.d ^ fc) - dd) // 2 % (pl_.D // 2)


def group_values(pl_, x):
    out = [x, pl_.swap_core(x)]
    for step in range(1, pl_.Q):
        perm = [
            (i, i - i % pl_.Q + (i + step) % pl_.Q) for i in range(pl_.T)
        ]
        out.append(lax.ppermute(out[0], "tensor", perm))
        out.append(lax.ppermute(out[1], "tensor", perm))
    return out


def group_places(pl_):
    q = pl_.t % pl_.Q
    out = []
    for step in range(pl_.Q):
        sender = (q - step) % pl_.Q
        out.append((pl_.core, sender))
        out.append((1 - pl_.core, sender))
    return out


def group_received(pl_, blocks):
    total = pl_.swap_core(blocks[1])
    for step in range(1, pl_.Q):
        perm = [(i - i % pl_.Q + (i + step) % pl_.Q, i) for i in range(pl_.T)]
        own = lax.ppermute(blocks[2 * step], "tensor", perm)
        other = lax.ppermute(pl_.swap_core(blocks[2 * step + 1]), "tensor", perm)
        total = (total.astype(F32) + own.astype(F32) + other.astype(F32)).astype(BF)
    return total


RATE = HEAD**-0.5
TO_LOG2 = RATE * 1.4426950408889634
EXTRA = 16


def attend_kernel(q_ref, k_refs, v_refs, bias_ref, out_ref, lse_ref):
    rows = q_ref.shape[1]
    keys = bias_ref.shape[1]
    k = jnp.concatenate(
        [jnp.concatenate([r[...] for r in k_refs], axis=1), bias_ref[...].astype(BF), jnp.zeros((EXTRA - 1, keys), BF)]
    ).T
    v = jnp.concatenate(
        [jnp.concatenate([r[...] for r in v_refs], axis=1), jnp.ones((EXTRA, keys), BF)]
    )
    q = jnp.concatenate([q_ref[...], jnp.ones((EXTRA, rows), BF)])
    scores = mm(k, q)
    top = jnp.max(scores, axis=0, keepdims=True)
    expo = jnp.exp2((scores - top) * TO_LOG2).astype(BF)
    both = mm(v, expo)
    total = both[HEAD : HEAD + 1]
    out_ref[...] = (both[:HEAD] / total).astype(BF)
    lse_ref[0] = top + jnp.log2(total) * (1.0 / TO_LOG2)


def attend(q, ks, vs, bias):
    width, rows = q.shape
    heads, n = width // HEAD, len(ks)
    head = pl.BlockSpec((HEAD, rows), lambda h: (h, 0))

    def kernel(*refs):
        attend_kernel(refs[0], refs[1 : 1 + n], refs[1 + n : 1 + 2 * n], *refs[1 + 2 * n :])

    return pl.pallas_call(
        kernel,
        grid=(heads,),
        in_specs=[head] * (1 + 2 * n) + [pl.BlockSpec(bias.shape, lambda h: (0, 0))],
        out_specs=[head, pl.BlockSpec((1, 1, rows), lambda h: (h, 0, 0))],
        out_shape=[
            jax.ShapeDtypeStruct((width, rows), BF),
            jax.ShapeDtypeStruct((heads, 1, rows), F32),
        ],
        compiler_params=pltpu.CompilerParams(vmem_limit_bytes=56 * 2**20),
        cost_estimate=pl.CostEstimate(
            flops=4 * heads * rows * bias.shape[1] * 256, bytes_accessed=6 * width * rows, transcendentals=0
        ),
        name="attend_forward",
    )(q, *ks, *vs, bias)


def attend_back_kernel(
    q_ref, k_refs, v_refs, bias_ref, lse_ref, mixed_ref, dmixed_ref, dq_ref, dk_refs, dv_refs, *, span
):
    rows = q_ref.shape[1]
    keys = bias_ref.shape[1]
    k_flat = jnp.concatenate([r[...] for r in k_refs], axis=1)
    k = jnp.concatenate(
        [k_flat, bias_ref[...].astype(BF), jnp.ones((3, keys), BF), jnp.zeros((EXTRA - 4, keys), BF)]
    ).T
    v = jnp.concatenate(
        [jnp.concatenate([r[...] for r in v_refs], axis=1), jnp.ones((EXTRA, keys), BF)]
    ).T
    dmixed = dmixed_ref[...]
    delta = -jnp.sum(dmixed.astype(F32) * mixed_ref[...].astype(F32), axis=0, keepdims=True)
    d0 = delta.astype(BF)
    d1 = (delta - d0.astype(F32)).astype(BF)
    dmixed_more = jnp.concatenate([dmixed, d0, d1, jnp.zeros((EXTRA - 2, rows), BF)])
    lse = -lse_ref[0]
    l0 = lse.astype(BF)
    rest = lse - l0.astype(F32)
    l1 = rest.astype(BF)
    l2 = (rest - l1.astype(F32)).astype(BF)
    q_flat = q_ref[...]
    q = jnp.concatenate([q_flat, jnp.ones((1, rows), BF), l0, l1, l2, jnp.zeros((EXTRA - 4, rows), BF)])
    dk = jnp.zeros((HEAD, keys), F32)
    dv = jnp.zeros((HEAD, keys), F32)
    for start in range(0, rows, span):
        part = slice(start, start + span)
        probs = jnp.exp2(mm(k, q[:, part]) * TO_LOG2)
        dscores = (probs * mm(v, dmixed_more[:, part])).astype(BF)
        dq_ref[:, part] = (mm(k_flat, dscores) * RATE).astype(BF)
        dk = dk + mm_nt(q_flat[:, part], dscores)
        dv = dv + mm_nt(dmixed[:, part], probs.astype(BF))
    for i, (dk_ref, dv_ref) in enumerate(zip(dk_refs, dv_refs)):
        part = slice(i * rows, (i + 1) * rows)
        dk_ref[...] = (dk[:, part] * RATE).astype(BF)
        dv_ref[...] = dv[:, part].astype(BF)


def attend_back(q, ks, vs, bias, lse, mixed, dmixed):
    width, rows = q.shape
    keys = bias.shape[1]
    heads, n = width // HEAD, len(ks)
    span = rows // 2 if rows % 256 == 0 else rows
    head = pl.BlockSpec((HEAD, rows), lambda h: (h, 0))

    def kernel(*refs):
        ins, outs = refs[: 5 + 2 * n], refs[5 + 2 * n :]
        attend_back_kernel(
            ins[0], ins[1 : 1 + n], ins[1 + n : 1 + 2 * n], *ins[1 + 2 * n :], outs[0], outs[1 : 1 + n], outs[1 + n :], span=span
        )

    return pl.pallas_call(
        kernel,
        grid=(heads,),
        in_specs=[head] * (1 + 2 * n)
        + [
            pl.BlockSpec(bias.shape, lambda h: (0, 0)),
            pl.BlockSpec((1, 1, rows), lambda h: (h, 0, 0)),
            head,
            head,
        ],
        out_specs=[head] * (1 + 2 * n),
        out_shape=[jax.ShapeDtypeStruct((width, rows), BF)] * (1 + 2 * n),
        compiler_params=pltpu.CompilerParams(vmem_limit_bytes=56 * 2**20),
        cost_estimate=pl.CostEstimate(
            flops=8 * heads * rows * keys * 256, bytes_accessed=12 * width * rows, transcendentals=0
        ),
        name="attend_backward",
    )(q, *ks, *vs, bias, lse, mixed, dmixed)


def heads_weights(pl_, parts):
    first, second, first_other, second_other = parts
    planes, pairs, lines, half, width = first.shape
    D, T = pl_.D, pl_.T
    if D == 4 and half == HEAD:
        index = plane_places(pl_)
        order = jnp.stack([index // 2, index % 2], axis=1).reshape(-1).astype(jnp.int32)
        flat = lambda v: v.reshape(*v.shape[:2], lines * half, width)
        return (flat(first), flat(second), flat(first_other), flat(second_other), order), True
    gathered = [
        jnp.stack([first, first_other]).reshape(D, T, half, width),
        jnp.stack([second, second_other]).transpose(0, 2, 1, 3, 4, 5).reshape(D, T, half, width),
    ]
    index = plane_places(pl_)
    gathered = [[lax.dynamic_index_in_dim(v, index[i], 0, False) for v in gathered] for i in range(D)]
    gathered = jnp.stack([jnp.concatenate(v, axis=1) for v in gathered])
    gathered = gathered.reshape(4, D // 4, T, 2 * half, width).transpose(0, 2, 1, 3, 4)
    gathered = gathered.reshape(4, 1, -1, width)
    middle = gathered.shape[2] // 2
    first, second = gathered[:, :, :middle], gathered[:, :, middle:].transpose(1, 0, 2, 3)
    order = jnp.stack([jnp.zeros(4, jnp.int32), jnp.arange(4, dtype=jnp.int32)], axis=1).reshape(-1)
    return (first, second, first, second, order), False


def weight_copies(refs, buf, sems, plane, other):
    first, second = refs[2 * other], refs[2 * other + 1]
    pairs, size = first.shape[1], first.shape[2]
    copies = [
        pltpu.make_async_copy(first.at[plane, x], buf.at[pl.ds(x * size, size)], sems.at[x])
        for x in range(pairs)
    ]
    pairs, at, size = second.shape[0], pairs * size, second.shape[2]
    return copies + [
        pltpu.make_async_copy(second.at[x, plane], buf.at[pl.ds(at + x * size, size)], sems.at[2 + x])
        for x in range(pairs)
    ]


def load_weight(refs, order_ref, number, buf, sems):
    for other in range(2):

        @pl.when(order_ref[2 * number] == other)
        def _():
            for copy in weight_copies(refs, buf, sems, order_ref[2 * number + 1], other):
                copy.start()


def weight_wait(refs, buf, sems):
    for copy in weight_copies(refs, buf, sems, 0, 0):
        copy.wait()


def weight_specs():
    return [pl.BlockSpec(memory_space=pl.ANY)] * 4 + [pl.BlockSpec(memory_space=pltpu.SMEM)]


def whole(shape, dims=0):
    return pl.BlockSpec(shape, lambda *_: (0,) * len(shape))


def block_of(rows):
    return 256 if rows % 256 == 0 else 128


def by_rows(size, width):
    return pl.BlockSpec((size, width), lambda i: (i, 0))


def by_columns(height, size):
    return pl.BlockSpec((height, size), lambda i: (0, i))


def project_kernel(x_ref, gain_ref, a_ref, mark_ref, sel_ref, *refs):
    *w_refs, order_ref, q_ref, k_ref, v_ref, low_ref, bufs, sems = refs
    i = pl.program_id(0)

    @pl.when(i == 0)
    def _():
        for j in range(3):
            load_weight(w_refs, order_ref, j, bufs.at[j], sems.at[j])

    z, _ = norm_parts(x_ref[...].astype(F32))
    n1 = (z * gain_ref[...]).astype(BF)
    for j, out_ref in enumerate((q_ref, k_ref, v_ref)):
        low = (mm(n1, a_ref[j]) * mark_ref[j]).astype(BF)
        low_ref[j] = mm_nt(sel_ref[j], low).astype(BF)

        @pl.when(i == 0)
        def _():
            weight_wait(w_refs, bufs.at[j], sems.at[j])

        out_ref[...] = mm_nt(bufs[j], jnp.concatenate([n1, low], axis=1)).astype(BF)


def project(x, gain, a, marks, sels, w):
    rows, width = x.shape
    AR, R = a.shape[2], sels.shape[1]
    size = block_of(rows)
    return pl.pallas_call(
        project_kernel,
        grid=(rows // size,),
        in_specs=[
            by_rows(size, width),
            whole((1, width)),
            whole((3, width, AR)),
            whole((3, 1, AR)),
            whole((3, R, AR)),
            *weight_specs(),
        ],
        out_specs=[by_columns(width, size)] * 3 + [pl.BlockSpec((3, R, size), lambda i: (0, 0, i))],
        out_shape=[jax.ShapeDtypeStruct((width, rows), BF)] * 3 + [jax.ShapeDtypeStruct((3, R, rows), BF)],
        scratch_shapes=[
            pltpu.VMEM((3, width, width + AR), BF),
            pltpu.SemaphoreType.DMA((3, 4)),
        ],
        compiler_params=pltpu.CompilerParams(vmem_limit_bytes=56 * 2**20),
        cost_estimate=pl.CostEstimate(
            flops=6 * rows * width * width, bytes_accessed=6 * width * width, transcendentals=0
        ),
        name="project",
    )(x, gain, a, marks, sels, *w)


def leave_kernel(mixed_ref, x_ref, bo_ref, a1_ref, gain_ref, mark_ref, sel_ref, *refs):
    *w_refs, order_ref, hidden_ref, n2_ref, low_ref, buf, sems = refs
    i = pl.program_id(0)
    width = x_ref.shape[1]

    @pl.when(i == 0)
    def _():
        load_weight(w_refs, order_ref, 3, buf, sems)

    mixed = mixed_ref[...].T

    @pl.when(i == 0)
    def _():
        weight_wait(w_refs, buf, sems)

    both = mm(mixed, buf[...])
    low = (both[:, width:] * mark_ref[3]).astype(BF)
    low_ref[0] = mm_nt(sel_ref[3], low).astype(BF)
    hidden = x_ref[...].astype(F32) + both[:, :width] + mm(low, bo_ref[...])
    hidden_ref[...] = hidden
    z, _ = norm_parts(hidden)
    n2 = (z * gain_ref[...]).astype(BF)
    n2_ref[:, :width] = n2
    low = (mm(n2, a1_ref[...]) * mark_ref[4]).astype(BF)
    n2_ref[:, width:] = low
    low_ref[1] = mm_nt(sel_ref[4], low).astype(BF)


def leave(mixed, x, bo, a1, gain, marks, sels, w):
    rows, width = x.shape
    AR, R = a1.shape[1], sels.shape[1]
    size = block_of(rows)
    return pl.pallas_call(
        leave_kernel,
        grid=(rows // size,),
        in_specs=[
            by_columns(width, size),
            by_rows(size, width),
            whole((AR, width)),
            whole((width, AR)),
            whole((1, width)),
            whole((6, 1, AR)),
            whole((6, R, AR)),
            *weight_specs(),
        ],
        out_specs=[
            by_rows(size, width),
            by_rows(size, width + AR),
            pl.BlockSpec((2, R, size), lambda i: (0, 0, i)),
        ],
        out_shape=[
            jax.ShapeDtypeStruct((rows, width), F32),
            jax.ShapeDtypeStruct((rows, width + AR), BF),
            jax.ShapeDtypeStruct((2, R, rows), BF),
        ],
        scratch_shapes=[pltpu.VMEM((width, width + AR), BF), pltpu.SemaphoreType.DMA((4,))],
        compiler_params=pltpu.CompilerParams(vmem_limit_bytes=56 * 2**20),
        cost_estimate=pl.CostEstimate(
            flops=4 * rows * width * width, bytes_accessed=2 * width * width, transcendentals=0
        ),
        name="leave_attention",
    )(mixed, x, bo, a1, gain, marks, sels, *w)


def feed_kernel(
    x_ref, up_ref, live_ref, b2_ref, mark_ref, sel_ref, low_ref, w_ref, acc1_ref, acc2_ref, ga_ref, gb_ref, s_ref, ld_ref
):
    width = up_ref.shape[1]

    @pl.when(pl.program_id(0) == 0)
    def _():
        acc1_ref[...] = jnp.zeros_like(acc1_ref)
        acc2_ref[...] = jnp.zeros_like(acc2_ref)
        seed = (up_ref[...].astype(F32) * live_ref[...]).astype(BF)
        s_ref[:, :width] = seed
        low = (mm_nt(seed, b2_ref[...]) * mark_ref[5]).astype(BF)
        s_ref[:, width:] = low
        ld_ref[...] = mm_nt(sel_ref[5], low).astype(BF)

    wide = w_ref.shape[3]
    first = w_ref[:, 0].reshape(-1, wide)
    second = w_ref[:, 1].reshape(-1, wide)
    upper = mm_nt(x_ref[...], first)
    cdf = 0.5 * (1.0 + lax.erf(upper * (0.5**0.5)))
    active = (upper * cdf).astype(BF)
    dactive = mm_nt(s_ref[...], second)
    slope = cdf + upper * jnp.exp(-0.5 * upper * upper) * (1.0 / (2.0 * jnp.pi) ** 0.5)
    dupper = (dactive * slope).astype(BF)
    acc1_ref[...] += mm(active, second)
    acc2_ref[...] += mm(dupper, first)
    ga_ref[...] = mm(ld_ref[...], active)
    gb_ref[...] = mm(low_ref[1], dupper)


def feed(x, upstream, live, b2, marks, sels, low, w):
    rows, width = upstream.shape
    blocks, _, h, wide = w.shape
    AR, R = wide - width, low.shape[1]
    step = blocks
    while step * h > 1280:
        step //= 2
    part = pl.BlockSpec((R, step * h), lambda i: (0, i))
    return pl.pallas_call(
        feed_kernel,
        grid=(blocks // step,),
        in_specs=[
            whole((rows, wide)),
            whole((rows, width)),
            whole((rows, 1)),
            whole((AR, width)),
            whole((6, 1, AR)),
            whole((6, R, AR)),
            whole((2, R, rows)),
            pl.BlockSpec((step, 2, h, wide), lambda i: (i, 0, 0, 0)),
        ],
        out_specs=[whole((rows, wide)), whole((rows, wide)), part, part],
        out_shape=[jax.ShapeDtypeStruct((rows, wide), F32)] * 2
        + [jax.ShapeDtypeStruct((R, blocks * h), F32)] * 2,
        scratch_shapes=[pltpu.VMEM((rows, wide), BF), pltpu.VMEM((R, rows), BF)],
        compiler_params=pltpu.CompilerParams(vmem_limit_bytes=60 * 2**20),
        cost_estimate=pl.CostEstimate(
            flops=8 * rows * wide * blocks * h, bytes_accessed=4 * blocks * h * wide, transcendentals=0
        ),
        name="feed_forward",
    )(x, upstream, live, b2, marks, sels, low, w)


def turn_kernel(
    acc1_ref, acc2_ref, hidden_ref, n2_ref, up_ref, live_ref, mixed_ref, bo_ref, a1_ref, b2_ref, gain_ref,
    mark_ref, sel_ref, low_ref, *refs
):
    *w_refs, order_ref, layer_ref, dhidden_ref, dmixed_ref, grad_ref, buf, sems = refs
    i = pl.program_id(0)
    width = hidden_ref.shape[1]

    @pl.when(i == 0)
    def _():
        load_weight(w_refs, order_ref, 3, buf, sems)
        grad_ref[...] = jnp.zeros_like(grad_ref)

    hidden = hidden_ref[...]
    seed = (up_ref[...].astype(F32) * live_ref[...]).astype(BF)
    low = (acc1_ref[:, width:] * mark_ref[5]).astype(BF)
    branch = acc1_ref[:, :width] + mm(low, b2_ref[...])
    layer_ref[...] = jnp.where(live_ref[...] > 0, hidden + branch, 0.0).astype(BF)
    grad_ref[3] += mm(mm_nt(sel_ref[5], low).astype(BF), seed)
    low = (acc2_ref[:, width:] * mark_ref[4]).astype(BF)
    grad_ref[2] += mm(mm_nt(sel_ref[4], low).astype(BF), n2_ref[:, :width])
    dn2 = acc2_ref[:, :width] + mm_nt(low, a1_ref[...])
    z, rate = norm_parts(hidden)
    dhidden = seed.astype(F32) + norm_back(z, rate, dn2 * gain_ref[...])
    dhidden_ref[...] = dhidden
    dattn = dhidden.astype(BF)
    grad_ref[1] += mm(low_ref[0], dattn)
    low = (mm_nt(dattn, bo_ref[...]) * mark_ref[3]).astype(BF)
    grad_ref[0] += mm_nt(mm_nt(sel_ref[3], low).astype(BF), mixed_ref[...])

    @pl.when(i == 0)
    def _():
        weight_wait(w_refs, buf, sems)

    dmixed_ref[...] = mm_nt(buf[...], jnp.concatenate([dattn, low], axis=1)).astype(BF)


def turn(acc1, acc2, hidden, n2, upstream, live, mixed, bo, a1, b2, gain, marks, sels, low, w):
    rows, width = hidden.shape
    AR, R = a1.shape[1], sels.shape[1]
    size = block_of(rows)
    return pl.pallas_call(
        turn_kernel,
        grid=(rows // size,),
        in_specs=[
            by_rows(size, width + AR),
            by_rows(size, width + AR),
            by_rows(size, width),
            by_rows(size, width + AR),
            by_rows(size, width),
            by_rows(size, 1),
            by_columns(width, size),
            whole((AR, width)),
            whole((width, AR)),
            whole((AR, width)),
            whole((1, width)),
            whole((6, 1, AR)),
            whole((6, R, AR)),
            pl.BlockSpec((2, R, size), lambda i: (0, 0, i)),
            *weight_specs(),
        ],
        out_specs=[by_rows(size, width), by_rows(size, width), by_columns(width, size), whole((4, R, width))],
        out_shape=[
            jax.ShapeDtypeStruct((rows, width), BF),
            jax.ShapeDtypeStruct((rows, width), F32),
            jax.ShapeDtypeStruct((width, rows), BF),
            jax.ShapeDtypeStruct((4, R, width), F32),
        ],
        scratch_shapes=[pltpu.VMEM((width, width + AR), BF), pltpu.SemaphoreType.DMA((4,))],
        compiler_params=pltpu.CompilerParams(vmem_limit_bytes=56 * 2**20),
        cost_estimate=pl.CostEstimate(
            flops=4 * rows * width * width, bytes_accessed=16 * rows * width, transcendentals=0
        ),
        name="turn",
    )(acc1, acc2, hidden, n2, upstream, live, mixed, bo, a1, b2, gain, marks, sels, low, *w)


def finish_kernel(
    x_ref, dhidden_ref, gain_ref, a_ref, mark_ref, sel_ref, low_ref, dq_ref, dk_ref, dk2_ref, dv_ref, dv2_ref, *refs
):
    *w_refs, order_ref, out_ref, grad_ref, bufs, sems = refs
    i = pl.program_id(0)
    width = x_ref.shape[1]

    @pl.when(i == 0)
    def _():
        for j in range(3):
            load_weight(w_refs, order_ref, j, bufs.at[j], sems.at[j])
        grad_ref[...] = jnp.zeros_like(grad_ref)

    z, rate = norm_parts(x_ref[...].astype(F32))
    n1 = (z * gain_ref[...]).astype(BF)
    dn1 = jnp.zeros(x_ref.shape, F32)
    for j, own in enumerate((dq_ref, dk_ref, dv_ref)):
        dy = own[...]
        if j:
            dy = (dy.astype(F32) + (dk2_ref, dv2_ref)[j - 1][...].astype(F32)).astype(BF)

        @pl.when(i == 0)
        def _():
            weight_wait(w_refs, bufs.at[j], sems.at[j])

        both = mm(dy.T, bufs[j])
        low = (both[:, width:] * mark_ref[j]).astype(BF)
        grad_ref[0, j] += mm(mm_nt(sel_ref[j], low).astype(BF), n1)
        grad_ref[1, j] += mm_nt(low_ref[j], dy)
        dn1 = dn1 + both[:, :width] + mm_nt(low, a_ref[j])
    out_ref[...] = (dhidden_ref[...] + norm_back(z, rate, dn1 * gain_ref[...])).astype(BF)


def finish(x, dhidden, gain, a, marks, sels, low, dq, dk, dk2, dv, dv2, w):
    rows, width = x.shape
    AR, R = a.shape[2], sels.shape[1]
    size = block_of(rows)
    return pl.pallas_call(
        finish_kernel,
        grid=(rows // size,),
        in_specs=[
            by_rows(size, width),
            by_rows(size, width),
            whole((1, width)),
            whole((3, width, AR)),
            whole((3, 1, AR)),
            whole((3, R, AR)),
            pl.BlockSpec((3, R, size), lambda i: (0, 0, i)),
        ]
        + [by_columns(width, size)] * 5
        + weight_specs(),
        out_specs=[by_rows(size, width), whole((2, 3, R, width))],
        out_shape=[
            jax.ShapeDtypeStruct((rows, width), BF),
            jax.ShapeDtypeStruct((2, 3, R, width), F32),
        ],
        scratch_shapes=[
            pltpu.VMEM((3, width, width + AR), BF),
            pltpu.SemaphoreType.DMA((3, 4)),
        ],
        compiler_params=pltpu.CompilerParams(vmem_limit_bytes=58 * 2**20),
        cost_estimate=pl.CostEstimate(
            flops=6 * rows * width * width, bytes_accessed=6 * width * width, transcendentals=0
        ),
        name="finish",
    )(x, dhidden, gain, a, marks, sels, low, dq, dk, dk2, dv, dv2, *w)


def body(
    frames,
    upstream,
    clip_frame_length,
    clip_adapter_index,
    gain1,
    gain2,
    w_qkv,
    w_out,
    w_up,
    w_down,
    qkv_a,
    qkv_b,
    out_a,
    out_b,
    fc1_a,
    fc1_b,
    fc2_a,
    fc2_b,
):
    C, LF, W = frames.shape
    pl_ = Place(C, LF)
    D, T, d, t = pl_.D, pl_.T, pl_.d, pl_.t
    Hc = w_qkv.shape[2]
    U = w_up.shape[1]
    A, R = fc1_a.shape[0], fc1_a.shape[2]
    AR = A * R
    rows = pl_.rows
    heads = W // HEAD

    meta = jnp.concatenate([clip_frame_length[:, None], clip_adapter_index], axis=1)
    metas = lax.all_gather(meta, "dp")
    qkvo = jnp.concatenate([w_qkv.transpose(0, 2, 1), w_out[None]]).reshape(4 * Hc, W // D)
    qkvo = lax.all_to_all(qkvo, "dp", 0, 1, tiled=True)
    qkvo_low = jnp.concatenate(
        [qkv_b.transpose(0, 3, 1, 2).reshape(3, Hc, AR), out_a.transpose(1, 0, 2).reshape(1, Hc, AR)]
    ).reshape(D, 4 * Hc // D, AR)
    qkvo = jnp.concatenate([qkvo, lax.dynamic_index_in_dim(qkvo_low, d, 0, False)], axis=1)
    ffn = jnp.stack([w_up.T, w_down])
    ffn = lax.all_to_all(ffn, "dp", 1, 2, tiled=True)
    ffn_low = jnp.stack(
        [fc1_b.transpose(2, 0, 1).reshape(U, AR), fc2_a.transpose(1, 0, 2).reshape(U, AR)]
    ).reshape(2, D, U // D, AR)
    ffn = jnp.concatenate([ffn, lax.dynamic_index_in_dim(ffn_low, d, 1, False)], axis=2)
    count = qkvo.shape[0]
    half = count // 2
    heads_part = Gather(pl_, qkvo[:half], qkvo[half:])
    frames_by = by_chip(pl_, frames)
    heads_part.line()
    frames_by, ffn, metas = tie([heads_part], frames_by, ffn, metas)
    all_ffn = lax.all_gather(ffn, ("tensor", "dp"))
    frames_in = to_clip(pl_, frames_by)
    heads_part.middle()
    heads_part.last()
    (frames_in,) = tie([heads_part], frames_in)
    heads_part.core()
    weights, line = heads_weights(pl_, heads_part.parts)

    g = t // pl_.Q
    here = metas[d - pl_.core + g // C, g % C]
    length, picks = here[0], here[1:]
    marks = (jnp.arange(AR)[None, :] // R == picks[:, None]).astype(F32)

    flat_a = lambda a: a.swapaxes(-3, -2).reshape(*a.shape[:-3], W, AR)
    flat_b = lambda b: b.reshape(AR, W)
    marks = marks[:, None, :]
    sels = (jnp.arange(AR)[None, None, :] == (picks * R)[:, None, None] + jnp.arange(R)[None, :, None]).astype(BF)
    live = (pl_.positions(pl_.core, t % pl_.Q) < length).astype(F32)[:, None]
    keys_live = jnp.concatenate([pl_.positions(c, s) for c, s in group_places(pl_)]) < length
    bias = jnp.where(keys_live, 0.0, -1e30).astype(F32)[None]
    gain1, gain2 = gain1[None], gain2[None]
    a_all = flat_a(qkv_a)

    q, k, v, low1 = project(frames_in, gain1, a_all, marks[:3], sels[:3], weights)
    ks, vs = group_values(pl_, k), group_values(pl_, v)
    q, ks, vs, upstream = tie([], q, ks, vs, upstream)
    upstream_in = to_clip(pl_, by_chip(pl_, upstream))
    mixed, lse = attend(q, ks, vs, bias)
    bo, a1, b2 = flat_b(out_b), flat_a(fc1_a), flat_b(fc2_b)
    hidden, n2, low2 = leave(mixed, frames_in, bo, a1, gain2, marks, sels, weights)
    hidden, n2, low2, upstream_in = tie([], hidden, n2, low2, upstream_in)
    acc1, acc2, unit_a, unit_b = feed(n2, upstream_in, live, b2, marks, sels, low2, all_ffn)
    layer_rows, dhidden, dmixed, grads2 = turn(
        acc1, acc2, hidden, n2, upstream_in, live, mixed, bo, a1, b2, gain2, marks, sels, low2, weights
    )
    layer_output = from_clip(pl_, layer_rows)
    head_order = places(pl_, True).reshape(T, D)[:, d] % T
    clips = metas.reshape(D // 2, 2 * C, 7)[:, :, 1:]
    clips = jnp.repeat(clips, pl_.Q, axis=1)[:, None]
    clips = jnp.broadcast_to(clips, (D // 2, 2, T, 6)).reshape(D * T, 6)
    hot = (clips[:, :, None] == jnp.arange(A)).astype(BF)

    def owned(terms, picks_of):
        sizes = [v.shape[2] for v in terms]
        sent = jnp.concatenate([v.astype(BF) for v in terms], axis=2)
        sent = sent.reshape(D, R // D, T, -1).transpose(0, 2, 1, 3).reshape(D * T, R // D, -1)
        got = lax.all_to_all(sent, ("dp", "tensor"), 0, 0)
        out, at = [], 0
        for size, j in zip(sizes, picks_of):
            out.append(
                jnp.einsum("sa,srw->arw", hot[:, j], got[:, :, at : at + size], preferred_element_type=F32)
            )
            at += size
        return out

    by_tensor = lambda v: v.reshape(R, T, -1)

    def by_head(v):
        if line:
            v = v.reshape(R, 2, T, -1).swapaxes(1, 2)
        return jnp.take(by_tensor(v), head_order, axis=1)

    out_ga, out_gb, fc1_ga, fc2_gb, fc1_gb, fc2_ga = owned(
        [by_head(grads2[0]), *map(by_tensor, (grads2[1], grads2[2], grads2[3], unit_b, unit_a))],
        (3, 3, 4, 5, 4, 5),
    )

    dq, *dkv = attend_back(q, ks, vs, bias, lse, mixed, dmixed)
    dks, dvs = dkv[: len(dkv) // 2], dkv[len(dkv) // 2 :]
    dk2, dv2 = group_received(pl_, dks), group_received(pl_, dvs)
    early = (out_ga, out_gb, fc1_ga, fc2_gb, fc1_gb, fc2_ga)
    dq, layer_output, early = tie([], dq, layer_output, early)
    out_ga, out_gb, fc1_ga, fc2_gb, fc1_gb, fc2_ga = early
    dframes, grads1 = finish(
        frames_in, dhidden, gain1, a_all, marks[:3], sels[:3], low1, dq, dks[0], dk2, dvs[0], dv2, weights
    )
    frames_grad = from_clip(pl_, dframes).astype(F32)

    late = owned(
        [by_tensor(grads1[0, j]) for j in range(3)] + [by_head(grads1[1, j]) for j in range(3)],
        (0, 1, 2, 0, 1, 2),
    )
    flip = lambda a: jnp.swapaxes(a, -1, -2)
    return (
        layer_output,
        frames_grad,
        flip(jnp.stack(late[:3])),
        jnp.stack(late[3:]),
        flip(out_ga),
        out_gb,
        flip(fc1_ga),
        fc1_gb,
        flip(fc2_ga),
        fc2_gb,
    )


def solution(mesh):
    placed = (
        P("dp", "tensor", None),
        P("dp", "tensor", None),
        P("dp"),
        P("dp", None),
        P(),
        P(),
        P(None, "dp", "tensor"),
        P("tensor", "dp"),
        P("dp", "tensor"),
        P("tensor", "dp"),
        P(),
        P(None, None, None, "tensor"),
        P(None, "tensor", None),
        P(),
        P(),
        P(None, None, "tensor"),
        P(None, "tensor", None),
        P(),
    )
    return jax.shard_map(
        body,
        mesh=mesh,
        in_specs=placed,
        out_specs=(
            P("dp", "tensor", None),
            P("dp", "tensor", None),
            P(None, None, "tensor", "dp"),
            P(None, None, "dp", "tensor"),
            P(None, "tensor", "dp"),
            P(None, "dp", "tensor"),
            P(None, "tensor", "dp"),
            P(None, "dp", "tensor"),
            P(None, "tensor", "dp"),
            P(None, "dp", "tensor"),
        ),
        check_vma=False,
    )
```

time: 924 us -> 608 us (0.66)
  matrix products: 433 us -> 1.52 us
  Pallas kernels: 0 us -> 222 us
  local copies, waits for them, and re-layouts: 121 us -> 37.9 us
  other arithmetic: 88.6 us -> 31.3 us
  waiting for transfers between devices: 201 us -> 237 us
    dot_general x160 -> x12, matrix products: 433 us -> 1.52 us  [owned(): jnp.einsum('sa,srw->arw', hot[:, j], got[:, :, at:at + size], preferred_e...]
    pallas_call x0 -> x7, Pallas kernels: none -> 222 us  [the longest x1 59.7 us: feed(): pl.pallas_call(feed_kernel, grid=(blocks // step,), in_specs=[whole((rows...]
    ppermute x0 -> x10, waiting for transfers between devices: none -> 108 us  [the longest x8 57 us: ring(): out.append(lax.ppermute(out[-1], axis, perm))]
    all_to_all x2, waiting for transfers between devices: 66.8 us -> 37.5 us  [from_clip(): both = lax.all_to_all(y.reshape(pl_.T, pl_.S, W), 'tensor', 0, 0)]
    slice x8 -> x11, local copies, waits for them, and re-layouts: 29.1 us -> 2.85 us  [the longest x1 0.96 us: body(): grads2[0]]
    all_to_all x4, waiting for transfers between devices: 86.5 us -> 64.5 us  [the longest x2 39.8 us: to_clip(): return lax.all_to_all(both, 'tensor', 0, 0).reshape(pl_.rows, both.shape[2])]
    convert_element_type x27 -> x7, other arithmetic: 22.5 us -> 0.67 us  [the longest x1 0.26 us: body(): frames_grad = from_clip(pl_, dframes).astype(F32)]
    while x3 -> x0, local copies, waits for them, and re-layouts: 19.9 us -> none  [attend(): return lax.map(head, (q, k, v))]
  transfers between devices with their start and end apart: 17 -> 29, of which waited for: 11 -> 21; matrix products, arithmetic and copies ran while one was open for 32% -> 10% of each run, Pallas kernels for 0% -> 20%
where the time goes in v2:
time: 608 us; the launch traced here: 602 us
  waiting for transfers between devices  237 us (39%)
  Pallas kernels  222 us (37%)
  starting transfers between devices  52.3 us (9%)
  local copies, waits for them, and re-layouts  37.9 us (6%)
  other arithmetic  31.3 us (5%)
  between operations  14.9 us (2%)
    pallas_call x1, Pallas kernels, feed(): pl.pallas_call(feed_kernel, grid=(blocks // step,), in_specs=[whole((rows...  59.7 us
    ppermute x8, waiting for transfers between devices, ring(): out.append(lax.ppermute(out[-1], axis, perm))  57 us
    pallas_call x1, Pallas kernels, attend_back(): pl.pallas_call(kernel, grid=(heads,), in_specs=[head] * (1 + 2 * n) + [pl...  52.4 us
    ppermute x2, waiting for transfers between devices, pair(): return jnp.stack([v, lax.ppermute(v, 'tensor', perm)])  51.2 us
    all_to_all x2, waiting for transfers between devices, to_clip(): return lax.all_to_all(both, 'tensor', 0, 0).reshape(pl_.rows, both.shape[2])  39.8 us
    all_to_all x2, waiting for transfers between devices, from_clip(): both = lax.all_to_all(y.reshape(pl_.T, pl_.S, W), 'tensor', 0, 0)  37.5 us
    pallas_call x1, Pallas kernels, attend(): pl.pallas_call(kernel, grid=(heads,), in_specs=[head] * (1 + 2 * n) + [pl...  30.5 us
    pallas_call x1, Pallas kernels, finish(): pl.pallas_call(finish_kernel, grid=(rows // size,), in_specs=[by_rows(siz...  26.8 us
  transfers between devices with their start and end apart: 29, of which 21 were waited for; matrix products, arithmetic and copies ran while one was open for 10% of the time, Pallas kernels for 20%

profile of v2, /device:TPU:0, one launch (start us, length us, event | category | flops | bytes accessed | tf_op | source)
XLA Modules:
  0.0 602.3 jit_solution(11655975994239241287)
XLA Ops:
  9.2 4.2 all-to-all-start
  18.9 3.1 all-to-all-done
  22.0 3.5 all-to-all-start.1
  42.5 5.2 all-gather.2
  49.2 3.2 collective-permute-done.3
  58.6 4.2 collective-permute-done.4
  74.5 3.8 all-to-all-start.2
  80.3 33.4 %collective-permute-done.7 = bf16[4,80,1408]{2,1,0:T(8,128)(2,1)} collective-permute-done((bf16[4,80,1408]{2,1,0:T(8,128)(2,1)}, bf16[4,80,1408]{2,1,0:T(8,128)(2,1)}, u32[]{:S(2)}, u32[]{:S(2)}) %collective-permute-start.7) | collective-permute-done | bytes 901152 | tf_op jit(solution)/shard_map/ppermute | solution.py:105
  117.9 2.7 collective-permute-start.10
  120.6 44.3 %collective-permute-done.8 = bf16[2,4,80,1408]{3,2,1,0:T(8,128)(2,1)S(1)} collective-permute-done((bf16[2,4,80,1408]{3,2,1,0:T(8,128)(2,1)S(1)}, bf16[2,4,80,1408]{3,2,1,0:T(8,128)(2,1)S(1)}, u32[]{:S(2)}, u32[]{:S(2)}) %collective-permute-start.8) | collective-permute-done | bytes 1802272 | tf_op jit(solution)/shard_map/ppermute | solution.py:91
  167.1 17.7 %collective-permute-done.10 = bf16[2,4,80,1408]{3,2,1,0:T(8,128)(2,1)S(1)} collective-permute-done((bf16[2,4,80,1408]{3,2,1,0:T(8,128)(2,1)S(1)}, bf16[2,4,80,1408]{3,2,1,0:T(8,128)(2,1)S(1)}, u32[]{:S(2)}, u32[]{:S(2)}) %collective-permute-start.10) | collective-permute-done | bytes 1802272 | tf_op jit(solution)/shard_map/ppermute | solution.py:105
  193.6 5.2 collective-permute-done.12
  198.7 24.6 %project.1 = (bf16[1280,768]{1,0:T(8,128)(2,1)}, bf16[1280,768]{1,0:T(8,128)(2,1)}, bf16[1280,768]{1,0:T(8,128)(2,1)}, bf16[3,16,768]{2,1,0:T(8,128)(2,1)}) custom-call(bf16[768,1280]{1,0:T(8,128)(2,1)} %bitcast.276, f32[1,1280]{1,0:T(1,128)} %broadcast_in_dim.73.gain_ref, bf16[3,1280,128]{2,1,0:T(8,128)(2,1)} %copy.201.a_ref, ...), custom_call_target="tpu_custom_call" | custom-call | flops 7549747200 | bytes 9830400 | tf_op jit(solution)/shard_map/project/pallas_call | solution.py:398
  223.9 3.8 collective-permute-done.13.refs_2_
  227.7 2.8 collective-permute-done.14.refs_4_
  236.4 7.2 %all-to-all-start.3 = ((bf16[8,96,1280]{2,1,0:T(8,128)(2,1)}), bf16[8,96,1280]{2,1,0:T(8,128)(2,1)S(1)}, u32[]{:S(2)}, u32[]{:S(2)}) async-start(bf16[8,96,1280]{2,1,0:T(8,128)(2,1)} %bitcast.286), calls=%async_computation.3 | async-start | bytes 3932160 | tf_op jit(solution)/shard_map/all_to_all | solution.py:73
  247.8 30.5 %attend_forward.1 = (bf16[1280,768]{1,0:T(8,128)(2,1)}, f32[16,1,768]{2,1,0:T(1,128)}) custom-call(bf16[1280,768]{1,0:T(8,128)(2,1)} %get-tuple-element.71.refs_0_, bf16[1280,768]{1,0:T(8,128)(2,1)} %get-tuple-element.72.refs_1_, bf16[1280,768]{1,0:T(8,128)(2,1)} %collective-permute-done.13.refs_2_, bf16[1280,768]{1,0:T(8,128)(2,1)} %get-tuple-element.74.refs_3_, ...), custom_call_target="tpu_custom_call" | custom-call | flops 19327352832 | bytes 5898240 | tf_op jit(solution)/shard_map/attend_forward/pallas_call | solution.py:211
  278.3 12.0 %leave_attention.1 = (f32[768,1280]{1,0:T(8,128)}, bf16[768,1408]{1,0:T(8,128)(2,1)}, bf16[2,16,768]{2,1,0:T(8,128)(2,1)}) custom-call(bf16[1280,768]{1,0:T(8,128)(2,1)} %get-tuple-element.77.mixed_ref.refs_7_, bf16[768,1280]{1,0:T(8,128)(2,1)} %bitcast.277, bf16[128,1280]{1,0:T(8,128)(2,1)} %bitcast.297, bf16[1280,128]{1,0:T(8,128)(2,1)} %copy.202.a1_ref, ...), custom_call_target="tpu_custom_call" | custom-call | flops 5033164800 | bytes 3276800 | tf_op jit(solution)/shard_map/leave_attention/pallas_call | solution.py:455
  290.3 39.8 %all-to-all-done.3 = bf16[8,96,1280]{2,1,0:T(8,128)(2,1)S(1)} async-done(((bf16[8,96,1280]{2,1,0:T(8,128)(2,1)}), bf16[8,96,1280]{2,1,0:T(8,128)(2,1)S(1)}, u32[]{:S(2)}, u32[]{:S(2)}) %all-to-all-start.3) | async-done | bytes 1966112 | tf_op jit(solution)/shard_map/all_to_all | solution.py:73
  330.0 3.3 all-gather.5.cloned.1.call-done
  333.3 59.7 %feed_forward.1 = (f32[768,1408]{1,0:T(8,128)}, f32[768,1408]{1,0:T(8,128)}, f32[16,5120]{1,0:T(8,128)}, f32[16,5120]{1,0:T(8,128)}) custom-call(bf16[768,1408]{1,0:T(8,128)(2,1)} %get-tuple-element.82.x_ref.n2_ref, bf16[768,1280]{1,0:T(8,128)(2,1)} %bitcast.284, f32[768,1]{1,0:T(8,128)} %reshape.724.live_ref, bf16[128,1280]{1,0:T(8,128)(2,1)} %bitcast.310, ...), custom_call_target="tpu_custom_call" | custom-call | flops 44291850240 | bytes 28835840 | tf_op jit(solution)/shard_map/feed_forward/pallas_call | solution.py:525
  393.0 16.2 %turn.1 = (bf16[768,1280]{1,0:T(8,128)(2,1)}, f32[768,1280]{1,0:T(8,128)}, bf16[1280,768]{1,0:T(8,128)(2,1)}, f32[4,16,1280]{2,1,0:T(8,128)}) custom-call(f32[768,1408]{1,0:T(8,128)} %get-tuple-element.86.acc1_ref, f32[768,1408]{1,0:T(8,128)} %get-tuple-element.87.acc2_ref, f32[768,1280]{1,0:T(8,128)} %get-tuple-element.88.hidden_ref, ...), custom_call_target="tpu_custom_call" | custom-call | flops 5033164800 | bytes 15728640 | tf_op jit(solution)/shard_map/turn/pallas_call | solution.py:591
  414.0 3.7 all-to-all-start.5
  418.0 15.4 %all-to-all-done.5 = bf16[32,4,1920]{2,1,0:T(4,128)(2,1)S(1)} async-done(((bf16[32,4,1920]{2,1,0:T(4,128)(2,1)}), bf16[32,4,1920]{2,1,0:T(4,128)(2,1)S(1)}, u32[]{:S(2)}, u32[]{:S(2)}) %all-to-all-start.5) | async-done | bytes 491552 | tf_op jit(solution)/shard_map/all_to_all | solution.py:791
  433.4 3.8 all-to-all-start.4
  437.2 52.4 %attend_backward.1 = (bf16[1280,768]{1,0:T(8,128)(2,1)}, bf16[1280,768]{1,0:T(8,128)(2,1)}, bf16[1280,768]{1,0:T(8,128)(2,1)}, bf16[1280,768]{1,0:T(8,128)(2,1)}, bf16[1280,768]{1,0:T(8,128)(2,1)}) custom-call(bf16[1280,768]{1,0:T(8,128)(2,1)} %get-tuple-element.71.refs_0_, bf16[1280,768]{1,0:T(8,128)(2,1)} %get-tuple-element.72.refs_1_, ...), custom_call_target="tpu_custom_call" | custom-call | flops 38654705664 | bytes 11796480 | tf_op jit(solution)/shard_map/attend_backward/pallas_call | solution.py:280
  491.5 4.9 collective-permute-done.16
  498.2 26.8 %finish.1 = (bf16[768,1280]{1,0:T(8,128)(2,1)}, f32[2,3,16,1280]{3,2,1,0:T(8,128)}) custom-call(bf16[768,1280]{1,0:T(8,128)(2,1)} %bitcast.278, f32[768,1280]{1,0:T(8,128)} %get-tuple-element.96.dhidden_ref, f32[1,1280]{1,0:T(1,128)} %broadcast_in_dim.73.gain_ref, bf16[3,1280,128]{2,1,0:T(8,128)(2,1)} %copy.201.a_ref, f32[3,1,128]{2,1,0:T(1,128)} %reshape.666.mark_ref, ...), custom_call_target="tpu_custom_call" | custom-call | flops 7549747200 | bytes 9830400 | tf_op jit(solution)/shard_map/finish/pallas_call | solution.py:664
  525.0 6.1 %all-to-all-start.6 = ((bf16[8,96,1280]{2,1,0:T(8,128)(2,1)}), bf16[8,96,1280]{2,1,0:T(8,128)(2,1)S(1)}, u32[]{:S(2)}, u32[]{:S(2)}) async-start(bf16[8,96,1280]{2,1,0:T(8,128)(2,1)} %bitcast.292), calls=%async_computation.6 | async-start | bytes 3932160 | tf_op jit(solution)/shard_map/all_to_all | solution.py:78
  539.4 37.5 %all-to-all-done.6 = bf16[8,96,1280]{2,1,0:T(8,128)(2,1)S(1)} async-done(((bf16[8,96,1280]{2,1,0:T(8,128)(2,1)}), bf16[8,96,1280]{2,1,0:T(8,128)(2,1)S(1)}, u32[]{:S(2)}, u32[]{:S(2)}) %all-to-all-start.6) | async-done | bytes 1966112 | tf_op jit(solution)/shard_map/all_to_all | solution.py:78
  576.9 2.7 all-to-all-start.7
  580.9 9.3 %all-to-all-done.7 = bf16[32,4,960]{2,1,0:T(4,128)(2,1)S(1)} async-done(((bf16[32,4,960]{2,1,0:T(4,128)(2,1)}), bf16[32,4,960]{2,1,0:T(4,128)(2,1)S(1)}, u32[]{:S(2)}, u32[]{:S(2)}) %all-to-all-start.7) | async-done | bytes 245792 | tf_op jit(solution)/shard_map/all_to_all | solution.py:791
  (217 shorter events, 94.4 us)
Async XLA Ops:
  9.2 12.7 %all-to-all-start = ((bf16[4,160,320]{2,1,0:T(8,128)(2,1)}), bf16[4,160,320]{2,1,0:T(8,128)(2,1)S(1)}, u32[]{:S(2)}, u32[]{:S(2)}) async-start(bf16[4,160,320]{2,1,0:T(8,128)(2,1)} %pad_maximum_fusion.11), calls=%async_computation | async-start | bytes 983040 | tf_op jit(solution)/shard_map/all_to_all | solution.py:728
  14.5 48.3 %collective-permute-start.6 = (bf16[4,1,96,1280]{3,2,0,1:T(8,128)(2,1)}, bf16[4,1,96,1280]{3,2,0,1:T(8,128)(2,1)}, u32[]{:S(2)}, u32[]{:S(2)}) collective-permute-start(bf16[4,1,96,1280]{3,2,0,1:T(8,128)(2,1)} %select_bitcast_fusion.3), channel_id=1, source_target_pairs={{0,8},{8,0},{16,24},{24,16},{1,9},{9,1},{17,25},{25,17},{2,10},{10... | collective-permute-start | bytes 2949128 | tf_op jit(solution)/shard_map/ppermute | solution.py:53
  22.0 30.4 %all-to-all-start.1 = ((bf16[2,640,320]{2,0,1:T(2,128)(2,1)}), bf16[2,640,320]{2,0,1:T(2,128)(2,1)S(1)}, u32[]{:S(2)}, u32[]{:S(2)}) async-start(bf16[2,640,320]{2,0,1:T(2,128)(2,1)} %copy.196), calls=%async_computation.1 | async-start | bytes 1966080 | tf_op jit(solution)/shard_map/all_to_all | solution.py:734
  25.5 307.8 %all-gather.5.cloned.1.call-start = ((), (), s32[]{:S(2)}) async-start(), calls=%async_computation.8 | async-start | bytes 29736960 | tf_op jit(solution)/shard_map/all_gather | solution.py:745
  36.9 10.9 %collective-permute-start = (bf16[80,1408]{1,0:T(8,128)(2,1)}, bf16[80,1408]{1,0:T(8,128)(2,1)}, u32[]{:S(2)}, u32[]{:S(2)}) collective-permute-start(bf16[80,1408]{1,0:T(8,128)(2,1)} %get-tuple-element.185), channel_id=1, source_target_pairs={{0,2},{1,3},{2,4},{3,5},{4,6},{5,7},{6,0},{7,1},{8,10},{9,11},{10,... | collective-permute-start | bytes 675848 | tf_op jit(solution)/shard_map/ppermute | solution.py:91
  39.1 13.3 %collective-permute-start.3 = (bf16[80,1408]{1,0:T(8,128)(2,1)S(1)}, bf16[80,1408]{1,0:T(8,128)(2,1)}, u32[]{:S(2)}, u32[]{:S(2)}) collective-permute-start(bf16[80,1408]{1,0:T(8,128)(2,1)S(1)} %get-tuple-element.184), channel_id=1, source_target_pairs={{0,2},{1,3},{2,4},{3,5},{4,6},{5,7},{6,0},{7,1},{8,10},{9,11},{10,... | collective-permute-start | bytes 675848 | tf_op jit(solution)/shard_map/ppermute | solution.py:91
  47.8 10.1 %collective-permute-start.1 = (bf16[80,1408]{1,0:T(8,128)(2,1)}, bf16[80,1408]{1,0:T(8,128)(2,1)}, u32[]{:S(2)}, u32[]{:S(2)}) collective-permute-start(bf16[80,1408]{1,0:T(8,128)(2,1)} %collective-permute-done), channel_id=1, source_target_pairs={{0,2},{1,3},{2,4},{3,5},{4,6},{5,7},{6,0},{7,1},{8,10},{9,11},{10,... | collective-permute-start | bytes 675848 | tf_op jit(solution)/shard_map/ppermute | solution.py:91
  52.4 10.4 %collective-permute-start.4 = (bf16[80,1408]{1,0:T(8,128)(2,1)}, bf16[80,1408]{1,0:T(8,128)(2,1)S(1)}, u32[]{:S(2)}, u32[]{:S(2)}) collective-permute-start(bf16[80,1408]{1,0:T(8,128)(2,1)} %collective-permute-done.3), channel_id=1, source_target_pairs={{0,2},{1,3},{2,4},{3,5},{4,6},{5,7},{6,0},{7,1},{8,10},{9,11},{10,... | collective-permute-start | bytes 675848 | tf_op jit(solution)/shard_map/ppermute | solution.py:91
  58.0 9.9 %collective-permute-start.2 = (bf16[80,1408]{1,0:T(8,128)(2,1)}, bf16[80,1408]{1,0:T(8,128)(2,1)S(1)}, u32[]{:S(2)}, u32[]{:S(2)}) collective-permute-start(bf16[80,1408]{1,0:T(8,128)(2,1)} %collective-permute-done.1), channel_id=1, source_target_pairs={{0,2},{1,3},{2,4},{3,5},{4,6},{5,7},{6,0},{7,1},{8,10},{9,11},{10,... | collective-permute-start | bytes 675848 | tf_op jit(solution)/shard_map/ppermute | solution.py:91
  62.8 9.0 %collective-permute-start.5 = (bf16[80,1408]{1,0:T(8,128)(2,1)S(1)}, bf16[80,1408]{1,0:T(8,128)(2,1)S(1)}, u32[]{:S(2)}, u32[]{:S(2)}) collective-permute-start(bf16[80,1408]{1,0:T(8,128)(2,1)S(1)} %collective-permute-done.4), channel_id=1, source_target_pairs={{0,2},{1,3},{2,4},{3,5},{4,6},{5,7},{6,0},{7,1},{8,10},{9,11},{10,... | collective-permute-start | bytes 675848 | tf_op jit(solution)/shard_map/ppermute | solution.py:91
  73.0 40.8 %collective-permute-start.7 = (bf16[4,80,1408]{2,1,0:T(8,128)(2,1)}, bf16[4,80,1408]{2,1,0:T(8,128)(2,1)}, u32[]{:S(2)}, u32[]{:S(2)}) collective-permute-start(bf16[4,80,1408]{2,1,0:T(8,128)(2,1)} %pad_maximum_fusion.7), channel_id=1, source_target_pairs={{0,1},{1,0},{2,3},{3,2},{4,5},{5,4},{6,7},{7,6},{8,9},{9,8},{10,11... | collective-permute-start | bytes 2703368 | tf_op jit(solution)/shard_map/ppermute | solution.py:105
  74.5 112.4 %all-to-all-start.2 = ((bf16[8,96,1280]{2,1,0:T(8,128)(2,1)}), bf16[8,96,1280]{2,1,0:T(8,128)(2,1)S(1)}, u32[]{:S(2)}, u32[]{:S(2)}) async-start(bf16[8,96,1280]{2,1,0:T(8,128)(2,1)} %bitcast.283), calls=%async_computation.2 | async-start | bytes 3932160 | tf_op jit(solution)/shard_map/all_to_all | solution.py:73
  78.3 39.3 %collective-permute-start.9 = (bf16[4,80,1408]{2,1,0:T(8,128)(2,1)S(1)}, bf16[4,80,1408]{2,1,0:T(8,128)(2,1)S(1)}, u32[]{:S(2)}, u32[]{:S(2)}) collective-permute-start(bf16[4,80,1408]{2,1,0:T(8,128)(2,1)S(1)} %pad_maximum_fusion.8), channel_id=1, source_target_pairs={{0,16},{8,24},{16,0},{24,8},{1,17},{9,25},{17,1},{25,9},{2,18},{10... | collective-permute-start | bytes 2703368 | tf_op jit(solution)/shard_map/ppermute | solution.py:91
  115.5 49.4 %collective-permute-start.8 = (bf16[2,4,80,1408]{3,2,1,0:T(8,128)(2,1)S(1)}, bf16[2,4,80,1408]{3,2,1,0:T(8,128)(2,1)S(1)}, u32[]{:S(2)}, u32[]{:S(2)}) collective-permute-start(bf16[2,4,80,1408]{3,2,1,0:T(8,128)(2,1)S(1)} %get-tuple-element.174), channel_id=1, source_target_pairs={{0,16},{8,24},{16,0},{24,8},{1,17},{9,25},{17,1},{25,9},{2,18},{10... | collective-permute-start | bytes 5406728 | tf_op jit(solution)/shard_map/ppermute | solution.py:91
  117.9 66.9 %collective-permute-start.10 = (bf16[2,4,80,1408]{3,2,1,0:T(8,128)(2,1)S(1)}, bf16[2,4,80,1408]{3,2,1,0:T(8,128)(2,1)S(1)}, u32[]{:S(2)}, u32[]{:S(2)}) collective-permute-start(bf16[2,4,80,1408]{3,2,1,0:T(8,128)(2,1)S(1)} %get-tuple-element.172), channel_id=1, source_target_pairs={{0,1},{1,0},{2,3},{3,2},{4,5},{5,4},{6,7},{7,6},{8,9},{9,8},{10,11... | collective-permute-start | bytes 5406728 | tf_op jit(solution)/shard_map/ppermute | solution.py:105
  186.9 11.8 %copy-start = (bf16[8,96,1280]{2,1,0:T(8,128)(2,1)}, bf16[8,96,1280]{2,1,0:T(8,128)(2,1)S(1)}, u32[]{:S(2)}) copy-start(bf16[8,96,1280]{2,1,0:T(8,128)(2,1)S(1)} %all-to-all-done.2) | copy-start | bytes 5898244
  186.9 6.7 %collective-permute-start.11 = (bf16[2,2,4,80,1408]{4,3,2,1,0:T(8,128)(2,1)}, bf16[2,2,4,80,1408]{4,3,2,1,0:T(8,128)(2,1)}, u32[]{:S(2)}, u32[]{:S(2)}) collective-permute-start(bf16[2,2,4,80,1408]{4,3,2,1,0:T(8,128)(2,1)} %pad_maximum_fusion), channel_id=1, source_target_pairs={{0,8},{8,0},{16,24},{24,16},{1,9},{9,1},{17,25},{25,17},{2,10},{10... | collective-permute-start | bytes 10813448 | tf_op jit(solution)/shard_map/ppermute | solution.py:53
  186.9 11.8 %collective-permute-start.12 = (bf16[2,2,4,80,1408]{4,3,2,1,0:T(8,128)(2,1)}, bf16[2,2,4,80,1408]{4,3,2,1,0:T(8,128)(2,1)}, u32[]{:S(2)}, u32[]{:S(2)}) collective-permute-start(bf16[2,2,4,80,1408]{4,3,2,1,0:T(8,128)(2,1)} %pad_maximum_fusion.1), channel_id=1, source_target_pairs={{0,8},{8,0},{16,24},{24,16},{1,9},{9,1},{17,25},{25,17},{2,10},{10... | collective-permute-start | bytes 10813448 | tf_op jit(solution)/shard_map/ppermute | solution.py:53
  191.3 32.0 %copy-start.10 = (bf16[6,16,128]{2,1,0:T(8,128)(2,1)}, bf16[6,16,128]{2,1,0:T(8,128)(2,1)S(1)}, u32[]{:S(2)}) copy-start(bf16[6,16,128]{2,1,0:T(8,128)(2,1)S(1)} %fusion.28.sel_ref) | copy-start | bytes 73732
  223.3 11.5 %copy-start.2 = (bf16[4,192,1280]{2,1,0:T(8,128)(2,1)S(1)}, bf16[4,192,1280]{2,1,0:T(8,128)(2,1)}, u32[]{:S(2)}) copy-start(bf16[4,192,1280]{2,1,0:T(8,128)(2,1)} %param.21) | copy-start | bytes 5898244
  223.3 4.4 collective-permute-start.13
  223.5 7.0 %collective-permute-start.14 = (bf16[1280,768]{1,0:T(8,128)(2,1)}, bf16[1280,768]{1,0:T(8,128)(2,1)}, u32[]{:S(2)}, u32[]{:S(2)}) collective-permute-start(bf16[1280,768]{1,0:T(8,128)(2,1)} %get-tuple-element.74.refs_3_), channel_id=1, source_target_pairs={{0,8},{8,0},{16,24},{24,16},{1,9},{9,1},{17,25},{25,17},{2,10},{10... | collective-permute-start | bytes 5898248 | tf_op jit(solution)/shard_map/ppermute | solution.py:53
  232.2 2.6 collective-permute-start.15
  236.4 93.6 %all-to-all-start.3 = ((bf16[8,96,1280]{2,1,0:T(8,128)(2,1)}), bf16[8,96,1280]{2,1,0:T(8,128)(2,1)S(1)}, u32[]{:S(2)}, u32[]{:S(2)}) async-start(bf16[8,96,1280]{2,1,0:T(8,128)(2,1)} %bitcast.286), calls=%async_computation.3 | async-start | bytes 3932160 | tf_op jit(solution)/shard_map/all_to_all | solution.py:73
  414.0 19.4 %all-to-all-start.5 = ((bf16[32,4,1920]{2,1,0:T(4,128)(2,1)}), bf16[32,4,1920]{2,1,0:T(4,128)(2,1)S(1)}, u32[]{:S(2)}, u32[]{:S(2)}) async-start(bf16[32,4,1920]{2,1,0:T(4,128)(2,1)} %bitcast.76), calls=%async_computation.5 | async-start | bytes 983040 | tf_op jit(solution)/shard_map/all_to_all | solution.py:791
  433.4 57.2 %all-to-all-start.4 = ((bf16[8,96,1280]{2,1,0:T(8,128)(2,1)}), bf16[8,96,1280]{2,1,0:T(8,128)(2,1)S(1)}, u32[]{:S(2)}, u32[]{:S(2)}) async-start(bf16[8,96,1280]{2,1,0:T(8,128)(2,1)} %bitcast.291), calls=%async_computation.4 | async-start | bytes 3932160 | tf_op jit(solution)/shard_map/all_to_all | solution.py:78
  489.6 8.6 %collective-permute-start.17 = (bf16[1280,768]{1,0:T(8,128)(2,1)}, bf16[1280,768]{1,0:T(8,128)(2,1)}, u32[]{:S(2)}, u32[]{:S(2)}) collective-permute-start(bf16[1280,768]{1,0:T(8,128)(2,1)} %get-tuple-element.100), channel_id=1, source_target_pairs={{0,8},{8,0},{16,24},{24,16},{1,9},{9,1},{17,25},{25,17},{2,10},{10... | collective-permute-start | bytes 5898248 | tf_op jit(solution)/shard_map/ppermute | solution.py:53
  489.7 8.6 %collective-permute-start.18 = (bf16[1280,768]{1,0:T(8,128)(2,1)}, bf16[1280,768]{1,0:T(8,128)(2,1)}, u32[]{:S(2)}, u32[]{:S(2)}) collective-permute-start(bf16[1280,768]{1,0:T(8,128)(2,1)} %get-tuple-element.102), channel_id=1, source_target_pairs={{0,8},{8,0},{16,24},{24,16},{1,9},{9,1},{17,25},{25,17},{2,10},{10... | collective-permute-start | bytes 5898248 | tf_op jit(solution)/shard_map/ppermute | solution.py:53
  490.7 5.7 collective-permute-start.16
  525.0 51.8 %all-to-all-start.6 = ((bf16[8,96,1280]{2,1,0:T(8,128)(2,1)}), bf16[8,96,1280]{2,1,0:T(8,128)(2,1)S(1)}, u32[]{:S(2)}, u32[]{:S(2)}) async-start(bf16[8,96,1280]{2,1,0:T(8,128)(2,1)} %bitcast.292), calls=%async_computation.6 | async-start | bytes 3932160 | tf_op jit(solution)/shard_map/all_to_all | solution.py:78
  576.9 13.4 %all-to-all-start.7 = ((bf16[32,4,960]{2,1,0:T(4,128)(2,1)}), bf16[32,4,960]{2,1,0:T(4,128)(2,1)S(1)}, u32[]{:S(2)}, u32[]{:S(2)}) async-start(bf16[32,4,960]{2,1,0:T(4,128)(2,1)} %bitcast.97), calls=%async_computation.7 | async-start | bytes 524288 | tf_op jit(solution)/shard_map/all_to_all | solution.py:791
  580.7 12.0 %collective-permute-start.19 = (bf16[4,1,96,1280]{3,2,0,1:T(8,128)(2,1)}, bf16[4,1,96,1280]{3,2,0,1:T(8,128)(2,1)S(1)}, u32[]{:S(2)}, u32[]{:S(2)}) collective-permute-start(bf16[4,1,96,1280]{3,2,0,1:T(8,128)(2,1)} %select_bitcast_fusion), channel_id=1, source_target_pairs={{0,8},{8,0},{16,24},{24,16},{1,9},{9,1},{17,25},{25,17},{2,10},{10... | collective-permute-start | bytes 2949128 | tf_op jit(solution)/shard_map/ppermute | solution.py:53
  (12 other events, 74.1 us)
Sparse Core Ops, SparseCore 0:
  73.1 260.1 all-gather.4

commit v3 on v2

--- a/solution.py
+++ b/solution.py
@@ -73,15 +73,29 @@
     return lax.all_to_all(both, "tensor", 0, 0).reshape(pl_.rows, both.shape[2])
 
 
-def from_clip(pl_, y):
+def from_clip(pl_, y, terms):
     W = y.shape[-1]
-    both = lax.all_to_all(y.reshape(pl_.T, pl_.S, W), "tensor", 0, 0)
-    both = both.reshape(2, pl_.C, pl_.Q, pl_.S, W)
+    T, R, w = terms.shape
+    sent = jnp.concatenate([y.reshape(T, pl_.S, W), terms.astype(BF).reshape(T, -1, W)], axis=1)
+    got = lax.all_to_all(sent, "tensor", 0, 0)
+    both = got[:, : pl_.S].reshape(2, pl_.C, pl_.Q, pl_.S, W)
     first = pl_.core == 0
     mine, theirs = jnp.where(first, both[0], both[1]), jnp.where(first, both[1], both[0])
-    got = pl_.swap_core(theirs)
-    even, odd = jnp.where(first, mine, got), jnp.where(first, got, mine)
-    return jnp.stack([even, odd], axis=2).reshape(pl_.C, pl_.LF, W)
+    other = pl_.swap_core(theirs)
+    even, odd = jnp.where(first, mine, other), jnp.where(first, other, mine)
+    rows = jnp.stack([even, odd], axis=2).reshape(pl_.C, pl_.LF, W)
+    return rows, got[:, pl_.S :].reshape(T, R, w)
+
+
+def to_owners(pl_, terms):
+    T, R, w = terms.shape
+    D = pl_.D
+    parts = terms.reshape(T, D, R // D, w).swapaxes(0, 1)
+    out = []
+    for step in range(D):
+        part = lax.dynamic_index_in_dim(parts, pl_.d ^ step, 0, False)
+        out.append(lax.ppermute(part, "dp", [(i, i ^ step) for i in range(D)]) if step else part)
+    return jnp.stack(out)
 
 
 def ring(x, axis, stride, size):
@@ -97,8 +111,17 @@
         self.place = place
         self.parts = (first, second)
 
-    def line(self):
-        self.parts = [ring(v, "tensor", 2, self.place.T) for v in self.parts]
+    def line(self, between):
+        size = self.place.T
+        perm = [(i, (i + 2) % size) for i in range(size)]
+        lines = [[v] for v in self.parts]
+        for step in range(size // 2 - 1):
+            for line in lines:
+                line.append(lax.ppermute(line[-1], "tensor", perm))
+            if step == 0:
+                lines, between = lax.optimization_barrier((lines, between))
+        self.parts = [jnp.stack(line) for line in lines]
+        return between
 
     def pair(self, v):
         perm = [(i, i ^ 1) for i in range(self.place.T)]
@@ -394,7 +417,7 @@
 def project(x, gain, a, marks, sels, w):
     rows, width = x.shape
     AR, R = a.shape[2], sels.shape[1]
-    size = block_of(rows)
+    size = rows
     return pl.pallas_call(
         project_kernel,
         grid=(rows // size,),
@@ -739,14 +762,15 @@
     count = qkvo.shape[0]
     half = count // 2
     heads_part = Gather(pl_, qkvo[:half], qkvo[half:])
-    frames_by = by_chip(pl_, frames)
-    heads_part.line()
-    frames_by, ffn, metas = tie([heads_part], frames_by, ffn, metas)
+    frames_by, upstream_by = by_chip(pl_, frames), by_chip(pl_, upstream)
+    ffn = heads_part.line(ffn)
+    frames_by, metas = tie([heads_part], frames_by, metas)
     all_ffn = lax.all_gather(ffn, ("tensor", "dp"))
     frames_in = to_clip(pl_, frames_by)
     heads_part.middle()
     heads_part.last()
-    (frames_in,) = tie([heads_part], frames_in)
+    frames_in, upstream_by = tie([heads_part], frames_in, upstream_by)
+    upstream_in = to_clip(pl_, upstream_by)
     heads_part.core()
     weights, line = heads_weights(pl_, heads_part.parts)
 
@@ -767,8 +791,6 @@
 
     q, k, v, low1 = project(frames_in, gain1, a_all, marks[:3], sels[:3], weights)
     ks, vs = group_values(pl_, k), group_values(pl_, v)
-    q, ks, vs, upstream = tie([], q, ks, vs, upstream)
-    upstream_in = to_clip(pl_, by_chip(pl_, upstream))
     mixed, lse = attend(q, ks, vs, bias)
     bo, a1, b2 = flat_b(out_b), flat_a(fc1_a), flat_b(fc2_b)
     hidden, n2, low2 = leave(mixed, frames_in, bo, a1, gain2, marks, sels, weights)
@@ -777,18 +799,25 @@
     layer_rows, dhidden, dmixed, grads2 = turn(
         acc1, acc2, hidden, n2, upstream_in, live, mixed, bo, a1, b2, gain2, marks, sels, low2, weights
     )
-    layer_output = from_clip(pl_, layer_rows)
     head_order = places(pl_, True).reshape(T, D)[:, d] % T
     clips = metas.reshape(D // 2, 2 * C, 7)[:, :, 1:]
     clips = jnp.repeat(clips, pl_.Q, axis=1)[:, None]
-    clips = jnp.broadcast_to(clips, (D // 2, 2, T, 6)).reshape(D * T, 6)
+    clips = jnp.broadcast_to(clips, (D // 2, 2, T, 6)).reshape(D, T, 6)
+    clips = jnp.take(clips, d ^ jnp.arange(D), axis=0).reshape(D * T, 6)
     hot = (clips[:, :, None] == jnp.arange(A)).astype(BF)
-
-    def owned(terms, picks_of):
-        sizes = [v.shape[2] for v in terms]
-        sent = jnp.concatenate([v.astype(BF) for v in terms], axis=2)
-        sent = sent.reshape(D, R // D, T, -1).transpose(0, 2, 1, 3).reshape(D * T, R // D, -1)
-        got = lax.all_to_all(sent, ("dp", "tensor"), 0, 0)
+    by_tensor = lambda v: v.reshape(R, T, -1)
+
+    def by_head(v):
+        if line:
+            v = v.reshape(R, 2, T, -1).swapaxes(1, 2)
+        return jnp.take(by_tensor(v), head_order, axis=1)
+
+    def joined(terms):
+        return jnp.concatenate([v.astype(BF) for v in terms], axis=2).swapaxes(0, 1)
+
+    def owned(got, sizes, picks_of):
+        got = to_owners(pl_, got)
+        got = got.reshape(D * T, R // D, -1)
         out, at = [], 0
         for size, j in zip(sizes, picks_of):
             out.append(
@@ -797,33 +826,21 @@
             at += size
         return out
 
-    by_tensor = lambda v: v.reshape(R, T, -1)
-
-    def by_head(v):
-        if line:
-            v = v.reshape(R, 2, T, -1).swapaxes(1, 2)
-        return jnp.take(by_tensor(v), head_order, axis=1)
-
-    out_ga, out_gb, fc1_ga, fc2_gb, fc1_gb, fc2_ga = owned(
-        [by_head(grads2[0]), *map(by_tensor, (grads2[1], grads2[2], grads2[3], unit_b, unit_a))],
-        (3, 3, 4, 5, 4, 5),
-    )
-
+    wm = W // T
+    terms = joined([by_head(grads2[0]), *map(by_tensor, (grads2[1], grads2[2], grads2[3], unit_b, unit_a))])
+    layer_output, early = from_clip(pl_, layer_rows, terms)
     dq, *dkv = attend_back(q, ks, vs, bias, lse, mixed, dmixed)
     dks, dvs = dkv[: len(dkv) // 2], dkv[len(dkv) // 2 :]
     dk2, dv2 = group_received(pl_, dks), group_received(pl_, dvs)
-    early = (out_ga, out_gb, fc1_ga, fc2_gb, fc1_gb, fc2_ga)
     dq, layer_output, early = tie([], dq, layer_output, early)
-    out_ga, out_gb, fc1_ga, fc2_gb, fc1_gb, fc2_ga = early
     dframes, grads1 = finish(
         frames_in, dhidden, gain1, a_all, marks[:3], sels[:3], low1, dq, dks[0], dk2, dvs[0], dv2, weights
     )
-    frames_grad = from_clip(pl_, dframes).astype(F32)
-
-    late = owned(
-        [by_tensor(grads1[0, j]) for j in range(3)] + [by_head(grads1[1, j]) for j in range(3)],
-        (0, 1, 2, 0, 1, 2),
-    )
+    out_ga, out_gb, fc1_ga, fc2_gb, fc1_gb, fc2_ga = owned(early, (wm,) * 4 + (U,) * 2, (3, 3, 4, 5, 4, 5))
+    terms = joined([by_tensor(grads1[0, j]) for j in range(3)] + [by_head(grads1[1, j]) for j in range(3)])
+    frames_grad, late = from_clip(pl_, dframes, terms)
+    frames_grad = frames_grad.astype(F32)
+    late = owned(late, (wm,) * 6, (0, 1, 2, 0, 1, 2))
     flip = lambda a: jnp.swapaxes(a, -1, -2)
     return (
         layer_output,

time: 608 us -> 589 us (0.969)
  waiting for transfers between devices: 237 us -> 211 us
  starting transfers between devices: 52.3 us -> 68.2 us
  Pallas kernels: 222 us -> 215 us
    ppermute x0 -> x12, waiting for transfers between devices: none -> 31.1 us  [the longest x6 22 us: line(): line.append(lax.ppermute(line[-1], 'tensor', perm))]
    ppermute x8 -> x2, waiting for transfers between devices: 57 us -> 32.6 us  [ring(): out.append(lax.ppermute(out[-1], axis, perm))]
    all_to_all x4 -> x2, waiting for transfers between devices: 62.2 us -> 41.5 us  [from_clip(): got = lax.all_to_all(sent, 'tensor', 0, 0)]
    all_to_all x2, starting transfers between devices: 11 us -> 30.7 us  [to_clip(): return lax.all_to_all(both, 'tensor', 0, 0).reshape(pl_.rows, both.shape[2])]
    all_to_all x2, waiting for transfers between devices: 39.8 us -> 24.8 us  [to_clip(): return lax.all_to_all(both, 'tensor', 0, 0).reshape(pl_.rows, both.shape[2])]
    ppermute x0 -> x12, starting transfers between devices: none -> 13.4 us  [the longest x6 9.4 us: line(): line.append(lax.ppermute(line[-1], 'tensor', perm))]
    ppermute x10, waiting for transfers between devices: 20.5 us -> 10.2 us  [swap_core(): return lax.ppermute(x, 'dp', self.swap)]
    ppermute x8 -> x2, starting transfers between devices: 10 us -> 0.43 us  [ring(): out.append(lax.ppermute(out[-1], axis, perm))]
  transfers between devices with their start and end apart: 29 -> 33, of which waited for: 21 -> 19; matrix products, arithmetic and copies ran while one was open for 10% -> 8% of each run, Pallas kernels for 20% -> 19%
where the time goes in v3:
time: 589 us; the launch traced here: 581 us
  Pallas kernels  215 us (37%)
  waiting for transfers between devices  211 us (36%)
  starting transfers between devices  68.2 us (12%)
  local copies, waits for them, and re-layouts  33.7 us (6%)
  other arithmetic  30.9 us (5%)
  between operations  15.2 us (3%)
    pallas_call x1, Pallas kernels, feed(): pl.pallas_call(feed_kernel, grid=(blocks // step,), in_specs=[whole((rows...  59.3 us
    ppermute x2, waiting for transfers between devices, pair(): return jnp.stack([v, lax.ppermute(v, 'tensor', perm)])  57.2 us
    pallas_call x1, Pallas kernels, attend_back(): pl.pallas_call(kernel, grid=(heads,), in_specs=[head] * (1 + 2 * n) + [pl...  52.4 us
    all_to_all x2, waiting for transfers between devices, from_clip(): got = lax.all_to_all(sent, 'tensor', 0, 0)  41.5 us
    ppermute x2, waiting for transfers between devices, ring(): out.append(lax.ppermute(out[-1], axis, perm))  32.6 us
    all_to_all x2, starting transfers between devices, to_clip(): return lax.all_to_all(both, 'tensor', 0, 0).reshape(pl_.rows, both.shape[2])  30.7 us
    pallas_call x1, Pallas kernels, attend(): pl.pallas_call(kernel, grid=(heads,), in_specs=[head] * (1 + 2 * n) + [pl...  30.5 us
    pallas_call x1, Pallas kernels, finish(): pl.pallas_call(finish_kernel, grid=(rows // size,), in_specs=[by_rows(siz...  26.8 us
  transfers between devices with their start and end apart: 33, of which 19 were waited for; matrix products, arithmetic and copies ran while one was open for 8% of the time, Pallas kernels for 19%

profile of v3, /device:TPU:0, one launch (start us, length us, event | category | flops | bytes accessed | tf_op | source)
XLA Modules:
  0.0 581.3 jit_solution(1242698569728516435)
XLA Ops:
  9.2 4.2 all-to-all-start
  13.6 2.6 copy.211
  16.2 5.7 all-to-all-done
  21.9 3.5 all-to-all-start.1
  27.5 2.3 collective-permute-start
  31.4 7.8 %all-to-all-done.1 = bf16[2,640,320]{2,0,1:T(2,128)(2,1)S(1)} async-done(((bf16[2,640,320]{2,0,1:T(2,128)(2,1)}), bf16[2,640,320]{2,0,1:T(2,128)(2,1)S(1)}, u32[]{:S(2)}, u32[]{:S(2)}) %all-to-all-start.1) | async-done | bytes 819232 | tf_op jit(solution)/shard_map/all_to_all | solution.py:757
  48.7 5.1 all-gather.2
  55.7 6.6 %collective-permute-done.4 = bf16[80,1408]{1,0:T(8,128)(2,1)} collective-permute-done((bf16[80,1408]{1,0:T(8,128)(2,1)}, bf16[80,1408]{1,0:T(8,128)(2,1)}, u32[]{:S(2)}, u32[]{:S(2)}) %collective-permute-start.4) | collective-permute-done | bytes 225312 | tf_op jit(solution)/shard_map/ppermute | solution.py:120
  65.6 6.2 %collective-permute-done.3 = bf16[80,1408]{1,0:T(8,128)(2,1)S(1)} collective-permute-done((bf16[80,1408]{1,0:T(8,128)(2,1)}, bf16[80,1408]{1,0:T(8,128)(2,1)S(1)}, u32[]{:S(2)}, u32[]{:S(2)}) %collective-permute-start.3) | collective-permute-done | bytes 225312 | tf_op jit(solution)/shard_map/ppermute | solution.py:120
  73.9 7.4 %collective-permute-done.5 = bf16[80,1408]{1,0:T(8,128)(2,1)S(1)} collective-permute-done((bf16[80,1408]{1,0:T(8,128)(2,1)}, bf16[80,1408]{1,0:T(8,128)(2,1)S(1)}, u32[]{:S(2)}, u32[]{:S(2)}) %collective-permute-start.5) | collective-permute-done | bytes 225312 | tf_op jit(solution)/shard_map/ppermute | solution.py:120
  84.1 10.8 %all-to-all-start.2 = ((bf16[8,96,1280]{2,1,0:T(8,128)(2,1)}), bf16[8,96,1280]{2,1,0:T(8,128)(2,1)S(1)}, u32[]{:S(2)}, u32[]{:S(2)}) async-start(bf16[8,96,1280]{2,1,0:T(8,128)(2,1)} %bitcast.312), calls=%async_computation.2 | async-start | bytes 3932160 | tf_op jit(solution)/shard_map/all_to_all | solution.py:73
  97.0 30.1 %collective-permute-done.7 = bf16[4,80,1408]{2,1,0:T(8,128)(2,1)} collective-permute-done((bf16[4,80,1408]{2,1,0:T(8,128)(2,1)}, bf16[4,80,1408]{2,1,0:T(8,128)(2,1)}, u32[]{:S(2)}, u32[]{:S(2)}) %collective-permute-start.7) | collective-permute-done | bytes 901152 | tf_op jit(solution)/shard_map/ppermute | solution.py:128
  129.2 2.5 collective-permute-start.10
  133.3 32.6 %collective-permute-done.8 = bf16[2,4,80,1408]{3,2,1,0:T(8,128)(2,1)S(1)} collective-permute-done((bf16[2,4,80,1408]{3,2,1,0:T(8,128)(2,1)S(1)}, bf16[2,4,80,1408]{3,2,1,0:T(8,128)(2,1)S(1)}, u32[]{:S(2)}, u32[]{:S(2)}) %collective-permute-start.8) | collective-permute-done | bytes 1802272 | tf_op jit(solution)/shard_map/ppermute | solution.py:105
  168.1 27.0 %collective-permute-done.10 = bf16[2,4,80,1408]{3,2,1,0:T(8,128)(2,1)S(1)} collective-permute-done((bf16[2,4,80,1408]{3,2,1,0:T(8,128)(2,1)S(1)}, bf16[2,4,80,1408]{3,2,1,0:T(8,128)(2,1)S(1)}, u32[]{:S(2)}, u32[]{:S(2)}) %collective-permute-start.10) | collective-permute-done | bytes 1802272 | tf_op jit(solution)/shard_map/ppermute | solution.py:128
  203.9 5.2 collective-permute-done.13
  209.1 17.9 %project.1 = (bf16[1280,768]{1,0:T(8,128)(2,1)}, bf16[1280,768]{1,0:T(8,128)(2,1)}, bf16[1280,768]{1,0:T(8,128)(2,1)}, bf16[3,16,768]{2,1,0:T(8,128)(2,1)}) custom-call(bf16[768,1280]{1,0:T(8,128)(2,1)} %bitcast.304, f32[1,1280]{1,0:T(1,128)} %broadcast_in_dim.87.gain_ref, bf16[3,1280,128]{2,1,0:T(8,128)(2,1)} %copy.221.a_ref, ...), custom_call_target="tpu_custom_call" | custom-call | flops 7549747200 | bytes 9830400 | tf_op jit(solution)/shard_map/project/pallas_call | solution.py:421
  227.7 19.9 %all-to-all-start.3 = ((bf16[8,96,1280]{2,1,0:T(8,128)(2,1)}), bf16[8,96,1280]{2,1,0:T(8,128)(2,1)S(1)}, u32[]{:S(2)}, u32[]{:S(2)}) async-start(bf16[8,96,1280]{2,1,0:T(8,128)(2,1)} %bitcast.311), calls=%async_computation.3 | async-start | bytes 3932160 | tf_op jit(solution)/shard_map/all_to_all | solution.py:73
  251.9 30.5 %attend_forward.1 = (bf16[1280,768]{1,0:T(8,128)(2,1)}, f32[16,1,768]{2,1,0:T(1,128)}) custom-call(bf16[1280,768]{1,0:T(8,128)(2,1)} %get-tuple-element.66.refs_0_, bf16[1280,768]{1,0:T(8,128)(2,1)} %get-tuple-element.67.refs_1_, bf16[1280,768]{1,0:T(8,128)(2,1)} %collective-permute-done.14.refs_2_, bf16[1280,768]{1,0:T(8,128)(2,1)} %get-tuple-element.68.refs_3_, ...), custom_call_target="tpu_custom_call" | custom-call | flops 19327352832 | bytes 5898240 | tf_op jit(solution)/shard_map/attend_forward/pallas_call | solution.py:234
  282.3 11.9 %leave_attention.1 = (f32[768,1280]{1,0:T(8,128)}, bf16[768,1408]{1,0:T(8,128)(2,1)}, bf16[2,16,768]{2,1,0:T(8,128)(2,1)}) custom-call(bf16[1280,768]{1,0:T(8,128)(2,1)} %get-tuple-element.70.mixed_ref.refs_7_, bf16[768,1280]{1,0:T(8,128)(2,1)} %bitcast.305, bf16[128,1280]{1,0:T(8,128)(2,1)} %bitcast.326, bf16[1280,128]{1,0:T(8,128)(2,1)} %copy.222.a1_ref, ...), custom_call_target="tpu_custom_call" | custom-call | flops 5033164800 | bytes 3276800 | tf_op jit(solution)/shard_map/leave_attention/pallas_call | solution.py:478
  294.3 24.8 %all-to-all-done.3 = bf16[8,96,1280]{2,1,0:T(8,128)(2,1)S(1)} async-done(((bf16[8,96,1280]{2,1,0:T(8,128)(2,1)}), bf16[8,96,1280]{2,1,0:T(8,128)(2,1)S(1)}, u32[]{:S(2)}, u32[]{:S(2)}) %all-to-all-start.3) | async-done | bytes 1966112 | tf_op jit(solution)/shard_map/all_to_all | solution.py:73
  320.3 59.3 %feed_forward.1 = (f32[768,1408]{1,0:T(8,128)}, f32[768,1408]{1,0:T(8,128)}, f32[16,5120]{1,0:T(8,128)}, f32[16,5120]{1,0:T(8,128)}) custom-call(bf16[768,1408]{1,0:T(8,128)(2,1)} %get-tuple-element.75.x_ref.n2_ref, bf16[768,1280]{1,0:T(8,128)(2,1)} %bitcast.313, f32[768,1]{1,0:T(8,128)} %reshape.789.live_ref, bf16[128,1280]{1,0:T(8,128)(2,1)} %bitcast.340, ...), custom_call_target="tpu_custom_call" | custom-call | flops 44291850240 | bytes 28835840 | tf_op jit(solution)/shard_map/feed_forward/pallas_call | solution.py:548
  379.6 16.4 %turn.1 = (bf16[768,1280]{1,0:T(8,128)(2,1)}, f32[768,1280]{1,0:T(8,128)}, bf16[1280,768]{1,0:T(8,128)(2,1)}, f32[4,16,1280]{2,1,0:T(8,128)}) custom-call(f32[768,1408]{1,0:T(8,128)} %get-tuple-element.79.acc1_ref, f32[768,1408]{1,0:T(8,128)} %get-tuple-element.80.acc2_ref, f32[768,1280]{1,0:T(8,128)} %get-tuple-element.81.hidden_ref, ...), custom_call_target="tpu_custom_call" | custom-call | flops 5033164800 | bytes 15728640 | tf_op jit(solution)/shard_map/turn/pallas_call | solution.py:614
  402.6 3.6 all-to-all-start.4
  406.2 52.4 %attend_backward.1 = (bf16[1280,768]{1,0:T(8,128)(2,1)}, bf16[1280,768]{1,0:T(8,128)(2,1)}, bf16[1280,768]{1,0:T(8,128)(2,1)}, bf16[1280,768]{1,0:T(8,128)(2,1)}, bf16[1280,768]{1,0:T(8,128)(2,1)}) custom-call(bf16[1280,768]{1,0:T(8,128)(2,1)} %get-tuple-element.66.refs_0_, bf16[1280,768]{1,0:T(8,128)(2,1)} %get-tuple-element.67.refs_1_, ...), custom_call_target="tpu_custom_call" | custom-call | flops 38654705664 | bytes 11796480 | tf_op jit(solution)/shard_map/attend_backward/pallas_call | solution.py:303
  459.2 3.1 all-to-all-done.4
  463.7 3.5 collective-permute-done.16
  470.2 26.8 %finish.1 = (bf16[768,1280]{1,0:T(8,128)(2,1)}, f32[2,3,16,1280]{3,2,1,0:T(8,128)}) custom-call(bf16[768,1280]{1,0:T(8,128)(2,1)} %bitcast.306, f32[768,1280]{1,0:T(8,128)} %get-tuple-element.89.dhidden_ref, f32[1,1280]{1,0:T(1,128)} %broadcast_in_dim.87.gain_ref, bf16[3,1280,128]{2,1,0:T(8,128)(2,1)} %copy.221.a_ref, f32[3,1,128]{2,1,0:T(1,128)} %reshape.723.mark_ref, ...), custom_call_target="tpu_custom_call" | custom-call | flops 7549747200 | bytes 9830400 | tf_op jit(solution)/shard_map/finish/pallas_call | solution.py:687
  504.4 6.3 %all-to-all-start.5 = ((bf16[8,108,1280]{2,1,0:T(8,128)(2,1)}), bf16[8,108,1280]{2,1,0:T(8,128)(2,1)S(1)}, u32[]{:S(2)}, u32[]{:S(2)}) async-start(bf16[8,108,1280]{2,1,0:T(8,128)(2,1)} %pad_maximum_fusion.3), calls=%async_computation.5 | async-start | bytes 4587520 | tf_op jit(solution)/shard_map/all_to_all | solution.py:80
  513.8 3.7 collective-permute-done.25
  517.5 2.7 collective-permute-done.24
  525.1 38.4 %all-to-all-done.5 = bf16[8,108,1280]{2,1,0:T(8,128)(2,1)S(1)} async-done(((bf16[8,108,1280]{2,1,0:T(8,128)(2,1)}), bf16[8,108,1280]{2,1,0:T(8,128)(2,1)S(1)}, u32[]{:S(2)}, u32[]{:S(2)}) %all-to-all-start.5) | async-done | bytes 2211872 | tf_op jit(solution)/shard_map/all_to_all | solution.py:80
  (260 shorter events, 85.1 us)
Async XLA Ops:
  9.2 12.7 %all-to-all-start = ((bf16[4,160,320]{2,1,0:T(8,128)(2,1)}), bf16[4,160,320]{2,1,0:T(8,128)(2,1)S(1)}, u32[]{:S(2)}, u32[]{:S(2)}) async-start(bf16[4,160,320]{2,1,0:T(8,128)(2,1)} %pad_maximum_fusion.13), calls=%async_computation | async-start | bytes 983040 | tf_op jit(solution)/shard_map/all_to_all | solution.py:751
  21.9 17.2 %all-to-all-start.1 = ((bf16[2,640,320]{2,0,1:T(2,128)(2,1)}), bf16[2,640,320]{2,0,1:T(2,128)(2,1)S(1)}, u32[]{:S(2)}, u32[]{:S(2)}) async-start(bf16[2,640,320]{2,0,1:T(2,128)(2,1)} %copy.211), calls=%async_computation.1 | async-start | bytes 1966080 | tf_op jit(solution)/shard_map/all_to_all | solution.py:757
  25.4 293.6 %all-gather.5.cloned.1.call-start = ((), (), s32[]{:S(2)}) async-start(), calls=%async_computation.6 | async-start | bytes 29736960 | tf_op jit(solution)/shard_map/all_gather | solution.py:768
  27.5 16.1 %collective-permute-start = (bf16[80,1408]{1,0:T(8,128)(2,1)S(1)}, bf16[80,1408]{1,0:T(8,128)(2,1)}, u32[]{:S(2)}, u32[]{:S(2)}) collective-permute-start(bf16[80,1408]{1,0:T(8,128)(2,1)S(1)} %get-tuple-element.55), channel_id=1, source_target_pairs={{0,2},{1,3},{2,4},{3,5},{4,6},{5,7},{6,0},{7,1},{8,10},{9,11},{10,... | collective-permute-start | bytes 675848 | tf_op jit(solution)/shard_map/ppermute | solution.py:120
  29.8 13.8 %collective-permute-start.1 = (bf16[80,1408]{1,0:T(8,128)(2,1)S(1)}, bf16[80,1408]{1,0:T(8,128)(2,1)}, u32[]{:S(2)}, u32[]{:S(2)}) collective-permute-start(bf16[80,1408]{1,0:T(8,128)(2,1)S(1)} %get-tuple-element.57), channel_id=1, source_target_pairs={{0,2},{1,3},{2,4},{3,5},{4,6},{5,7},{6,0},{7,1},{8,10},{9,11},{10,... | collective-permute-start | bytes 675848 | tf_op jit(solution)/shard_map/ppermute | solution.py:120
  44.7 19.2 %collective-permute-start.6 = (bf16[4,1,96,1280]{3,2,0,1:T(8,128)(2,1)}, bf16[4,1,96,1280]{3,2,0,1:T(8,128)(2,1)S(1)}, u32[]{:S(2)}, u32[]{:S(2)}) collective-permute-start(bf16[4,1,96,1280]{3,2,0,1:T(8,128)(2,1)} %select_bitcast_fusion.3), channel_id=1, source_target_pairs={{0,8},{8,0},{16,24},{24,16},{1,9},{9,1},{17,25},{25,17},{2,10},{10... | collective-permute-start | bytes 2949128 | tf_op jit(solution)/shard_map/ppermute | solution.py:53
  44.7 10.9 %collective-permute-start.2 = (bf16[80,1408]{1,0:T(8,128)(2,1)}, bf16[80,1408]{1,0:T(8,128)(2,1)}, u32[]{:S(2)}, u32[]{:S(2)}) collective-permute-start(bf16[80,1408]{1,0:T(8,128)(2,1)} %collective-permute-done), channel_id=1, source_target_pairs={{0,2},{1,3},{2,4},{3,5},{4,6},{5,7},{6,0},{7,1},{8,10},{9,11},{10,... | collective-permute-start | bytes 675848 | tf_op jit(solution)/shard_map/ppermute | solution.py:120
  47.0 15.3 %collective-permute-start.4 = (bf16[80,1408]{1,0:T(8,128)(2,1)}, bf16[80,1408]{1,0:T(8,128)(2,1)}, u32[]{:S(2)}, u32[]{:S(2)}) collective-permute-start(bf16[80,1408]{1,0:T(8,128)(2,1)} %collective-permute-done.1), channel_id=1, source_target_pairs={{0,2},{1,3},{2,4},{3,5},{4,6},{5,7},{6,0},{7,1},{8,10},{9,11},{10,... | collective-permute-start | bytes 675848 | tf_op jit(solution)/shard_map/ppermute | solution.py:120
  55.7 16.1 %collective-permute-start.3 = (bf16[80,1408]{1,0:T(8,128)(2,1)}, bf16[80,1408]{1,0:T(8,128)(2,1)S(1)}, u32[]{:S(2)}, u32[]{:S(2)}) collective-permute-start(bf16[80,1408]{1,0:T(8,128)(2,1)} %collective-permute-done.2), channel_id=1, source_target_pairs={{0,2},{1,3},{2,4},{3,5},{4,6},{5,7},{6,0},{7,1},{8,10},{9,11},{10,... | collective-permute-start | bytes 675848 | tf_op jit(solution)/shard_map/ppermute | solution.py:120
  62.2 19.0 %collective-permute-start.5 = (bf16[80,1408]{1,0:T(8,128)(2,1)}, bf16[80,1408]{1,0:T(8,128)(2,1)S(1)}, u32[]{:S(2)}, u32[]{:S(2)}) collective-permute-start(bf16[80,1408]{1,0:T(8,128)(2,1)} %collective-permute-done.4), channel_id=1, source_target_pairs={{0,2},{1,3},{2,4},{3,5},{4,6},{5,7},{6,0},{7,1},{8,10},{9,11},{10,... | collective-permute-start | bytes 675848 | tf_op jit(solution)/shard_map/ppermute | solution.py:120
  82.4 44.7 %collective-permute-start.7 = (bf16[4,80,1408]{2,1,0:T(8,128)(2,1)}, bf16[4,80,1408]{2,1,0:T(8,128)(2,1)}, u32[]{:S(2)}, u32[]{:S(2)}) collective-permute-start(bf16[4,80,1408]{2,1,0:T(8,128)(2,1)} %pad_maximum_fusion.10), channel_id=1, source_target_pairs={{0,1},{1,0},{2,3},{3,2},{4,5},{5,4},{6,7},{7,6},{8,9},{9,8},{10,11... | collective-permute-start | bytes 2703368 | tf_op jit(solution)/shard_map/ppermute | solution.py:128
  84.1 113.2 %all-to-all-start.2 = ((bf16[8,96,1280]{2,1,0:T(8,128)(2,1)}), bf16[8,96,1280]{2,1,0:T(8,128)(2,1)S(1)}, u32[]{:S(2)}, u32[]{:S(2)}) async-start(bf16[8,96,1280]{2,1,0:T(8,128)(2,1)} %bitcast.312), calls=%async_computation.2 | async-start | bytes 3932160 | tf_op jit(solution)/shard_map/all_to_all | solution.py:73
  94.9 34.0 %collective-permute-start.9 = (bf16[4,80,1408]{2,1,0:T(8,128)(2,1)S(1)}, bf16[4,80,1408]{2,1,0:T(8,128)(2,1)S(1)}, u32[]{:S(2)}, u32[]{:S(2)}) collective-permute-start(bf16[4,80,1408]{2,1,0:T(8,128)(2,1)S(1)} %pad_maximum_fusion.11), channel_id=1, source_target_pairs={{0,16},{8,24},{16,0},{24,8},{1,17},{9,25},{17,1},{25,9},{2,18},{10... | collective-permute-start | bytes 2703368 | tf_op jit(solution)/shard_map/ppermute | solution.py:105
  96.9 34.8 %collective-permute-start.11 = (bf16[4,1,96,1280]{3,2,0,1:T(8,128)(2,1)S(1)}, bf16[4,1,96,1280]{3,2,0,1:T(8,128)(2,1)S(1)}, u32[]{:S(2)}, u32[]{:S(2)}) collective-permute-start(bf16[4,1,96,1280]{3,2,0,1:T(8,128)(2,1)S(1)} %select_bitcast_fusion.2), channel_id=1, source_target_pairs={{0,8},{8,0},{16,24},{24,16},{1,9},{9,1},{17,25},{25,17},{2,10},{10... | collective-permute-start | bytes 2949128 | tf_op jit(solution)/shard_map/ppermute | solution.py:53
  128.8 37.1 %collective-permute-start.8 = (bf16[2,4,80,1408]{3,2,1,0:T(8,128)(2,1)S(1)}, bf16[2,4,80,1408]{3,2,1,0:T(8,128)(2,1)S(1)}, u32[]{:S(2)}, u32[]{:S(2)}) collective-permute-start(bf16[2,4,80,1408]{3,2,1,0:T(8,128)(2,1)S(1)} %get-tuple-element.162), channel_id=1, source_target_pairs={{0,16},{8,24},{16,0},{24,8},{1,17},{9,25},{17,1},{25,9},{2,18},{10... | collective-permute-start | bytes 5406728 | tf_op jit(solution)/shard_map/ppermute | solution.py:105
  129.2 66.0 %collective-permute-start.10 = (bf16[2,4,80,1408]{3,2,1,0:T(8,128)(2,1)S(1)}, bf16[2,4,80,1408]{3,2,1,0:T(8,128)(2,1)S(1)}, u32[]{:S(2)}, u32[]{:S(2)}) collective-permute-start(bf16[2,4,80,1408]{3,2,1,0:T(8,128)(2,1)S(1)} %get-tuple-element.160), channel_id=1, source_target_pairs={{0,1},{1,0},{2,3},{3,2},{4,5},{5,4},{6,7},{7,6},{8,9},{9,8},{10,11... | collective-permute-start | bytes 5406728 | tf_op jit(solution)/shard_map/ppermute | solution.py:128
  197.3 6.7 %collective-permute-start.12 = (bf16[2,2,4,80,1408]{4,3,2,1,0:T(8,128)(2,1)}, bf16[2,2,4,80,1408]{4,3,2,1,0:T(8,128)(2,1)}, u32[]{:S(2)}, u32[]{:S(2)}) collective-permute-start(bf16[2,2,4,80,1408]{4,3,2,1,0:T(8,128)(2,1)} %pad_maximum_fusion), channel_id=1, source_target_pairs={{0,8},{8,0},{16,24},{24,16},{1,9},{9,1},{17,25},{25,17},{2,10},{10... | collective-permute-start | bytes 10813448 | tf_op jit(solution)/shard_map/ppermute | solution.py:53
  197.3 11.8 %collective-permute-start.13 = (bf16[2,2,4,80,1408]{4,3,2,1,0:T(8,128)(2,1)}, bf16[2,2,4,80,1408]{4,3,2,1,0:T(8,128)(2,1)}, u32[]{:S(2)}, u32[]{:S(2)}) collective-permute-start(bf16[2,2,4,80,1408]{4,3,2,1,0:T(8,128)(2,1)} %pad_maximum_fusion.1), channel_id=1, source_target_pairs={{0,8},{8,0},{16,24},{24,16},{1,9},{9,1},{17,25},{25,17},{2,10},{10... | collective-permute-start | bytes 10813448 | tf_op jit(solution)/shard_map/ppermute | solution.py:53
  227.0 24.9 %collective-permute-start.14 = (bf16[1280,768]{1,0:T(8,128)(2,1)}, bf16[1280,768]{1,0:T(8,128)(2,1)}, u32[]{:S(2)}, u32[]{:S(2)}) collective-permute-start(bf16[1280,768]{1,0:T(8,128)(2,1)} %get-tuple-element.67.refs_1_), channel_id=1, source_target_pairs={{0,8},{8,0},{16,24},{24,16},{1,9},{9,1},{17,25},{25,17},{2,10},{10... | collective-permute-start | bytes 5898248 | tf_op jit(solution)/shard_map/ppermute | solution.py:53
  227.2 24.6 %collective-permute-start.15 = (bf16[1280,768]{1,0:T(8,128)(2,1)}, bf16[1280,768]{1,0:T(8,128)(2,1)}, u32[]{:S(2)}, u32[]{:S(2)}) collective-permute-start(bf16[1280,768]{1,0:T(8,128)(2,1)} %get-tuple-element.68.refs_3_), channel_id=1, source_target_pairs={{0,8},{8,0},{16,24},{24,16},{1,9},{9,1},{17,25},{25,17},{2,10},{10... | collective-permute-start | bytes 5898248 | tf_op jit(solution)/shard_map/ppermute | solution.py:53
  227.7 91.4 %all-to-all-start.3 = ((bf16[8,96,1280]{2,1,0:T(8,128)(2,1)}), bf16[8,96,1280]{2,1,0:T(8,128)(2,1)S(1)}, u32[]{:S(2)}, u32[]{:S(2)}) async-start(bf16[8,96,1280]{2,1,0:T(8,128)(2,1)} %bitcast.311), calls=%async_computation.3 | async-start | bytes 3932160 | tf_op jit(solution)/shard_map/all_to_all | solution.py:73
  402.6 59.7 %all-to-all-start.4 = ((bf16[8,120,1280]{2,1,0:T(8,128)(2,1)}), bf16[8,120,1280]{2,1,0:T(8,128)(2,1)S(1)}, u32[]{:S(2)}, u32[]{:S(2)}) async-start(bf16[8,120,1280]{2,1,0:T(8,128)(2,1)} %pad_maximum_fusion.2), calls=%async_computation.4 | async-start | bytes 4915200 | tf_op jit(solution)/shard_map/all_to_all | solution.py:80
  458.6 11.6 %collective-permute-start.17 = (bf16[1280,768]{1,0:T(8,128)(2,1)}, bf16[1280,768]{1,0:T(8,128)(2,1)}, u32[]{:S(2)}, u32[]{:S(2)}) collective-permute-start(bf16[1280,768]{1,0:T(8,128)(2,1)} %get-tuple-element.93), channel_id=1, source_target_pairs={{0,8},{8,0},{16,24},{24,16},{1,9},{9,1},{17,25},{25,17},{2,10},{10... | collective-permute-start | bytes 5898248 | tf_op jit(solution)/shard_map/ppermute | solution.py:53
  458.7 11.5 %collective-permute-start.18 = (bf16[1280,768]{1,0:T(8,128)(2,1)}, bf16[1280,768]{1,0:T(8,128)(2,1)}, u32[]{:S(2)}, u32[]{:S(2)}) collective-permute-start(bf16[1280,768]{1,0:T(8,128)(2,1)} %get-tuple-element.95), channel_id=1, source_target_pairs={{0,8},{8,0},{16,24},{24,16},{1,9},{9,1},{17,25},{25,17},{2,10},{10... | collective-permute-start | bytes 5898248 | tf_op jit(solution)/shard_map/ppermute | solution.py:53
  463.4 3.9 collective-permute-start.16
  504.4 59.0 %all-to-all-start.5 = ((bf16[8,108,1280]{2,1,0:T(8,128)(2,1)}), bf16[8,108,1280]{2,1,0:T(8,128)(2,1)S(1)}, u32[]{:S(2)}, u32[]{:S(2)}) async-start(bf16[8,108,1280]{2,1,0:T(8,128)(2,1)} %pad_maximum_fusion.3), calls=%async_computation.5 | async-start | bytes 4587520 | tf_op jit(solution)/shard_map/all_to_all | solution.py:80
  511.8 5.6 collective-permute-start.25
  511.9 8.2 %collective-permute-start.24 = (bf16[8,4,1920]{2,0,1:T(8,128)(2,1)S(1)}, bf16[8,4,1920]{2,0,1:T(8,128)(2,1)S(1)}, u32[]{:S(2)}, u32[]{:S(2)}) collective-permute-start(bf16[8,4,1920]{2,0,1:T(8,128)(2,1)S(1)} %get-tuple-element.165), channel_id=1, source_target_pairs={{0,16},{8,24},{16,0},{24,8},{1,17},{9,25},{17,1},{25,9},{2,18},{10... | collective-permute-start | bytes 368648 | tf_op jit(solution)/shard_map/ppermute | solution.py:97
  513.4 6.8 %collective-permute-start.23 = (bf16[8,4,1920]{2,0,1:T(8,128)(2,1)S(1)}, bf16[8,4,1920]{2,0,1:T(8,128)(2,1)S(1)}, u32[]{:S(2)}, u32[]{:S(2)}) collective-permute-start(bf16[8,4,1920]{2,0,1:T(8,128)(2,1)S(1)} %get-tuple-element.166), channel_id=1, source_target_pairs={{0,8},{8,0},{16,24},{24,16},{1,9},{9,1},{17,25},{25,17},{2,10},{10... | collective-permute-start | bytes 368648 | tf_op jit(solution)/shard_map/ppermute | solution.py:97
  564.1 5.0 collective-permute-start.21
  564.8 4.3 collective-permute-start.20
  566.2 5.4 collective-permute-start.19
  (24 other events, 332.5 us)
Sparse Core Ops, SparseCore 0:
  43.8 270.6 all-gather.4

commit v4 on v3

--- a/solution.py
+++ b/solution.py
@@ -75,16 +75,20 @@
 
 def from_clip(pl_, y, terms):
     W = y.shape[-1]
-    T, R, w = terms.shape
+    T = pl_.T
     sent = jnp.concatenate([y.reshape(T, pl_.S, W), terms.astype(BF).reshape(T, -1, W)], axis=1)
-    got = lax.all_to_all(sent, "tensor", 0, 0)
+    return lax.all_to_all(sent, "tensor", 0, 0)
+
+
+def from_sources(pl_, got, R):
+    T, _, W = got.shape
     both = got[:, : pl_.S].reshape(2, pl_.C, pl_.Q, pl_.S, W)
     first = pl_.core == 0
     mine, theirs = jnp.where(first, both[0], both[1]), jnp.where(first, both[1], both[0])
     other = pl_.swap_core(theirs)
     even, odd = jnp.where(first, mine, other), jnp.where(first, other, mine)
     rows = jnp.stack([even, odd], axis=2).reshape(pl_.C, pl_.LF, W)
-    return rows, got[:, pl_.S :].reshape(T, R, w)
+    return rows, got[:, pl_.S :].reshape(T, R, -1)
 
 
 def to_owners(pl_, terms):
@@ -204,7 +208,7 @@
 EXTRA = 16
 
 
-def attend_kernel(q_ref, k_refs, v_refs, bias_ref, out_ref, lse_ref):
+def attend_kernel(q_ref, k_refs, v_refs, bias_ref, out_ref, expo_ref, inverse_ref):
     rows = q_ref.shape[1]
     keys = bias_ref.shape[1]
     k = jnp.concatenate(
@@ -217,10 +221,11 @@
     scores = mm(k, q)
     top = jnp.max(scores, axis=0, keepdims=True)
     expo = jnp.exp2((scores - top) * TO_LOG2).astype(BF)
+    expo_ref[0] = expo
     both = mm(v, expo)
     total = both[HEAD : HEAD + 1]
     out_ref[...] = (both[:HEAD] / total).astype(BF)
-    lse_ref[0] = top + jnp.log2(total) * (1.0 / TO_LOG2)
+    inverse_ref[0] = 1.0 / total
 
 
 def attend(q, ks, vs, bias):
@@ -235,9 +240,14 @@
         kernel,
         grid=(heads,),
         in_specs=[head] * (1 + 2 * n) + [pl.BlockSpec(bias.shape, lambda h: (0, 0))],
-        out_specs=[head, pl.BlockSpec((1, 1, rows), lambda h: (h, 0, 0))],
+        out_specs=[
+            head,
+            pl.BlockSpec((1, bias.shape[1], rows), lambda h: (h, 0, 0)),
+            pl.BlockSpec((1, 1, rows), lambda h: (h, 0, 0)),
+        ],
         out_shape=[
             jax.ShapeDtypeStruct((width, rows), BF),
+            jax.ShapeDtypeStruct((heads, bias.shape[1], rows), BF),
             jax.ShapeDtypeStruct((heads, 1, rows), F32),
         ],
         compiler_params=pltpu.CompilerParams(vmem_limit_bytes=56 * 2**20),
@@ -249,49 +259,42 @@
 
 
 def attend_back_kernel(
-    q_ref, k_refs, v_refs, bias_ref, lse_ref, mixed_ref, dmixed_ref, dq_ref, dk_refs, dv_refs, *, span
+    q_ref, k_refs, v_refs, expo_ref, inverse_ref, mixed_ref, dmixed_ref, dq_ref, dk_refs, dv_refs, *, span
 ):
     rows = q_ref.shape[1]
-    keys = bias_ref.shape[1]
-    k_flat = jnp.concatenate([r[...] for r in k_refs], axis=1)
-    k = jnp.concatenate(
-        [k_flat, bias_ref[...].astype(BF), jnp.ones((3, keys), BF), jnp.zeros((EXTRA - 4, keys), BF)]
-    ).T
+    keys = expo_ref.shape[1]
+    k = jnp.concatenate([r[...] for r in k_refs], axis=1)
     v = jnp.concatenate(
         [jnp.concatenate([r[...] for r in v_refs], axis=1), jnp.ones((EXTRA, keys), BF)]
     ).T
-    dmixed = dmixed_ref[...]
-    delta = -jnp.sum(dmixed.astype(F32) * mixed_ref[...].astype(F32), axis=0, keepdims=True)
+    inverse = inverse_ref[0]
+    dmixed = dmixed_ref[...].astype(F32)
+    delta = -jnp.sum(dmixed * mixed_ref[...].astype(F32), axis=0, keepdims=True) * inverse
     d0 = delta.astype(BF)
     d1 = (delta - d0.astype(F32)).astype(BF)
+    dmixed = (dmixed * inverse).astype(BF)
     dmixed_more = jnp.concatenate([dmixed, d0, d1, jnp.zeros((EXTRA - 2, rows), BF)])
-    lse = -lse_ref[0]
-    l0 = lse.astype(BF)
-    rest = lse - l0.astype(F32)
-    l1 = rest.astype(BF)
-    l2 = (rest - l1.astype(F32)).astype(BF)
-    q_flat = q_ref[...]
-    q = jnp.concatenate([q_flat, jnp.ones((1, rows), BF), l0, l1, l2, jnp.zeros((EXTRA - 4, rows), BF)])
+    q = q_ref[...]
     dk = jnp.zeros((HEAD, keys), F32)
     dv = jnp.zeros((HEAD, keys), F32)
     for start in range(0, rows, span):
         part = slice(start, start + span)
-        probs = jnp.exp2(mm(k, q[:, part]) * TO_LOG2)
-        dscores = (probs * mm(v, dmixed_more[:, part])).astype(BF)
-        dq_ref[:, part] = (mm(k_flat, dscores) * RATE).astype(BF)
-        dk = dk + mm_nt(q_flat[:, part], dscores)
-        dv = dv + mm_nt(dmixed[:, part], probs.astype(BF))
+        expo = expo_ref[0, :, part]
+        dscores = (expo.astype(F32) * mm(v, dmixed_more[:, part])).astype(BF)
+        dq_ref[:, part] = (mm(k, dscores) * RATE).astype(BF)
+        dk = dk + mm_nt(q[:, part], dscores)
+        dv = dv + mm_nt(dmixed[:, part], expo)
     for i, (dk_ref, dv_ref) in enumerate(zip(dk_refs, dv_refs)):
         part = slice(i * rows, (i + 1) * rows)
         dk_ref[...] = (dk[:, part] * RATE).astype(BF)
         dv_ref[...] = dv[:, part].astype(BF)
 
 
-def attend_back(q, ks, vs, bias, lse, mixed, dmixed):
+def attend_back(q, ks, vs, expo, inverse, mixed, dmixed):
     width, rows = q.shape
-    keys = bias.shape[1]
+    keys = expo.shape[1]
     heads, n = width // HEAD, len(ks)
-    span = rows // 2 if rows % 256 == 0 else rows
+    span = rows
     head = pl.BlockSpec((HEAD, rows), lambda h: (h, 0))
 
     def kernel(*refs):
@@ -305,7 +308,7 @@
         grid=(heads,),
         in_specs=[head] * (1 + 2 * n)
         + [
-            pl.BlockSpec(bias.shape, lambda h: (0, 0)),
+            pl.BlockSpec((1, keys, rows), lambda h: (h, 0, 0)),
             pl.BlockSpec((1, 1, rows), lambda h: (h, 0, 0)),
             head,
             head,
@@ -317,7 +320,7 @@
             flops=8 * heads * rows * keys * 256, bytes_accessed=12 * width * rows, transcendentals=0
         ),
         name="attend_backward",
-    )(q, *ks, *vs, bias, lse, mixed, dmixed)
+    )(q, *ks, *vs, expo, inverse, mixed, dmixed)
 
 
 def heads_weights(pl_, parts):
@@ -508,7 +511,7 @@
 
 
 def feed_kernel(
-    x_ref, up_ref, live_ref, b2_ref, mark_ref, sel_ref, low_ref, w_ref, acc1_ref, acc2_ref, ga_ref, gb_ref, s_ref, ld_ref
+    x_ref, up_ref, live_ref, b2_ref, mark_ref, sel_ref, low_ref, w_ref, l_ref, acc1_ref, acc2_ref, ga_ref, gb_ref, s_ref, ld_ref
 ):
     width = up_ref.shape[1]
 
@@ -525,21 +528,24 @@
     wide = w_ref.shape[3]
     first = w_ref[:, 0].reshape(-1, wide)
     second = w_ref[:, 1].reshape(-1, wide)
-    upper = mm_nt(x_ref[...], first)
+    upper = mm_nt(x_ref[:, :width], first) + mm(x_ref[:, width:], l_ref[0])
     cdf = 0.5 * (1.0 + lax.erf(upper * (0.5**0.5)))
     active = (upper * cdf).astype(BF)
-    dactive = mm_nt(s_ref[...], second)
+    dactive = mm_nt(s_ref[:, :width], second) + mm(s_ref[:, width:], l_ref[1])
     slope = cdf + upper * jnp.exp(-0.5 * upper * upper) * (1.0 / (2.0 * jnp.pi) ** 0.5)
     dupper = (dactive * slope).astype(BF)
-    acc1_ref[...] += mm(active, second)
-    acc2_ref[...] += mm(dupper, first)
+    acc1_ref[:, :width] += mm(active, second)
+    acc1_ref[:, width:] += mm_nt(active, l_ref[1])
+    acc2_ref[:, :width] += mm(dupper, first)
+    acc2_ref[:, width:] += mm_nt(dupper, l_ref[0])
     ga_ref[...] = mm(ld_ref[...], active)
     gb_ref[...] = mm(low_ref[1], dupper)
 
 
-def feed(x, upstream, live, b2, marks, sels, low, w):
+def feed(x, upstream, live, b2, marks, sels, low, w, inner):
     rows, width = upstream.shape
-    blocks, _, h, wide = w.shape
+    blocks, _, h, _ = w.shape
+    wide = x.shape[1]
     AR, R = wide - width, low.shape[1]
     step = blocks
     while step * h > 1280:
@@ -556,7 +562,8 @@
             whole((6, 1, AR)),
             whole((6, R, AR)),
             whole((2, R, rows)),
-            pl.BlockSpec((step, 2, h, wide), lambda i: (i, 0, 0, 0)),
+            pl.BlockSpec((step, 2, h, width), lambda i: (i, 0, 0, 0)),
+            pl.BlockSpec((2, AR, step * h), lambda i: (0, 0, i)),
         ],
         out_specs=[whole((rows, wide)), whole((rows, wide)), part, part],
         out_shape=[jax.ShapeDtypeStruct((rows, wide), F32)] * 2
@@ -567,7 +574,7 @@
             flops=8 * rows * wide * blocks * h, bytes_accessed=4 * blocks * h * wide, transcendentals=0
         ),
         name="feed_forward",
-    )(x, upstream, live, b2, marks, sels, low, w)
+    )(x, upstream, live, b2, marks, sels, low, w, inner)
 
 
 def turn_kernel(
@@ -663,6 +670,7 @@
     z, rate = norm_parts(x_ref[...].astype(F32))
     n1 = (z * gain_ref[...]).astype(BF)
     dn1 = jnp.zeros(x_ref.shape, F32)
+    lows, picked = [], []
     for j, own in enumerate((dq_ref, dk_ref, dv_ref)):
         dy = own[...]
         if j:
@@ -674,9 +682,15 @@
 
         both = mm(dy.T, bufs[j])
         low = (both[:, width:] * mark_ref[j]).astype(BF)
-        grad_ref[0, j] += mm(mm_nt(sel_ref[j], low).astype(BF), n1)
+        lows.append(low)
+        picked.append(mm_nt(sel_ref[j], low).astype(BF))
         grad_ref[1, j] += mm_nt(low_ref[j], dy)
-        dn1 = dn1 + both[:, :width] + mm_nt(low, a_ref[j])
+        dn1 = dn1 + both[:, :width]
+    dn1 = dn1 + mm_nt(jnp.concatenate(lows, axis=1), jnp.concatenate([a_ref[j] for j in range(3)], axis=1))
+    grads = mm(jnp.concatenate(picked), n1)
+    R = sel_ref.shape[1]
+    for j in range(3):
+        grad_ref[0, j] += grads[j * R : (j + 1) * R]
     out_ref[...] = (dhidden_ref[...] + norm_back(z, rate, dn1 * gain_ref[...])).astype(BF)
 
 
@@ -755,10 +769,6 @@
     qkvo = jnp.concatenate([qkvo, lax.dynamic_index_in_dim(qkvo_low, d, 0, False)], axis=1)
     ffn = jnp.stack([w_up.T, w_down])
     ffn = lax.all_to_all(ffn, "dp", 1, 2, tiled=True)
-    ffn_low = jnp.stack(
-        [fc1_b.transpose(2, 0, 1).reshape(U, AR), fc2_a.transpose(1, 0, 2).reshape(U, AR)]
-    ).reshape(2, D, U // D, AR)
-    ffn = jnp.concatenate([ffn, lax.dynamic_index_in_dim(ffn_low, d, 1, False)], axis=2)
     count = qkvo.shape[0]
     half = count // 2
     heads_part = Gather(pl_, qkvo[:half], qkvo[half:])
@@ -769,8 +779,18 @@
     frames_in = to_clip(pl_, frames_by)
     heads_part.middle()
     heads_part.last()
+    of_plane = jnp.repeat(lax.dynamic_slice_in_dim(metas, d - pl_.core, 2).reshape(2 * C, 7), pl_.Q, axis=0)
+    hot_up, hot_down = [(of_plane[:, j, None] == jnp.arange(A)).astype(BF) for j in (5, 6)]
+    inner_by = jnp.stack(
+        [
+            jnp.einsum("ta,aru->tru", hot_up, fc1_b, preferred_element_type=F32).astype(BF),
+            jnp.einsum("ta,aru->tru", hot_down, fc2_a.swapaxes(1, 2), preferred_element_type=F32).astype(BF),
+        ],
+        axis=1,
+    ).reshape(T, -1, W)
+    upstream_by = jnp.concatenate([upstream_by, inner_by], axis=1)
     frames_in, upstream_by = tie([heads_part], frames_in, upstream_by)
-    upstream_in = to_clip(pl_, upstream_by)
+    upstream_in = lax.all_to_all(upstream_by, "tensor", 0, 0)
     heads_part.core()
     weights, line = heads_weights(pl_, heads_part.parts)
 
@@ -791,11 +811,15 @@
 
     q, k, v, low1 = project(frames_in, gain1, a_all, marks[:3], sels[:3], weights)
     ks, vs = group_values(pl_, k), group_values(pl_, v)
-    mixed, lse = attend(q, ks, vs, bias)
+    mixed, expo, inverse = attend(q, ks, vs, bias)
     bo, a1, b2 = flat_b(out_b), flat_a(fc1_a), flat_b(fc2_b)
     hidden, n2, low2 = leave(mixed, frames_in, bo, a1, gain2, marks, sels, weights)
     hidden, n2, low2, upstream_in = tie([], hidden, n2, low2, upstream_in)
-    acc1, acc2, unit_a, unit_b = feed(n2, upstream_in, live, b2, marks, sels, low2, all_ffn)
+    inner_in = upstream_in[:, pl_.S :].reshape(T, 2, R, U).transpose(1, 2, 0, 3).reshape(2, 1, R, T * U)
+    upstream_in = upstream_in[:, : pl_.S].reshape(pl_.rows, W)
+    inner_in = inner_in * marks[4:].astype(BF).reshape(2, A, R, 1)
+    inner_in = inner_in.reshape(2, AR, T * U)
+    acc1, acc2, unit_a, unit_b = feed(n2, upstream_in, live, b2, marks, sels, low2, all_ffn, inner_in)
     layer_rows, dhidden, dmixed, grads2 = turn(
         acc1, acc2, hidden, n2, upstream_in, live, mixed, bo, a1, b2, gain2, marks, sels, low2, weights
     )
@@ -828,17 +852,19 @@
 
     wm = W // T
     terms = joined([by_head(grads2[0]), *map(by_tensor, (grads2[1], grads2[2], grads2[3], unit_b, unit_a))])
-    layer_output, early = from_clip(pl_, layer_rows, terms)
-    dq, *dkv = attend_back(q, ks, vs, bias, lse, mixed, dmixed)
+    layer_got = from_clip(pl_, layer_rows, terms)
+    dq, *dkv = attend_back(q, ks, vs, expo, inverse, mixed, dmixed)
     dks, dvs = dkv[: len(dkv) // 2], dkv[len(dkv) // 2 :]
     dk2, dv2 = group_received(pl_, dks), group_received(pl_, dvs)
-    dq, layer_output, early = tie([], dq, layer_output, early)
+    dq, layer_got = tie([], dq, layer_got)
     dframes, grads1 = finish(
         frames_in, dhidden, gain1, a_all, marks[:3], sels[:3], low1, dq, dks[0], dk2, dvs[0], dv2, weights
     )
+    dframes, layer_got = tie([], dframes, layer_got)
+    layer_output, early = from_sources(pl_, layer_got, R)
     out_ga, out_gb, fc1_ga, fc2_gb, fc1_gb, fc2_ga = owned(early, (wm,) * 4 + (U,) * 2, (3, 3, 4, 5, 4, 5))
     terms = joined([by_tensor(grads1[0, j]) for j in range(3)] + [by_head(grads1[1, j]) for j in range(3)])
-    frames_grad, late = from_clip(pl_, dframes, terms)
+    frames_grad, late = from_sources(pl_, from_clip(pl_, dframes, terms), R)
     frames_grad = frames_grad.astype(F32)
     late = owned(late, (wm,) * 6, (0, 1, 2, 0, 1, 2))
     flip = lambda a: jnp.swapaxes(a, -1, -2)

time: 589 us -> 578 us (0.981)
  other arithmetic: 30.9 us -> 45.7 us
  starting transfers between devices: 68.2 us -> 53.6 us
  waiting for transfers between devices: 211 us -> 201 us
    all_to_all x2 -> x1, waiting for transfers between devices: 24.8 us -> 0.01 us  [to_clip(): return lax.all_to_all(both, 'tensor', 0, 0).reshape(pl_.rows, both.shape[2])]
    all_to_all x2 -> x1, starting transfers between devices: 30.7 us -> 6.84 us  [to_clip(): return lax.all_to_all(both, 'tensor', 0, 0).reshape(pl_.rows, both.shape[2])]
    all_to_all x2 -> x3, waiting for transfers between devices: 41.5 us -> 57.7 us  [the longest x2 44.9 us: from_clip(): return lax.all_to_all(sent, 'tensor', 0, 0)]
    ppermute x2, waiting for transfers between devices: 57.2 us -> 69.1 us  [pair(): return jnp.stack([v, lax.ppermute(v, 'tensor', perm)])]
    ppermute x2, waiting for transfers between devices: 32.6 us -> 21.7 us  [ring(): out.append(lax.ppermute(out[-1], axis, perm))]
    all_to_all x2 -> x3, starting transfers between devices: 9.92 us -> 19.9 us  [the longest x1 11.5 us: body(): upstream_in = lax.all_to_all(upstream_by, 'tensor', 0, 0)]
    pallas_call x1, Pallas kernels: 52.4 us -> 44.6 us  [attend_back(): pl.pallas_call(kernel, grid=(heads,), in_specs=[head] * (1 + 2 * n) + [pl...]
  transfers between devices with their start and end apart: 33 -> 33, of which waited for: 19 -> 19; matrix products, arithmetic and copies ran while one was open for 8% -> 10% of each run, Pallas kernels for 19% -> 19%
where the time goes in v4:
time: 578 us; the launch traced here: 571 us
  Pallas kernels  211 us (37%)
  waiting for transfers between devices  201 us (35%)
  starting transfers between devices  53.6 us (9%)
  other arithmetic  45.7 us (8%)
  local copies, waits for them, and re-layouts  36.6 us (6%)
  between operations  15.3 us (3%)
    ppermute x2, waiting for transfers between devices, pair(): return jnp.stack([v, lax.ppermute(v, 'tensor', perm)])  69.1 us
    pallas_call x1, Pallas kernels, feed(): pl.pallas_call(feed_kernel, grid=(blocks // step,), in_specs=[whole((rows...  59.7 us
    all_to_all x2, waiting for transfers between devices, from_clip(): return lax.all_to_all(sent, 'tensor', 0, 0)  44.9 us
    pallas_call x1, Pallas kernels, attend_back(): pl.pallas_call(kernel, grid=(heads,), in_specs=[head] * (1 + 2 * n) + [pl...  44.6 us
    pallas_call x1, Pallas kernels, attend(): pl.pallas_call(kernel, grid=(heads,), in_specs=[head] * (1 + 2 * n) + [pl...  35.3 us
    pallas_call x1, Pallas kernels, finish(): pl.pallas_call(finish_kernel, grid=(rows // size,), in_specs=[by_rows(siz...  25 us
    ppermute x6, waiting for transfers between devices, line(): line.append(lax.ppermute(line[-1], 'tensor', perm))  24.3 us
    ppermute x2, waiting for transfers between devices, ring(): out.append(lax.ppermute(out[-1], axis, perm))  21.7 us
  transfers between devices with their start and end apart: 33, of which 19 were waited for; matrix products, arithmetic and copies ran while one was open for 10% of the time, Pallas kernels for 19%

profile of v4, /device:TPU:0, one launch (start us, length us, event | category | flops | bytes accessed | tf_op | source)
XLA Modules:
  0.0 570.6 jit_solution(11857396051941062587)
XLA Ops:
  9.2 4.2 all-to-all-start
  16.2 5.8 %all-to-all-done = bf16[4,160,320]{2,1,0:T(8,128)(2,1)S(1)} async-done(((bf16[4,160,320]{2,1,0:T(8,128)(2,1)}), bf16[4,160,320]{2,1,0:T(8,128)(2,1)S(1)}, u32[]{:S(2)}, u32[]{:S(2)}) %all-to-all-start) | async-done | bytes 409632 | tf_op jit(solution)/shard_map/all_to_all | solution.py:765
  21.9 3.5 all-to-all-start.1
  31.0 8.2 %all-to-all-done.1 = bf16[2,640,320]{2,0,1:T(2,128)(2,1)S(1)} async-done(((bf16[2,640,320]{2,0,1:T(2,128)(2,1)}), bf16[2,640,320]{2,0,1:T(2,128)(2,1)S(1)}, u32[]{:S(2)}, u32[]{:S(2)}) %all-to-all-start.1) | async-done | bytes 819232 | tf_op jit(solution)/shard_map/all_to_all | solution.py:771
  46.6 5.1 all-gather.2
  54.0 7.1 %collective-permute-done.2 = bf16[80,1408]{1,0:T(8,128)(2,1)} collective-permute-done((bf16[80,1408]{1,0:T(8,128)(2,1)}, bf16[80,1408]{1,0:T(8,128)(2,1)}, u32[]{:S(2)}, u32[]{:S(2)}) %collective-permute-start.2) | collective-permute-done | bytes 225312 | tf_op jit(solution)/shard_map/ppermute | solution.py:124
  63.7 7.0 %collective-permute-done.5 = bf16[80,1408]{1,0:T(8,128)(2,1)S(1)} collective-permute-done((bf16[80,1408]{1,0:T(8,128)(2,1)}, bf16[80,1408]{1,0:T(8,128)(2,1)S(1)}, u32[]{:S(2)}, u32[]{:S(2)}) %collective-permute-start.5) | collective-permute-done | bytes 225312 | tf_op jit(solution)/shard_map/ppermute | solution.py:124
  72.9 7.0 %collective-permute-done.3 = bf16[80,1408]{1,0:T(8,128)(2,1)S(1)} collective-permute-done((bf16[80,1408]{1,0:T(8,128)(2,1)}, bf16[80,1408]{1,0:T(8,128)(2,1)S(1)}, u32[]{:S(2)}, u32[]{:S(2)}) %collective-permute-start.3) | collective-permute-done | bytes 225312 | tf_op jit(solution)/shard_map/ppermute | solution.py:124
  85.6 6.8 %all-to-all-start.2 = ((bf16[8,96,1280]{2,1,0:T(8,128)(2,1)}), bf16[8,96,1280]{2,1,0:T(8,128)(2,1)S(1)}, u32[]{:S(2)}, u32[]{:S(2)}) async-start(bf16[8,96,1280]{2,1,0:T(8,128)(2,1)} %bitcast.327), calls=%async_computation.2 | async-start | bytes 3932160 | tf_op jit(solution)/shard_map/all_to_all | solution.py:73
  92.4 21.7 %collective-permute-done.9 = bf16[4,80,1408]{2,1,0:T(8,128)(2,1)} collective-permute-done((bf16[4,80,1408]{2,1,0:T(8,128)(2,1)}, bf16[4,80,1408]{2,1,0:T(8,128)(2,1)}, u32[]{:S(2)}, u32[]{:S(2)}) %collective-permute-start.9) | collective-permute-done | bytes 901152 | tf_op jit(solution)/shard_map/ppermute | solution.py:109
  114.2 3.5 fusion.58
  119.2 11.9 %collective-permute-done.7 = bf16[4,80,1408]{2,1,0:T(8,128)(2,1)} collective-permute-done((bf16[4,80,1408]{2,1,0:T(8,128)(2,1)S(1)}, bf16[4,80,1408]{2,1,0:T(8,128)(2,1)}, u32[]{:S(2)}, u32[]{:S(2)}) %collective-permute-start.7) | collective-permute-done | bytes 901152 | tf_op jit(solution)/shard_map/ppermute | solution.py:132
  131.1 3.4 fusion.59
  138.3 3.2 pad_maximum_fusion.3
  141.5 57.2 %collective-permute-done.10 = bf16[2,4,80,1408]{3,2,1,0:T(8,128)(2,1)} collective-permute-done((bf16[2,4,80,1408]{3,2,1,0:T(8,128)(2,1)}, bf16[2,4,80,1408]{3,2,1,0:T(8,128)(2,1)}, u32[]{:S(2)}, u32[]{:S(2)}) %collective-permute-start.10) | collective-permute-done | bytes 1802272 | tf_op jit(solution)/shard_map/ppermute | solution.py:132
  198.7 3.9 pad_maximum_fusion.1
  202.6 3.9 pad_maximum_fusion
  213.2 5.5 collective-permute-done.13
  218.8 17.9 %project.1 = (bf16[1280,768]{1,0:T(8,128)(2,1)}, bf16[1280,768]{1,0:T(8,128)(2,1)}, bf16[1280,768]{1,0:T(8,128)(2,1)}, bf16[3,16,768]{2,1,0:T(8,128)(2,1)}) custom-call(bf16[768,1280]{1,0:T(8,128)(2,1)} %bitcast.320, f32[1,1280]{1,0:T(1,128)} %broadcast_in_dim.89.gain_ref, bf16[3,1280,128]{2,1,0:T(8,128)(2,1)} %copy.233.a_ref, ...), custom_call_target="tpu_custom_call" | custom-call | flops 7549747200 | bytes 9830400 | tf_op jit(solution)/shard_map/project/pallas_call | solution.py:424
  237.3 11.5 %all-to-all-start.3 = ((bf16[8,112,1280]{2,1,0:T(8,128)(2,1)}), bf16[8,112,1280]{2,1,0:T(8,128)(2,1)S(1)}, u32[]{:S(2)}, u32[]{:S(2)}) async-start(bf16[8,112,1280]{2,1,0:T(8,128)(2,1)} %pad_maximum_fusion.3), calls=%async_computation.3 | async-start | bytes 4587520 | tf_op jit(solution)/shard_map/all_to_all | solution.py:793
  253.2 35.3 %attend_forward.1 = (bf16[1280,768]{1,0:T(8,128)(2,1)}, bf16[16,1536,768]{2,1,0:T(8,128)(2,1)}, f32[16,1,768]{2,1,0:T(1,128)}) custom-call(bf16[1280,768]{1,0:T(8,128)(2,1)} %get-tuple-element.68.refs_0_, bf16[1280,768]{1,0:T(8,128)(2,1)} %get-tuple-element.69.refs_1_, bf16[1280,768]{1,0:T(8,128)(2,1)} %collective-permute-done.14.refs_2_, ...), custom_call_target="tpu_custom_call" | custom-call | flops 19327352832 | bytes 5898240 | tf_op jit(solution)/shard_map/attend_forward/pallas_call | solution.py:239
  288.4 11.9 %leave_attention.1 = (f32[768,1280]{1,0:T(8,128)}, bf16[768,1408]{1,0:T(8,128)(2,1)}, bf16[2,16,768]{2,1,0:T(8,128)(2,1)}) custom-call(bf16[1280,768]{1,0:T(8,128)(2,1)} %get-tuple-element.71.mixed_ref.refs_7_, bf16[768,1280]{1,0:T(8,128)(2,1)} %bitcast.321, bf16[128,1280]{1,0:T(8,128)(2,1)} %bitcast.339, bf16[1280,128]{1,0:T(8,128)(2,1)} %copy.234.a1_ref, ...), custom_call_target="tpu_custom_call" | custom-call | flops 5033164800 | bytes 3276800 | tf_op jit(solution)/shard_map/leave_attention/pallas_call | solution.py:481
  300.4 12.8 %all-to-all-done.3 = bf16[8,112,1280]{2,1,0:T(8,128)(2,1)S(1)} async-done(((bf16[8,112,1280]{2,1,0:T(8,128)(2,1)}), bf16[8,112,1280]{2,1,0:T(8,128)(2,1)S(1)}, u32[]{:S(2)}, u32[]{:S(2)}) %all-to-all-start.3) | async-done | bytes 2293792 | tf_op jit(solution)/shard_map/all_to_all | solution.py:793
  316.5 59.7 %feed_forward.1 = (f32[768,1408]{1,0:T(8,128)}, f32[768,1408]{1,0:T(8,128)}, f32[16,5120]{1,0:T(8,128)}, f32[16,5120]{1,0:T(8,128)}) custom-call(bf16[768,1408]{1,0:T(8,128)(2,1)} %get-tuple-element.76.x_ref.n2_ref, bf16[768,1280]{1,0:T(8,128)(2,1)} %bitcast.328, f32[768,1]{1,0:T(8,128)} %reshape.795.live_ref, bf16[128,1280]{1,0:T(8,128)(2,1)} %bitcast.354, ...), custom_call_target="tpu_custom_call" | custom-call | flops 44291850240 | bytes 28835840 | tf_op jit(solution)/shard_map/feed_forward/pallas_call | solution.py:554
  376.2 16.4 %turn.1 = (bf16[768,1280]{1,0:T(8,128)(2,1)}, f32[768,1280]{1,0:T(8,128)}, bf16[1280,768]{1,0:T(8,128)(2,1)}, f32[4,16,1280]{2,1,0:T(8,128)}) custom-call(f32[768,1408]{1,0:T(8,128)} %get-tuple-element.80.acc1_ref, f32[768,1408]{1,0:T(8,128)} %get-tuple-element.81.acc2_ref, f32[768,1280]{1,0:T(8,128)} %get-tuple-element.82.hidden_ref, ...), custom_call_target="tpu_custom_call" | custom-call | flops 5033164800 | bytes 15728640 | tf_op jit(solution)/shard_map/turn/pallas_call | solution.py:621
  399.1 3.6 all-to-all-start.4
  402.7 44.6 %attend_backward.1 = (bf16[1280,768]{1,0:T(8,128)(2,1)}, bf16[1280,768]{1,0:T(8,128)(2,1)}, bf16[1280,768]{1,0:T(8,128)(2,1)}, bf16[1280,768]{1,0:T(8,128)(2,1)}, bf16[1280,768]{1,0:T(8,128)(2,1)}) custom-call(bf16[1280,768]{1,0:T(8,128)(2,1)} %get-tuple-element.68.refs_0_, bf16[1280,768]{1,0:T(8,128)(2,1)} %get-tuple-element.69.refs_1_, ...), custom_call_target="tpu_custom_call" | custom-call | flops 38654705664 | bytes 11796480 | tf_op jit(solution)/shard_map/attend_backward/pallas_call | solution.py:306
  447.9 11.1 %all-to-all-done.4 = bf16[8,120,1280]{2,1,0:T(8,128)(2,1)S(1)} async-done(((bf16[8,120,1280]{2,1,0:T(8,128)(2,1)}), bf16[8,120,1280]{2,1,0:T(8,128)(2,1)S(1)}, u32[]{:S(2)}, u32[]{:S(2)}) %all-to-all-start.4) | async-done | bytes 2457632 | tf_op jit(solution)/shard_map/all_to_all | solution.py:80
  458.9 25.0 %finish.1 = (bf16[768,1280]{1,0:T(8,128)(2,1)}, f32[2,3,16,1280]{3,2,1,0:T(8,128)}) custom-call(bf16[768,1280]{1,0:T(8,128)(2,1)} %bitcast.322, f32[768,1280]{1,0:T(8,128)} %get-tuple-element.83.dhidden_ref, f32[1,1280]{1,0:T(1,128)} %broadcast_in_dim.89.gain_ref, bf16[3,1280,128]{2,1,0:T(8,128)(2,1)} %copy.233.a_ref, f32[3,1,128]{2,1,0:T(1,128)} %slice.195.mark_ref, ...), custom_call_target="tpu_custom_call" | custom-call | flops 7549747200 | bytes 9830400 | tf_op jit(solution)/shard_map/finish/pallas_call | solution.py:701
  493.0 4.7 all-to-all-start.5
  503.6 3.7 collective-permute-done.24
  515.9 33.8 %all-to-all-done.5 = bf16[8,108,1280]{2,1,0:T(8,128)(2,1)} async-done(((bf16[8,108,1280]{2,1,0:T(8,128)(2,1)}), bf16[8,108,1280]{2,1,0:T(8,128)(2,1)}, u32[]{:S(2)}, u32[]{:S(2)}) %all-to-all-start.5) | async-done | bytes 2211872 | tf_op jit(solution)/shard_map/all_to_all | solution.py:80
  (276 shorter events, 94.5 us)
Async XLA Ops:
  9.2 12.7 %all-to-all-start = ((bf16[4,160,320]{2,1,0:T(8,128)(2,1)}), bf16[4,160,320]{2,1,0:T(8,128)(2,1)S(1)}, u32[]{:S(2)}, u32[]{:S(2)}) async-start(bf16[4,160,320]{2,1,0:T(8,128)(2,1)} %pad_maximum_fusion.13), calls=%async_computation | async-start | bytes 983040 | tf_op jit(solution)/shard_map/all_to_all | solution.py:765
  21.9 17.2 %all-to-all-start.1 = ((bf16[2,640,320]{2,0,1:T(2,128)(2,1)}), bf16[2,640,320]{2,0,1:T(2,128)(2,1)S(1)}, u32[]{:S(2)}, u32[]{:S(2)}) async-start(bf16[2,640,320]{2,0,1:T(2,128)(2,1)} %copy.221), calls=%async_computation.1 | async-start | bytes 1966080 | tf_op jit(solution)/shard_map/all_to_all | solution.py:771
  25.5 291.0 %all-gather.5.cloned.1.call-start = ((), (), s32[]{:S(2)}) async-start(), calls=%async_computation.6 | async-start | bytes 27033600 | tf_op jit(solution)/shard_map/all_gather | solution.py:778
  27.2 14.3 %collective-permute-start = (bf16[80,1408]{1,0:T(8,128)(2,1)S(1)}, bf16[80,1408]{1,0:T(8,128)(2,1)}, u32[]{:S(2)}, u32[]{:S(2)}) collective-permute-start(bf16[80,1408]{1,0:T(8,128)(2,1)S(1)} %get-tuple-element.57), channel_id=1, source_target_pairs={{0,2},{1,3},{2,4},{3,5},{4,6},{5,7},{6,0},{7,1},{8,10},{9,11},{10,... | collective-permute-start | bytes 675848 | tf_op jit(solution)/shard_map/ppermute | solution.py:124
  29.5 13.0 %collective-permute-start.1 = (bf16[80,1408]{1,0:T(8,128)(2,1)}, bf16[80,1408]{1,0:T(8,128)(2,1)}, u32[]{:S(2)}, u32[]{:S(2)}) collective-permute-start(bf16[80,1408]{1,0:T(8,128)(2,1)} %get-tuple-element.59), channel_id=1, source_target_pairs={{0,2},{1,3},{2,4},{3,5},{4,6},{5,7},{6,0},{7,1},{8,10},{9,11},{10,... | collective-permute-start | bytes 675848 | tf_op jit(solution)/shard_map/ppermute | solution.py:124
  43.6 18.4 %collective-permute-start.6 = (bf16[4,1,96,1280]{3,2,0,1:T(8,128)(2,1)}, bf16[4,1,96,1280]{3,2,0,1:T(8,128)(2,1)S(1)}, u32[]{:S(2)}, u32[]{:S(2)}) collective-permute-start(bf16[4,1,96,1280]{3,2,0,1:T(8,128)(2,1)} %select_bitcast_fusion.3), channel_id=1, source_target_pairs={{0,8},{8,0},{16,24},{24,16},{1,9},{9,1},{17,25},{25,17},{2,10},{10... | collective-permute-start | bytes 2949128 | tf_op jit(solution)/shard_map/ppermute | solution.py:53
  43.6 10.4 %collective-permute-start.4 = (bf16[80,1408]{1,0:T(8,128)(2,1)}, bf16[80,1408]{1,0:T(8,128)(2,1)}, u32[]{:S(2)}, u32[]{:S(2)}) collective-permute-start(bf16[80,1408]{1,0:T(8,128)(2,1)} %collective-permute-done.1), channel_id=1, source_target_pairs={{0,2},{1,3},{2,4},{3,5},{4,6},{5,7},{6,0},{7,1},{8,10},{9,11},{10,... | collective-permute-start | bytes 675848 | tf_op jit(solution)/shard_map/ppermute | solution.py:124
  44.9 16.2 %collective-permute-start.2 = (bf16[80,1408]{1,0:T(8,128)(2,1)}, bf16[80,1408]{1,0:T(8,128)(2,1)}, u32[]{:S(2)}, u32[]{:S(2)}) collective-permute-start(bf16[80,1408]{1,0:T(8,128)(2,1)} %collective-permute-done), channel_id=1, source_target_pairs={{0,2},{1,3},{2,4},{3,5},{4,6},{5,7},{6,0},{7,1},{8,10},{9,11},{10,... | collective-permute-start | bytes 675848 | tf_op jit(solution)/shard_map/ppermute | solution.py:124
  54.0 16.7 %collective-permute-start.5 = (bf16[80,1408]{1,0:T(8,128)(2,1)}, bf16[80,1408]{1,0:T(8,128)(2,1)S(1)}, u32[]{:S(2)}, u32[]{:S(2)}) collective-permute-start(bf16[80,1408]{1,0:T(8,128)(2,1)} %collective-permute-done.4), channel_id=1, source_target_pairs={{0,2},{1,3},{2,4},{3,5},{4,6},{5,7},{6,0},{7,1},{8,10},{9,11},{10,... | collective-permute-start | bytes 675848 | tf_op jit(solution)/shard_map/ppermute | solution.py:124
  61.1 18.8 %collective-permute-start.3 = (bf16[80,1408]{1,0:T(8,128)(2,1)}, bf16[80,1408]{1,0:T(8,128)(2,1)S(1)}, u32[]{:S(2)}, u32[]{:S(2)}) collective-permute-start(bf16[80,1408]{1,0:T(8,128)(2,1)} %collective-permute-done.2), channel_id=1, source_target_pairs={{0,2},{1,3},{2,4},{3,5},{4,6},{5,7},{6,0},{7,1},{8,10},{9,11},{10,... | collective-permute-start | bytes 675848 | tf_op jit(solution)/shard_map/ppermute | solution.py:124
  81.1 33.1 %collective-permute-start.9 = (bf16[4,80,1408]{2,1,0:T(8,128)(2,1)}, bf16[4,80,1408]{2,1,0:T(8,128)(2,1)}, u32[]{:S(2)}, u32[]{:S(2)}) collective-permute-start(bf16[4,80,1408]{2,1,0:T(8,128)(2,1)} %pad_maximum_fusion.11), channel_id=1, source_target_pairs={{0,16},{8,24},{16,0},{24,8},{1,17},{9,25},{17,1},{25,9},{2,18},{10... | collective-permute-start | bytes 2703368 | tf_op jit(solution)/shard_map/ppermute | solution.py:109
  83.0 48.1 %collective-permute-start.7 = (bf16[4,80,1408]{2,1,0:T(8,128)(2,1)S(1)}, bf16[4,80,1408]{2,1,0:T(8,128)(2,1)}, u32[]{:S(2)}, u32[]{:S(2)}) collective-permute-start(bf16[4,80,1408]{2,1,0:T(8,128)(2,1)S(1)} %pad_maximum_fusion.10), channel_id=1, source_target_pairs={{0,1},{1,0},{2,3},{3,2},{4,5},{5,4},{6,7},{7,6},{8,9},{9,8},{10,11... | collective-permute-start | bytes 2703368 | tf_op jit(solution)/shard_map/ppermute | solution.py:132
  85.6 48.9 %collective-permute-start.11 = (bf16[4,1,96,1280]{3,2,0,1:T(8,128)(2,1)}, bf16[4,1,96,1280]{3,2,0,1:T(8,128)(2,1)}, u32[]{:S(2)}, u32[]{:S(2)}) collective-permute-start(bf16[4,1,96,1280]{3,2,0,1:T(8,128)(2,1)} %select_bitcast_fusion.2), channel_id=1, source_target_pairs={{0,8},{8,0},{16,24},{24,16},{1,9},{9,1},{17,25},{25,17},{2,10},{10... | collective-permute-start | bytes 2949128 | tf_op jit(solution)/shard_map/ppermute | solution.py:53
  85.6 120.9 %all-to-all-start.2 = ((bf16[8,96,1280]{2,1,0:T(8,128)(2,1)}), bf16[8,96,1280]{2,1,0:T(8,128)(2,1)S(1)}, u32[]{:S(2)}, u32[]{:S(2)}) async-start(bf16[8,96,1280]{2,1,0:T(8,128)(2,1)} %bitcast.327), calls=%async_computation.2 | async-start | bytes 3932160 | tf_op jit(solution)/shard_map/all_to_all | solution.py:73
  117.7 81.0 %collective-permute-start.10 = (bf16[2,4,80,1408]{3,2,1,0:T(8,128)(2,1)}, bf16[2,4,80,1408]{3,2,1,0:T(8,128)(2,1)}, u32[]{:S(2)}, u32[]{:S(2)}) collective-permute-start(bf16[2,4,80,1408]{3,2,1,0:T(8,128)(2,1)} %get-tuple-element.166), channel_id=1, source_target_pairs={{0,1},{1,0},{2,3},{3,2},{4,5},{5,4},{6,7},{7,6},{8,9},{9,8},{10,11... | collective-permute-start | bytes 5406728 | tf_op jit(solution)/shard_map/ppermute | solution.py:132
  134.5 68.1 %collective-permute-start.8 = (bf16[2,4,80,1408]{3,2,1,0:T(8,128)(2,1)}, bf16[2,4,80,1408]{3,2,1,0:T(8,128)(2,1)}, u32[]{:S(2)}, u32[]{:S(2)}) collective-permute-start(bf16[2,4,80,1408]{3,2,1,0:T(8,128)(2,1)} %get-tuple-element.168), channel_id=1, source_target_pairs={{0,16},{8,24},{16,0},{24,8},{1,17},{9,25},{17,1},{25,9},{2,18},{10... | collective-permute-start | bytes 5406728 | tf_op jit(solution)/shard_map/ppermute | solution.py:109
  206.5 6.7 %collective-permute-start.12 = (bf16[2,2,4,80,1408]{4,3,2,1,0:T(8,128)(2,1)}, bf16[2,2,4,80,1408]{4,3,2,1,0:T(8,128)(2,1)}, u32[]{:S(2)}, u32[]{:S(2)}) collective-permute-start(bf16[2,2,4,80,1408]{4,3,2,1,0:T(8,128)(2,1)} %pad_maximum_fusion), channel_id=1, source_target_pairs={{0,8},{8,0},{16,24},{24,16},{1,9},{9,1},{17,25},{25,17},{2,10},{10... | collective-permute-start | bytes 10813448 | tf_op jit(solution)/shard_map/ppermute | solution.py:53
  206.6 12.2 %collective-permute-start.13 = (bf16[2,2,4,80,1408]{4,3,2,1,0:T(8,128)(2,1)}, bf16[2,2,4,80,1408]{4,3,2,1,0:T(8,128)(2,1)}, u32[]{:S(2)}, u32[]{:S(2)}) collective-permute-start(bf16[2,2,4,80,1408]{4,3,2,1,0:T(8,128)(2,1)} %pad_maximum_fusion.1), channel_id=1, source_target_pairs={{0,8},{8,0},{16,24},{24,16},{1,9},{9,1},{17,25},{25,17},{2,10},{10... | collective-permute-start | bytes 10813448 | tf_op jit(solution)/shard_map/ppermute | solution.py:53
  236.6 16.5 %collective-permute-start.14 = (bf16[1280,768]{1,0:T(8,128)(2,1)}, bf16[1280,768]{1,0:T(8,128)(2,1)}, u32[]{:S(2)}, u32[]{:S(2)}) collective-permute-start(bf16[1280,768]{1,0:T(8,128)(2,1)} %get-tuple-element.69.refs_1_), channel_id=1, source_target_pairs={{0,8},{8,0},{16,24},{24,16},{1,9},{9,1},{17,25},{25,17},{2,10},{10... | collective-permute-start | bytes 5898248 | tf_op jit(solution)/shard_map/ppermute | solution.py:53
  236.8 16.3 %collective-permute-start.15 = (bf16[1280,768]{1,0:T(8,128)(2,1)}, bf16[1280,768]{1,0:T(8,128)(2,1)}, u32[]{:S(2)}, u32[]{:S(2)}) collective-permute-start(bf16[1280,768]{1,0:T(8,128)(2,1)} %get-tuple-element.70.refs_3_), channel_id=1, source_target_pairs={{0,8},{8,0},{16,24},{24,16},{1,9},{9,1},{17,25},{25,17},{2,10},{10... | collective-permute-start | bytes 5898248 | tf_op jit(solution)/shard_map/ppermute | solution.py:53
  237.3 75.8 %all-to-all-start.3 = ((bf16[8,112,1280]{2,1,0:T(8,128)(2,1)}), bf16[8,112,1280]{2,1,0:T(8,128)(2,1)S(1)}, u32[]{:S(2)}, u32[]{:S(2)}) async-start(bf16[8,112,1280]{2,1,0:T(8,128)(2,1)} %pad_maximum_fusion.3), calls=%async_computation.3 | async-start | bytes 4587520 | tf_op jit(solution)/shard_map/all_to_all | solution.py:793
  399.1 59.8 %all-to-all-start.4 = ((bf16[8,120,1280]{2,1,0:T(8,128)(2,1)}), bf16[8,120,1280]{2,1,0:T(8,128)(2,1)S(1)}, u32[]{:S(2)}, u32[]{:S(2)}) async-start(bf16[8,120,1280]{2,1,0:T(8,128)(2,1)} %pad_maximum_fusion.2), calls=%async_computation.4 | async-start | bytes 4915200 | tf_op jit(solution)/shard_map/all_to_all | solution.py:80
  447.3 11.6 %collective-permute-start.16 = (bf16[1280,768]{1,0:T(8,128)(2,1)}, bf16[1280,768]{1,0:T(8,128)(2,1)}, u32[]{:S(2)}, u32[]{:S(2)}) collective-permute-start(bf16[1280,768]{1,0:T(8,128)(2,1)} %get-tuple-element.95), channel_id=1, source_target_pairs={{0,8},{8,0},{16,24},{24,16},{1,9},{9,1},{17,25},{25,17},{2,10},{10... | collective-permute-start | bytes 5898248 | tf_op jit(solution)/shard_map/ppermute | solution.py:53
  447.4 11.6 %collective-permute-start.17 = (bf16[1280,768]{1,0:T(8,128)(2,1)}, bf16[1280,768]{1,0:T(8,128)(2,1)}, u32[]{:S(2)}, u32[]{:S(2)}) collective-permute-start(bf16[1280,768]{1,0:T(8,128)(2,1)} %get-tuple-element.97), channel_id=1, source_target_pairs={{0,8},{8,0},{16,24},{24,16},{1,9},{9,1},{17,25},{25,17},{2,10},{10... | collective-permute-start | bytes 5898248 | tf_op jit(solution)/shard_map/ppermute | solution.py:53
  493.0 56.7 %all-to-all-start.5 = ((bf16[8,108,1280]{2,1,0:T(8,128)(2,1)}), bf16[8,108,1280]{2,1,0:T(8,128)(2,1)}, u32[]{:S(2)}, u32[]{:S(2)}) async-start(bf16[8,108,1280]{2,1,0:T(8,128)(2,1)} %pad_maximum_fusion.4), calls=%async_computation.5 | async-start | bytes 4587520 | tf_op jit(solution)/shard_map/all_to_all | solution.py:80
  501.1 6.2 %collective-permute-start.24 = (bf16[8,4,1920]{2,0,1:T(8,128)(2,1)S(1)}, bf16[8,4,1920]{2,0,1:T(8,128)(2,1)S(1)}, u32[]{:S(2)}, u32[]{:S(2)}) collective-permute-start(bf16[8,4,1920]{2,0,1:T(8,128)(2,1)S(1)} %bitcast.369), channel_id=1, source_target_pairs={{0,16},{8,24},{16,0},{24,8},{1,17},{9,25},{17,1},{25,9},{2,18},{10... | collective-permute-start | bytes 368648 | tf_op jit(solution)/shard_map/ppermute | solution.py:101
  502.9 6.2 %collective-permute-start.25 = (bf16[8,4,1920]{2,0,1:T(8,128)(2,1)S(1)}, bf16[8,4,1920]{2,0,1:T(8,128)(2,1)S(1)}, u32[]{:S(2)}, u32[]{:S(2)}) collective-permute-start(bf16[8,4,1920]{2,0,1:T(8,128)(2,1)S(1)} %bitcast.371), channel_id=1, source_target_pairs={{0,24},{8,16},{16,8},{24,0},{1,25},{9,17},{17,9},{25,1},{2,26},{10... | collective-permute-start | bytes 368648 | tf_op jit(solution)/shard_map/ppermute | solution.py:101
  503.2 10.8 %collective-permute-start.18 = (bf16[4,1,96,1280]{3,2,0,1:T(8,128)(2,1)S(1)}, bf16[4,1,96,1280]{3,2,0,1:T(8,128)(2,1)S(1)}, u32[]{:S(2)}, u32[]{:S(2)}) collective-permute-start(bf16[4,1,96,1280]{3,2,0,1:T(8,128)(2,1)S(1)} %select_bitcast_fusion.1), channel_id=1, source_target_pairs={{0,8},{8,0},{16,24},{24,16},{1,9},{9,1},{17,25},{25,17},{2,10},{10... | collective-permute-start | bytes 2949128 | tf_op jit(solution)/shard_map/ppermute | solution.py:53
  551.2 4.3 collective-permute-start.21
  553.0 3.9 collective-permute-start.22
  553.1 3.8 collective-permute-start.20
  555.2 4.2 collective-permute-start.19
  (26 other events, 518.0 us)
Sparse Core Ops, SparseCore 0:
  42.6 234.2 all-gather.4

commit v5 on v4

--- a/solution.py
+++ b/solution.py
@@ -122,7 +122,7 @@
         for step in range(size // 2 - 1):
             for line in lines:
                 line.append(lax.ppermute(line[-1], "tensor", perm))
-            if step == 0:
+            if step == min(1, size // 2 - 2):
                 lines, between = lax.optimization_barrier((lines, between))
         self.parts = [jnp.stack(line) for line in lines]
         return between
@@ -538,8 +538,8 @@
     acc1_ref[:, width:] += mm_nt(active, l_ref[1])
     acc2_ref[:, :width] += mm(dupper, first)
     acc2_ref[:, width:] += mm_nt(dupper, l_ref[0])
-    ga_ref[...] = mm(ld_ref[...], active)
-    gb_ref[...] = mm(low_ref[1], dupper)
+    ga_ref[...] = mm(ld_ref[...], active).astype(BF)
+    gb_ref[...] = mm(low_ref[1], dupper).astype(BF)
 
 
 def feed(x, upstream, live, b2, marks, sels, low, w, inner):
@@ -567,7 +567,7 @@
         ],
         out_specs=[whole((rows, wide)), whole((rows, wide)), part, part],
         out_shape=[jax.ShapeDtypeStruct((rows, wide), F32)] * 2
-        + [jax.ShapeDtypeStruct((R, blocks * h), F32)] * 2,
+        + [jax.ShapeDtypeStruct((R, blocks * h), BF)] * 2,
         scratch_shapes=[pltpu.VMEM((rows, wide), BF), pltpu.VMEM((R, rows), BF)],
         compiler_params=pltpu.CompilerParams(vmem_limit_bytes=60 * 2**20),
         cost_estimate=pl.CostEstimate(
@@ -581,7 +581,7 @@
     acc1_ref, acc2_ref, hidden_ref, n2_ref, up_ref, live_ref, mixed_ref, bo_ref, a1_ref, b2_ref, gain_ref,
     mark_ref, sel_ref, low_ref, *refs
 ):
-    *w_refs, order_ref, layer_ref, dhidden_ref, dmixed_ref, grad_ref, buf, sems = refs
+    *w_refs, order_ref, layer_ref, dhidden_ref, dmixed_ref, sums_ref, buf, sems, grad_ref = refs
     i = pl.program_id(0)
     width = hidden_ref.shape[1]
 
@@ -612,6 +612,10 @@
         weight_wait(w_refs, buf, sems)
 
     dmixed_ref[...] = mm_nt(buf[...], jnp.concatenate([dattn, low], axis=1)).astype(BF)
+
+    @pl.when(i == pl.num_programs(0) - 1)
+    def _():
+        sums_ref[...] = grad_ref[...].astype(BF)
 
 
 def turn(acc1, acc2, hidden, n2, upstream, live, mixed, bo, a1, b2, gain, marks, sels, low, w):
@@ -643,9 +647,13 @@
             jax.ShapeDtypeStruct((rows, width), BF),
             jax.ShapeDtypeStruct((rows, width), F32),
             jax.ShapeDtypeStruct((width, rows), BF),
-            jax.ShapeDtypeStruct((4, R, width), F32),
-        ],
-        scratch_shapes=[pltpu.VMEM((width, width + AR), BF), pltpu.SemaphoreType.DMA((4,))],
+            jax.ShapeDtypeStruct((4, R, width), BF),
+        ],
+        scratch_shapes=[
+            pltpu.VMEM((width, width + AR), BF),
+            pltpu.SemaphoreType.DMA((4,)),
+            pltpu.VMEM((4, R, width), F32),
+        ],
         compiler_params=pltpu.CompilerParams(vmem_limit_bytes=56 * 2**20),
         cost_estimate=pl.CostEstimate(
             flops=4 * rows * width * width, bytes_accessed=16 * rows * width, transcendentals=0
@@ -657,7 +665,7 @@
 def finish_kernel(
     x_ref, dhidden_ref, gain_ref, a_ref, mark_ref, sel_ref, low_ref, dq_ref, dk_ref, dk2_ref, dv_ref, dv2_ref, *refs
 ):
-    *w_refs, order_ref, out_ref, grad_ref, bufs, sems = refs
+    *w_refs, order_ref, out_ref, sums_ref, bufs, sems, grad_ref = refs
     i = pl.program_id(0)
     width = x_ref.shape[1]
 
@@ -692,6 +700,10 @@
     for j in range(3):
         grad_ref[0, j] += grads[j * R : (j + 1) * R]
     out_ref[...] = (dhidden_ref[...] + norm_back(z, rate, dn1 * gain_ref[...])).astype(BF)
+
+    @pl.when(i == pl.num_programs(0) - 1)
+    def _():
+        sums_ref[...] = grad_ref[...].astype(BF)
 
 
 def finish(x, dhidden, gain, a, marks, sels, low, dq, dk, dk2, dv, dv2, w):
@@ -715,11 +727,12 @@
         out_specs=[by_rows(size, width), whole((2, 3, R, width))],
         out_shape=[
             jax.ShapeDtypeStruct((rows, width), BF),
-            jax.ShapeDtypeStruct((2, 3, R, width), F32),
+            jax.ShapeDtypeStruct((2, 3, R, width), BF),
         ],
         scratch_shapes=[
             pltpu.VMEM((3, width, width + AR), BF),
             pltpu.SemaphoreType.DMA((3, 4)),
+            pltpu.VMEM((2, 3, R, width), F32),
         ],
         compiler_params=pltpu.CompilerParams(vmem_limit_bytes=58 * 2**20),
         cost_estimate=pl.CostEstimate(
@@ -773,12 +786,7 @@
     half = count // 2
     heads_part = Gather(pl_, qkvo[:half], qkvo[half:])
     frames_by, upstream_by = by_chip(pl_, frames), by_chip(pl_, upstream)
-    ffn = heads_part.line(ffn)
-    frames_by, metas = tie([heads_part], frames_by, metas)
-    all_ffn = lax.all_gather(ffn, ("tensor", "dp"))
-    frames_in = to_clip(pl_, frames_by)
-    heads_part.middle()
-    heads_part.last()
+    ffn, metas = heads_part.line((ffn, metas))
     of_plane = jnp.repeat(lax.dynamic_slice_in_dim(metas, d - pl_.core, 2).reshape(2 * C, 7), pl_.Q, axis=0)
     hot_up, hot_down = [(of_plane[:, j, None] == jnp.arange(A)).astype(BF) for j in (5, 6)]
     inner_by = jnp.stack(
@@ -788,9 +796,16 @@
         ],
         axis=1,
     ).reshape(T, -1, W)
-    upstream_by = jnp.concatenate([upstream_by, inner_by], axis=1)
+    frames_by = jnp.concatenate([frames_by, inner_by], axis=1)
+    (frames_by,) = tie([heads_part], frames_by)
+    all_ffn = lax.all_gather(ffn, ("tensor", "dp"))
+    frames_in = lax.all_to_all(frames_by, "tensor", 0, 0)
+    heads_part.middle()
+    heads_part.last()
     frames_in, upstream_by = tie([heads_part], frames_in, upstream_by)
-    upstream_in = lax.all_to_all(upstream_by, "tensor", 0, 0)
+    inner_in = frames_in[:, pl_.S :].reshape(T, 2, R, U).transpose(1, 2, 0, 3).reshape(2, 1, R, T * U)
+    frames_in = frames_in[:, : pl_.S].reshape(pl_.rows, W)
+    upstream_in = to_clip(pl_, upstream_by)
     heads_part.core()
     weights, line = heads_weights(pl_, heads_part.parts)
 
@@ -815,8 +830,6 @@
     bo, a1, b2 = flat_b(out_b), flat_a(fc1_a), flat_b(fc2_b)
     hidden, n2, low2 = leave(mixed, frames_in, bo, a1, gain2, marks, sels, weights)
     hidden, n2, low2, upstream_in = tie([], hidden, n2, low2, upstream_in)
-    inner_in = upstream_in[:, pl_.S :].reshape(T, 2, R, U).transpose(1, 2, 0, 3).reshape(2, 1, R, T * U)
-    upstream_in = upstream_in[:, : pl_.S].reshape(pl_.rows, W)
     inner_in = inner_in * marks[4:].astype(BF).reshape(2, A, R, 1)
     inner_in = inner_in.reshape(2, AR, T * U)
     acc1, acc2, unit_a, unit_b = feed(n2, upstream_in, live, b2, marks, sels, low2, all_ffn, inner_in)

time: 578 us -> 558 us (0.965)
  other arithmetic: 45.7 us -> 30.8 us
    all_to_all x1, waiting for transfers between devices: 0.01 us -> 19.2 us  [to_clip(): return lax.all_to_all(both, 'tensor', 0, 0).reshape(pl_.rows, both.shape[2])]
    all_to_all x1, waiting for transfers between devices: 12.8 us -> 0.01 us  [body(): frames_in = lax.all_to_all(frames_by, 'tensor', 0, 0)]
    ppermute x2, waiting for transfers between devices: 69.1 us -> 79.5 us  [pair(): return jnp.stack([v, lax.ppermute(v, 'tensor', perm)])]
    ppermute x2, waiting for transfers between devices: 21.7 us -> 12.8 us  [ring(): out.append(lax.ppermute(out[-1], axis, perm))]
    all_to_all x1, waiting for transfers between devices: 8.16 us -> 0.01 us  [body(): ffn = lax.all_to_all(ffn, 'dp', 1, 2, tiled=True)]
    all_to_all x1, starting transfers between devices: 11.5 us -> 5.51 us  [body(): frames_in = lax.all_to_all(frames_by, 'tensor', 0, 0)]
  transfers between devices with their start and end apart: 33 -> 33, of which waited for: 19 -> 19; matrix products, arithmetic and copies ran while one was open for 10% -> 9% of each run, Pallas kernels for 19% -> 20%
where the time goes in v5:
time: 558 us; the launch traced here: 551 us
  Pallas kernels  211 us (38%)
  waiting for transfers between devices  201 us (36%)
  starting transfers between devices  48.9 us (9%)
  local copies, waits for them, and re-layouts  36.1 us (6%)
  other arithmetic  30.8 us (6%)
  between operations  15.3 us (3%)
    ppermute x2, waiting for transfers between devices, pair(): return jnp.stack([v, lax.ppermute(v, 'tensor', perm)])  79.5 us
    pallas_call x1, Pallas kernels, feed(): pl.pallas_call(feed_kernel, grid=(blocks // step,), in_specs=[whole((rows...  59.7 us
    all_to_all x2, waiting for transfers between devices, from_clip(): return lax.all_to_all(sent, 'tensor', 0, 0)  45.6 us
    pallas_call x1, Pallas kernels, attend_back(): pl.pallas_call(kernel, grid=(heads,), in_specs=[head] * (1 + 2 * n) + [pl...  44.6 us
    pallas_call x1, Pallas kernels, attend(): pl.pallas_call(kernel, grid=(heads,), in_specs=[head] * (1 + 2 * n) + [pl...  35 us
    ppermute x6, waiting for transfers between devices, line(): line.append(lax.ppermute(line[-1], 'tensor', perm))  25.3 us
    pallas_call x1, Pallas kernels, finish(): pl.pallas_call(finish_kernel, grid=(rows // size,), in_specs=[by_rows(siz...  25.1 us
    all_to_all x1, waiting for transfers between devices, to_clip(): return lax.all_to_all(both, 'tensor', 0, 0).reshape(pl_.rows, both.shape[2])  19.2 us
  transfers between devices with their start and end apart: 33, of which 19 were waited for; matrix products, arithmetic and copies ran while one was open for 9% of the time, Pallas kernels for 20%

profile of v5, /device:TPU:0, one launch (start us, length us, event | category | flops | bytes accessed | tf_op | source)
XLA Modules:
  0.0 550.9 jit_solution(8327452792924509550)
XLA Ops:
  9.2 4.2 all-to-all-start
  13.9 2.6 copy.221
  16.5 5.4 all-to-all-done
  22.0 3.5 all-to-all-start.1
  30.1 6.9 %collective-permute-done = bf16[80,1408]{1,0:T(8,128)(2,1)} collective-permute-done((bf16[80,1408]{1,0:T(8,128)(2,1)S(1)}, bf16[80,1408]{1,0:T(8,128)(2,1)}, u32[]{:S(2)}, u32[]{:S(2)}) %collective-permute-start) | collective-permute-done | bytes 225312 | tf_op jit(solution)/shard_map/ppermute | solution.py:124
  37.1 4.8 collective-permute-done.2
  42.1 5.2 all-gather.2
  55.0 7.7 %collective-permute-done.5 = bf16[80,1408]{1,0:T(8,128)(2,1)S(1)} collective-permute-done((bf16[80,1408]{1,0:T(8,128)(2,1)}, bf16[80,1408]{1,0:T(8,128)(2,1)S(1)}, u32[]{:S(2)}, u32[]{:S(2)}) %collective-permute-start.5) | collective-permute-done | bytes 225312 | tf_op jit(solution)/shard_map/ppermute | solution.py:124
  64.8 4.2 collective-permute-done.4
  73.4 5.5 %all-to-all-start.2 = ((bf16[8,112,1280]{2,1,0:T(8,128)(2,1)}), bf16[8,112,1280]{2,1,0:T(8,128)(2,1)S(1)}, u32[]{:S(2)}, u32[]{:S(2)}) async-start(bf16[8,112,1280]{2,1,0:T(8,128)(2,1)} %pad_maximum_fusion.3), calls=%async_computation.2 | async-start | bytes 4587520 | tf_op jit(solution)/shard_map/all_to_all | solution.py:802
  78.9 3.0 collective-permute-start.9
  85.5 12.8 %collective-permute-done.9 = bf16[4,80,1408]{2,1,0:T(8,128)(2,1)S(1)} collective-permute-done((bf16[4,80,1408]{2,1,0:T(8,128)(2,1)}, bf16[4,80,1408]{2,1,0:T(8,128)(2,1)S(1)}, u32[]{:S(2)}, u32[]{:S(2)}) %collective-permute-start.9) | collective-permute-done | bytes 901152 | tf_op jit(solution)/shard_map/ppermute | solution.py:109
  100.2 36.7 %collective-permute-done.7 = bf16[4,80,1408]{2,1,0:T(8,128)(2,1)S(1)} collective-permute-done((bf16[4,80,1408]{2,1,0:T(8,128)(2,1)S(1)}, bf16[4,80,1408]{2,1,0:T(8,128)(2,1)S(1)}, u32[]{:S(2)}, u32[]{:S(2)}) %collective-permute-start.7) | collective-permute-done | bytes 901152 | tf_op jit(solution)/shard_map/ppermute | solution.py:132
  137.2 4.2 collective-permute-start.8
  143.1 42.8 %collective-permute-done.10 = bf16[2,4,80,1408]{3,2,1,0:T(8,128)(2,1)S(1)} collective-permute-done((bf16[2,4,80,1408]{3,2,1,0:T(8,128)(2,1)S(1)}, bf16[2,4,80,1408]{3,2,1,0:T(8,128)(2,1)S(1)}, u32[]{:S(2)}, u32[]{:S(2)}) %collective-permute-start.10) | collective-permute-done | bytes 1802272 | tf_op jit(solution)/shard_map/ppermute | solution.py:132
  185.8 2.3 pad_maximum_fusion.1
  197.2 5.2 collective-permute-done.13
  202.3 17.9 %project.1 = (bf16[1280,768]{1,0:T(8,128)(2,1)}, bf16[1280,768]{1,0:T(8,128)(2,1)}, bf16[1280,768]{1,0:T(8,128)(2,1)}, bf16[3,16,768]{2,1,0:T(8,128)(2,1)}) custom-call(bf16[768,1280]{1,0:T(8,128)(2,1)} %bitcast.320, f32[1,1280]{1,0:T(1,128)} %broadcast_in_dim.89.gain_ref, bf16[3,1280,128]{2,1,0:T(8,128)(2,1)} %copy.233.a_ref, ...), custom_call_target="tpu_custom_call" | custom-call | flops 7549747200 | bytes 9830400 | tf_op jit(solution)/shard_map/project/pallas_call | solution.py:424
  220.9 4.5 all-to-all-start.3
  231.6 35.0 %attend_forward.1 = (bf16[1280,768]{1,0:T(8,128)(2,1)}, bf16[16,1536,768]{2,1,0:T(8,128)(2,1)}, f32[16,1,768]{2,1,0:T(1,128)}) custom-call(bf16[1280,768]{1,0:T(8,128)(2,1)} %get-tuple-element.72.refs_0_, bf16[1280,768]{1,0:T(8,128)(2,1)} %get-tuple-element.73.refs_1_, bf16[1280,768]{1,0:T(8,128)(2,1)} %collective-permute-done.14.refs_2_, ...), custom_call_target="tpu_custom_call" | custom-call | flops 19327352832 | bytes 5898240 | tf_op jit(solution)/shard_map/attend_forward/pallas_call | solution.py:239
  266.6 11.9 %leave_attention.1 = (f32[768,1280]{1,0:T(8,128)}, bf16[768,1408]{1,0:T(8,128)(2,1)}, bf16[2,16,768]{2,1,0:T(8,128)(2,1)}) custom-call(bf16[1280,768]{1,0:T(8,128)(2,1)} %get-tuple-element.75.mixed_ref.refs_7_, bf16[768,1280]{1,0:T(8,128)(2,1)} %bitcast.321, bf16[128,1280]{1,0:T(8,128)(2,1)} %bitcast.340, bf16[1280,128]{1,0:T(8,128)(2,1)} %copy.234.a1_ref, ...), custom_call_target="tpu_custom_call" | custom-call | flops 5033164800 | bytes 3276800 | tf_op jit(solution)/shard_map/leave_attention/pallas_call | solution.py:481
  278.6 19.2 %all-to-all-done.3 = bf16[8,96,1280]{2,1,0:T(8,128)(2,1)} async-done(((bf16[8,96,1280]{2,1,0:T(8,128)(2,1)}), bf16[8,96,1280]{2,1,0:T(8,128)(2,1)}, u32[]{:S(2)}, u32[]{:S(2)}) %all-to-all-start.3) | async-done | bytes 1966112 | tf_op jit(solution)/shard_map/all_to_all | solution.py:73
  297.9 59.7 %feed_forward.1 = (f32[768,1408]{1,0:T(8,128)}, f32[768,1408]{1,0:T(8,128)}, bf16[16,5120]{1,0:T(8,128)(2,1)}, bf16[16,5120]{1,0:T(8,128)(2,1)}) custom-call(bf16[768,1408]{1,0:T(8,128)(2,1)} %get-tuple-element.80.x_ref.n2_ref, bf16[768,1280]{1,0:T(8,128)(2,1)} %bitcast.61.up_ref, f32[768,1]{1,0:T(8,128)} %reshape.793.live_ref, bf16[128,1280]{1,0:T(8,128)(2,1)} %bitcast.356, ...), custom_call_target="tpu_custom_call" | custom-call | flops 44291850240 | bytes 28835840 | tf_op jit(solution)/shard_map/feed_forward/pallas_call | solution.py:554
  357.6 17.2 %turn.1 = (bf16[768,1280]{1,0:T(8,128)(2,1)}, f32[768,1280]{1,0:T(8,128)}, bf16[1280,768]{1,0:T(8,128)(2,1)}, bf16[4,16,1280]{2,1,0:T(8,128)(2,1)}) custom-call(f32[768,1408]{1,0:T(8,128)} %get-tuple-element.84.acc1_ref, f32[768,1408]{1,0:T(8,128)} %get-tuple-element.85.acc2_ref, f32[768,1280]{1,0:T(8,128)} %get-tuple-element.86.hidden_ref, ...), custom_call_target="tpu_custom_call" | custom-call | flops 5033164800 | bytes 15728640 | tf_op jit(solution)/shard_map/turn/pallas_call | solution.py:625
  380.0 3.6 all-to-all-start.4
  383.6 44.6 %attend_backward.1 = (bf16[1280,768]{1,0:T(8,128)(2,1)}, bf16[1280,768]{1,0:T(8,128)(2,1)}, bf16[1280,768]{1,0:T(8,128)(2,1)}, bf16[1280,768]{1,0:T(8,128)(2,1)}, bf16[1280,768]{1,0:T(8,128)(2,1)}) custom-call(bf16[1280,768]{1,0:T(8,128)(2,1)} %get-tuple-element.72.refs_0_, bf16[1280,768]{1,0:T(8,128)(2,1)} %get-tuple-element.73.refs_1_, ...), custom_call_target="tpu_custom_call" | custom-call | flops 38654705664 | bytes 11796480 | tf_op jit(solution)/shard_map/attend_backward/pallas_call | solution.py:306
  428.8 11.4 %all-to-all-done.4 = bf16[8,120,1280]{2,1,0:T(8,128)(2,1)S(1)} async-done(((bf16[8,120,1280]{2,1,0:T(8,128)(2,1)}), bf16[8,120,1280]{2,1,0:T(8,128)(2,1)S(1)}, u32[]{:S(2)}, u32[]{:S(2)}) %all-to-all-start.4) | async-done | bytes 2457632 | tf_op jit(solution)/shard_map/all_to_all | solution.py:80
  440.2 25.1 %finish.1 = (bf16[768,1280]{1,0:T(8,128)(2,1)}, bf16[2,3,16,1280]{3,2,1,0:T(8,128)(2,1)}) custom-call(bf16[768,1280]{1,0:T(8,128)(2,1)} %bitcast.322, f32[768,1280]{1,0:T(8,128)} %get-tuple-element.87.dhidden_ref, f32[1,1280]{1,0:T(1,128)} %broadcast_in_dim.89.gain_ref, bf16[3,1280,128]{2,1,0:T(8,128)(2,1)} %copy.233.a_ref, f32[3,1,128]{2,1,0:T(1,128)} %slice.190.mark_ref, ...), custom_call_target="tpu_custom_call" | custom-call | flops 7549747200 | bytes 9830400 | tf_op jit(solution)/shard_map/finish/pallas_call | solution.py:713
  470.0 3.1 pad_maximum_fusion.4
  473.1 4.6 all-to-all-start.5
  483.6 3.7 collective-permute-done.24
  495.8 34.2 %all-to-all-done.5 = bf16[8,108,1280]{2,1,0:T(8,128)(2,1)} async-done(((bf16[8,108,1280]{2,1,0:T(8,128)(2,1)}), bf16[8,108,1280]{2,1,0:T(8,128)(2,1)}, u32[]{:S(2)}, u32[]{:S(2)}) %all-to-all-start.5) | async-done | bytes 2211872 | tf_op jit(solution)/shard_map/all_to_all | solution.py:80
  (266 shorter events, 83.1 us)
Async XLA Ops:
  9.2 12.7 %all-to-all-start = ((bf16[4,160,320]{2,1,0:T(8,128)(2,1)}), bf16[4,160,320]{2,1,0:T(8,128)(2,1)S(1)}, u32[]{:S(2)}, u32[]{:S(2)}) async-start(bf16[4,160,320]{2,1,0:T(8,128)(2,1)} %pad_maximum_fusion.13), calls=%async_computation | async-start | bytes 983040 | tf_op jit(solution)/shard_map/all_to_all | solution.py:778
  22.0 25.2 %all-to-all-start.1 = ((bf16[2,640,320]{2,0,1:T(2,128)(2,1)}), bf16[2,640,320]{2,0,1:T(2,128)(2,1)S(1)}, u32[]{:S(2)}, u32[]{:S(2)}) async-start(bf16[2,640,320]{2,0,1:T(2,128)(2,1)} %copy.221), calls=%async_computation.1 | async-start | bytes 1966080 | tf_op jit(solution)/shard_map/all_to_all | solution.py:784
  25.5 272.4 %all-gather.5.cloned.1.call-start = ((), (), s32[]{:S(2)}) async-start(), calls=%async_computation.6 | async-start | bytes 27033600 | tf_op jit(solution)/shard_map/all_gather | solution.py:801
  26.3 10.8 %collective-permute-start = (bf16[80,1408]{1,0:T(8,128)(2,1)S(1)}, bf16[80,1408]{1,0:T(8,128)(2,1)}, u32[]{:S(2)}, u32[]{:S(2)}) collective-permute-start(bf16[80,1408]{1,0:T(8,128)(2,1)S(1)} %get-tuple-element.59), channel_id=1, source_target_pairs={{0,2},{1,3},{2,4},{3,5},{4,6},{5,7},{6,0},{7,1},{8,10},{9,11},{10,... | collective-permute-start | bytes 675848 | tf_op jit(solution)/shard_map/ppermute | solution.py:124
  28.5 13.3 %collective-permute-start.2 = (bf16[80,1408]{1,0:T(8,128)(2,1)S(1)}, bf16[80,1408]{1,0:T(8,128)(2,1)}, u32[]{:S(2)}, u32[]{:S(2)}) collective-permute-start(bf16[80,1408]{1,0:T(8,128)(2,1)S(1)} %get-tuple-element.62), channel_id=1, source_target_pairs={{0,2},{1,3},{2,4},{3,5},{4,6},{5,7},{6,0},{7,1},{8,10},{9,11},{10,... | collective-permute-start | bytes 675848 | tf_op jit(solution)/shard_map/ppermute | solution.py:124
  37.0 12.5 %collective-permute-start.1 = (bf16[80,1408]{1,0:T(8,128)(2,1)}, bf16[80,1408]{1,0:T(8,128)(2,1)}, u32[]{:S(2)}, u32[]{:S(2)}) collective-permute-start(bf16[80,1408]{1,0:T(8,128)(2,1)} %collective-permute-done), channel_id=1, source_target_pairs={{0,2},{1,3},{2,4},{3,5},{4,6},{5,7},{6,0},{7,1},{8,10},{9,11},{10,... | collective-permute-start | bytes 675848 | tf_op jit(solution)/shard_map/ppermute | solution.py:124
  41.9 9.4 %collective-permute-start.3 = (bf16[80,1408]{1,0:T(8,128)(2,1)}, bf16[80,1408]{1,0:T(8,128)(2,1)}, u32[]{:S(2)}, u32[]{:S(2)}) collective-permute-start(bf16[80,1408]{1,0:T(8,128)(2,1)} %collective-permute-done.2), channel_id=1, source_target_pairs={{0,2},{1,3},{2,4},{3,5},{4,6},{5,7},{6,0},{7,1},{8,10},{9,11},{10,... | collective-permute-start | bytes 675848 | tf_op jit(solution)/shard_map/ppermute | solution.py:124
  52.4 17.9 %collective-permute-start.6 = (bf16[4,1,96,1280]{3,2,0,1:T(8,128)(2,1)}, bf16[4,1,96,1280]{3,2,0,1:T(8,128)(2,1)}, u32[]{:S(2)}, u32[]{:S(2)}) collective-permute-start(bf16[4,1,96,1280]{3,2,0,1:T(8,128)(2,1)} %select_bitcast_fusion.3), channel_id=1, source_target_pairs={{0,8},{8,0},{16,24},{24,16},{1,9},{9,1},{17,25},{25,17},{2,10},{10... | collective-permute-start | bytes 2949128 | tf_op jit(solution)/shard_map/ppermute | solution.py:53
  52.4 10.3 %collective-permute-start.5 = (bf16[80,1408]{1,0:T(8,128)(2,1)}, bf16[80,1408]{1,0:T(8,128)(2,1)S(1)}, u32[]{:S(2)}, u32[]{:S(2)}) collective-permute-start(bf16[80,1408]{1,0:T(8,128)(2,1)} %collective-permute-done.3), channel_id=1, source_target_pairs={{0,2},{1,3},{2,4},{3,5},{4,6},{5,7},{6,0},{7,1},{8,10},{9,11},{10,... | collective-permute-start | bytes 675848 | tf_op jit(solution)/shard_map/ppermute | solution.py:124
  53.4 15.6 %collective-permute-start.4 = (bf16[80,1408]{1,0:T(8,128)(2,1)}, bf16[80,1408]{1,0:T(8,128)(2,1)S(1)}, u32[]{:S(2)}, u32[]{:S(2)}) collective-permute-start(bf16[80,1408]{1,0:T(8,128)(2,1)} %collective-permute-done.1), channel_id=1, source_target_pairs={{0,2},{1,3},{2,4},{3,5},{4,6},{5,7},{6,0},{7,1},{8,10},{9,11},{10,... | collective-permute-start | bytes 675848 | tf_op jit(solution)/shard_map/ppermute | solution.py:124
  73.4 116.9 %all-to-all-start.2 = ((bf16[8,112,1280]{2,1,0:T(8,128)(2,1)}), bf16[8,112,1280]{2,1,0:T(8,128)(2,1)S(1)}, u32[]{:S(2)}, u32[]{:S(2)}) async-start(bf16[8,112,1280]{2,1,0:T(8,128)(2,1)} %pad_maximum_fusion.3), calls=%async_computation.2 | async-start | bytes 4587520 | tf_op jit(solution)/shard_map/all_to_all | solution.py:802
  78.9 19.4 %collective-permute-start.9 = (bf16[4,80,1408]{2,1,0:T(8,128)(2,1)}, bf16[4,80,1408]{2,1,0:T(8,128)(2,1)S(1)}, u32[]{:S(2)}, u32[]{:S(2)}) collective-permute-start(bf16[4,80,1408]{2,1,0:T(8,128)(2,1)} %pad_maximum_fusion.11), channel_id=1, source_target_pairs={{0,16},{8,24},{16,0},{24,8},{1,17},{9,25},{17,1},{25,9},{2,18},{10... | collective-permute-start | bytes 2703368 | tf_op jit(solution)/shard_map/ppermute | solution.py:109
  81.9 55.1 %collective-permute-start.7 = (bf16[4,80,1408]{2,1,0:T(8,128)(2,1)S(1)}, bf16[4,80,1408]{2,1,0:T(8,128)(2,1)S(1)}, u32[]{:S(2)}, u32[]{:S(2)}) collective-permute-start(bf16[4,80,1408]{2,1,0:T(8,128)(2,1)S(1)} %pad_maximum_fusion.10), channel_id=1, source_target_pairs={{0,1},{1,0},{2,3},{3,2},{4,5},{5,4},{6,7},{7,6},{8,9},{9,8},{10,11... | collective-permute-start | bytes 2703368 | tf_op jit(solution)/shard_map/ppermute | solution.py:132
  85.4 56.0 %collective-permute-start.11 = (bf16[4,1,96,1280]{3,2,0,1:T(8,128)(2,1)S(1)}, bf16[4,1,96,1280]{3,2,0,1:T(8,128)(2,1)S(1)}, u32[]{:S(2)}, u32[]{:S(2)}) collective-permute-start(bf16[4,1,96,1280]{3,2,0,1:T(8,128)(2,1)S(1)} %select_bitcast_fusion.2), channel_id=1, source_target_pairs={{0,8},{8,0},{16,24},{24,16},{1,9},{9,1},{17,25},{25,17},{2,10},{10... | collective-permute-start | bytes 2949128 | tf_op jit(solution)/shard_map/ppermute | solution.py:53
  98.5 87.3 %collective-permute-start.10 = (bf16[2,4,80,1408]{3,2,1,0:T(8,128)(2,1)S(1)}, bf16[2,4,80,1408]{3,2,1,0:T(8,128)(2,1)S(1)}, u32[]{:S(2)}, u32[]{:S(2)}) collective-permute-start(bf16[2,4,80,1408]{3,2,1,0:T(8,128)(2,1)S(1)} %get-tuple-element.170), channel_id=1, source_target_pairs={{0,1},{1,0},{2,3},{3,2},{4,5},{5,4},{6,7},{7,6},{8,9},{9,8},{10,11... | collective-permute-start | bytes 5406728 | tf_op jit(solution)/shard_map/ppermute | solution.py:132
  137.2 50.9 %collective-permute-start.8 = (bf16[2,4,80,1408]{3,2,1,0:T(8,128)(2,1)S(1)}, bf16[2,4,80,1408]{3,2,1,0:T(8,128)(2,1)S(1)}, u32[]{:S(2)}, u32[]{:S(2)}) collective-permute-start(bf16[2,4,80,1408]{3,2,1,0:T(8,128)(2,1)S(1)} %get-tuple-element.172), channel_id=1, source_target_pairs={{0,16},{8,24},{16,0},{24,8},{1,17},{9,25},{17,1},{25,9},{2,18},{10... | collective-permute-start | bytes 5406728 | tf_op jit(solution)/shard_map/ppermute | solution.py:109
  190.3 6.9 %collective-permute-start.12 = (bf16[2,2,4,80,1408]{4,3,2,1,0:T(8,128)(2,1)}, bf16[2,2,4,80,1408]{4,3,2,1,0:T(8,128)(2,1)}, u32[]{:S(2)}, u32[]{:S(2)}) collective-permute-start(bf16[2,2,4,80,1408]{4,3,2,1,0:T(8,128)(2,1)} %pad_maximum_fusion), channel_id=1, source_target_pairs={{0,8},{8,0},{16,24},{24,16},{1,9},{9,1},{17,25},{25,17},{2,10},{10... | collective-permute-start | bytes 10813448 | tf_op jit(solution)/shard_map/ppermute | solution.py:53
  190.3 12.0 %collective-permute-start.13 = (bf16[2,2,4,80,1408]{4,3,2,1,0:T(8,128)(2,1)}, bf16[2,2,4,80,1408]{4,3,2,1,0:T(8,128)(2,1)}, u32[]{:S(2)}, u32[]{:S(2)}) collective-permute-start(bf16[2,2,4,80,1408]{4,3,2,1,0:T(8,128)(2,1)} %pad_maximum_fusion.1), channel_id=1, source_target_pairs={{0,8},{8,0},{16,24},{24,16},{1,9},{9,1},{17,25},{25,17},{2,10},{10... | collective-permute-start | bytes 10813448 | tf_op jit(solution)/shard_map/ppermute | solution.py:53
  220.2 11.4 %collective-permute-start.14 = (bf16[1280,768]{1,0:T(8,128)(2,1)}, bf16[1280,768]{1,0:T(8,128)(2,1)}, u32[]{:S(2)}, u32[]{:S(2)}) collective-permute-start(bf16[1280,768]{1,0:T(8,128)(2,1)} %get-tuple-element.73.refs_1_), channel_id=1, source_target_pairs={{0,8},{8,0},{16,24},{24,16},{1,9},{9,1},{17,25},{25,17},{2,10},{10... | collective-permute-start | bytes 5898248 | tf_op jit(solution)/shard_map/ppermute | solution.py:53
  220.4 11.2 %collective-permute-start.15 = (bf16[1280,768]{1,0:T(8,128)(2,1)}, bf16[1280,768]{1,0:T(8,128)(2,1)}, u32[]{:S(2)}, u32[]{:S(2)}) collective-permute-start(bf16[1280,768]{1,0:T(8,128)(2,1)} %get-tuple-element.74.refs_3_), channel_id=1, source_target_pairs={{0,8},{8,0},{16,24},{24,16},{1,9},{9,1},{17,25},{25,17},{2,10},{10... | collective-permute-start | bytes 5898248 | tf_op jit(solution)/shard_map/ppermute | solution.py:53
  220.9 76.9 %all-to-all-start.3 = ((bf16[8,96,1280]{2,1,0:T(8,128)(2,1)}), bf16[8,96,1280]{2,1,0:T(8,128)(2,1)}, u32[]{:S(2)}, u32[]{:S(2)}) async-start(bf16[8,96,1280]{2,1,0:T(8,128)(2,1)} %bitcast.327), calls=%async_computation.3 | async-start | bytes 3932160 | tf_op jit(solution)/shard_map/all_to_all | solution.py:73
  380.0 60.2 %all-to-all-start.4 = ((bf16[8,120,1280]{2,1,0:T(8,128)(2,1)}), bf16[8,120,1280]{2,1,0:T(8,128)(2,1)S(1)}, u32[]{:S(2)}, u32[]{:S(2)}) async-start(bf16[8,120,1280]{2,1,0:T(8,128)(2,1)} %pad_maximum_fusion.2), calls=%async_computation.4 | async-start | bytes 4915200 | tf_op jit(solution)/shard_map/all_to_all | solution.py:80
  428.2 12.0 %collective-permute-start.16 = (bf16[1280,768]{1,0:T(8,128)(2,1)}, bf16[1280,768]{1,0:T(8,128)(2,1)}, u32[]{:S(2)}, u32[]{:S(2)}) collective-permute-start(bf16[1280,768]{1,0:T(8,128)(2,1)} %get-tuple-element.99), channel_id=1, source_target_pairs={{0,8},{8,0},{16,24},{24,16},{1,9},{9,1},{17,25},{25,17},{2,10},{10... | collective-permute-start | bytes 5898248 | tf_op jit(solution)/shard_map/ppermute | solution.py:53
  428.5 11.7 %collective-permute-start.17 = (bf16[1280,768]{1,0:T(8,128)(2,1)}, bf16[1280,768]{1,0:T(8,128)(2,1)}, u32[]{:S(2)}, u32[]{:S(2)}) collective-permute-start(bf16[1280,768]{1,0:T(8,128)(2,1)} %get-tuple-element.101), channel_id=1, source_target_pairs={{0,8},{8,0},{16,24},{24,16},{1,9},{9,1},{17,25},{25,17},{2,10},{10... | collective-permute-start | bytes 5898248 | tf_op jit(solution)/shard_map/ppermute | solution.py:53
  473.1 56.9 %all-to-all-start.5 = ((bf16[8,108,1280]{2,1,0:T(8,128)(2,1)}), bf16[8,108,1280]{2,1,0:T(8,128)(2,1)}, u32[]{:S(2)}, u32[]{:S(2)}) async-start(bf16[8,108,1280]{2,1,0:T(8,128)(2,1)} %pad_maximum_fusion.4), calls=%async_computation.5 | async-start | bytes 4587520 | tf_op jit(solution)/shard_map/all_to_all | solution.py:80
  481.1 6.2 %collective-permute-start.24 = (bf16[8,4,1920]{2,0,1:T(8,128)(2,1)S(1)}, bf16[8,4,1920]{2,0,1:T(8,128)(2,1)S(1)}, u32[]{:S(2)}, u32[]{:S(2)}) collective-permute-start(bf16[8,4,1920]{2,0,1:T(8,128)(2,1)S(1)} %bitcast.373), channel_id=1, source_target_pairs={{0,16},{8,24},{16,0},{24,8},{1,17},{9,25},{17,1},{25,9},{2,18},{10... | collective-permute-start | bytes 368648 | tf_op jit(solution)/shard_map/ppermute | solution.py:101
  482.6 6.5 %collective-permute-start.25 = (bf16[8,4,1920]{2,0,1:T(8,128)(2,1)S(1)}, bf16[8,4,1920]{2,0,1:T(8,128)(2,1)S(1)}, u32[]{:S(2)}, u32[]{:S(2)}) collective-permute-start(bf16[8,4,1920]{2,0,1:T(8,128)(2,1)S(1)} %bitcast.375), channel_id=1, source_target_pairs={{0,24},{8,16},{16,8},{24,0},{1,25},{9,17},{17,9},{25,1},{2,26},{10... | collective-permute-start | bytes 368648 | tf_op jit(solution)/shard_map/ppermute | solution.py:101
  483.2 10.8 %collective-permute-start.18 = (bf16[4,1,96,1280]{3,2,0,1:T(8,128)(2,1)S(1)}, bf16[4,1,96,1280]{3,2,0,1:T(8,128)(2,1)S(1)}, u32[]{:S(2)}, u32[]{:S(2)}) collective-permute-start(bf16[4,1,96,1280]{3,2,0,1:T(8,128)(2,1)S(1)} %select_bitcast_fusion.1), channel_id=1, source_target_pairs={{0,8},{8,0},{16,24},{24,16},{1,9},{9,1},{17,25},{25,17},{2,10},{10... | collective-permute-start | bytes 2949128 | tf_op jit(solution)/shard_map/ppermute | solution.py:53
  531.5 4.3 collective-permute-start.21
  533.0 4.2 collective-permute-start.22
  533.2 4.1 collective-permute-start.20
  535.5 4.2 collective-permute-start.19
  (24 other events, 253.6 us)
Sparse Core Ops, SparseCore 0:
  51.4 246.4 all-gather.4

commit v6 on v5

--- a/solution.py
+++ b/solution.py
@@ -406,8 +406,10 @@
 
     z, _ = norm_parts(x_ref[...].astype(F32))
     n1 = (z * gain_ref[...]).astype(BF)
+    lows = mm(n1, jnp.concatenate([a_ref[j] for j in range(3)], axis=1))
     for j, out_ref in enumerate((q_ref, k_ref, v_ref)):
-        low = (mm(n1, a_ref[j]) * mark_ref[j]).astype(BF)
+        AR = a_ref.shape[2]
+        low = (lows[:, j * AR : (j + 1) * AR] * mark_ref[j]).astype(BF)
         low_ref[j] = mm_nt(sel_ref[j], low).astype(BF)
 
         @pl.when(i == 0)
@@ -477,7 +479,7 @@
 def leave(mixed, x, bo, a1, gain, marks, sels, w):
     rows, width = x.shape
     AR, R = a1.shape[1], sels.shape[1]
-    size = block_of(rows)
+    size = rows
     return pl.pallas_call(
         leave_kernel,
         grid=(rows // size,),

time: 558 us -> 558 us (level)
  no operation moved by 1% of the time
where the time goes in v6:
time: 558 us; the launch traced here: 551 us
  Pallas kernels  210 us (38%)
  waiting for transfers between devices  201 us (36%)
  starting transfers between devices  49.4 us (9%)
  local copies, waits for them, and re-layouts  36.1 us (6%)
  other arithmetic  30.8 us (6%)
  between operations  15.5 us (3%)
    ppermute x2, waiting for transfers between devices, pair(): return jnp.stack([v, lax.ppermute(v, 'tensor', perm)])  79.5 us
    pallas_call x1, Pallas kernels, feed(): pl.pallas_call(feed_kernel, grid=(blocks // step,), in_specs=[whole((rows...  59.5 us
    all_to_all x2, waiting for transfers between devices, from_clip(): return lax.all_to_all(sent, 'tensor', 0, 0)  45.6 us
    pallas_call x1, Pallas kernels, attend_back(): pl.pallas_call(kernel, grid=(heads,), in_specs=[head] * (1 + 2 * n) + [pl...  44.6 us
    pallas_call x1, Pallas kernels, attend(): pl.pallas_call(kernel, grid=(heads,), in_specs=[head] * (1 + 2 * n) + [pl...  35 us
    ppermute x6, waiting for transfers between devices, line(): line.append(lax.ppermute(line[-1], 'tensor', perm))  25.3 us
    pallas_call x1, Pallas kernels, finish(): pl.pallas_call(finish_kernel, grid=(rows // size,), in_specs=[by_rows(siz...  25.1 us
    all_to_all x1, waiting for transfers between devices, to_clip(): return lax.all_to_all(both, 'tensor', 0, 0).reshape(pl_.rows, both.shape[2])  19.8 us
  transfers between devices with their start and end apart: 33, of which 19 were waited for; matrix products, arithmetic and copies ran while one was open for 9% of the time, Pallas kernels for 20%

profile of v6, /device:TPU:0, one launch (start us, length us, event | category | flops | bytes accessed | tf_op | source)
XLA Modules:
  0.0 551.0 jit_solution(5532889658616470131)
XLA Ops:
  9.2 4.2 all-to-all-start
  13.9 2.6 copy.221
  16.5 5.4 all-to-all-done
  22.0 3.5 all-to-all-start.1
  30.1 6.9 %collective-permute-done = bf16[80,1408]{1,0:T(8,128)(2,1)} collective-permute-done((bf16[80,1408]{1,0:T(8,128)(2,1)S(1)}, bf16[80,1408]{1,0:T(8,128)(2,1)}, u32[]{:S(2)}, u32[]{:S(2)}) %collective-permute-start) | collective-permute-done | bytes 225312 | tf_op jit(solution)/shard_map/ppermute | solution.py:124
  37.1 4.8 collective-permute-done.2
  42.1 5.2 all-gather.2
  55.0 7.7 %collective-permute-done.5 = bf16[80,1408]{1,0:T(8,128)(2,1)S(1)} collective-permute-done((bf16[80,1408]{1,0:T(8,128)(2,1)}, bf16[80,1408]{1,0:T(8,128)(2,1)S(1)}, u32[]{:S(2)}, u32[]{:S(2)}) %collective-permute-start.5) | collective-permute-done | bytes 225312 | tf_op jit(solution)/shard_map/ppermute | solution.py:124
  64.8 4.2 collective-permute-done.4
  73.4 5.5 %all-to-all-start.2 = ((bf16[8,112,1280]{2,1,0:T(8,128)(2,1)}), bf16[8,112,1280]{2,1,0:T(8,128)(2,1)S(1)}, u32[]{:S(2)}, u32[]{:S(2)}) async-start(bf16[8,112,1280]{2,1,0:T(8,128)(2,1)} %pad_maximum_fusion.3), calls=%async_computation.2 | async-start | bytes 4587520 | tf_op jit(solution)/shard_map/all_to_all | solution.py:804
  78.9 3.0 collective-permute-start.9
  85.5 12.8 %collective-permute-done.9 = bf16[4,80,1408]{2,1,0:T(8,128)(2,1)S(1)} collective-permute-done((bf16[4,80,1408]{2,1,0:T(8,128)(2,1)}, bf16[4,80,1408]{2,1,0:T(8,128)(2,1)S(1)}, u32[]{:S(2)}, u32[]{:S(2)}) %collective-permute-start.9) | collective-permute-done | bytes 901152 | tf_op jit(solution)/shard_map/ppermute | solution.py:109
  100.2 36.7 %collective-permute-done.7 = bf16[4,80,1408]{2,1,0:T(8,128)(2,1)S(1)} collective-permute-done((bf16[4,80,1408]{2,1,0:T(8,128)(2,1)S(1)}, bf16[4,80,1408]{2,1,0:T(8,128)(2,1)S(1)}, u32[]{:S(2)}, u32[]{:S(2)}) %collective-permute-start.7) | collective-permute-done | bytes 901152 | tf_op jit(solution)/shard_map/ppermute | solution.py:132
  137.2 4.2 collective-permute-start.8
  143.1 42.8 %collective-permute-done.10 = bf16[2,4,80,1408]{3,2,1,0:T(8,128)(2,1)S(1)} collective-permute-done((bf16[2,4,80,1408]{3,2,1,0:T(8,128)(2,1)S(1)}, bf16[2,4,80,1408]{3,2,1,0:T(8,128)(2,1)S(1)}, u32[]{:S(2)}, u32[]{:S(2)}) %collective-permute-start.10) | collective-permute-done | bytes 1802272 | tf_op jit(solution)/shard_map/ppermute | solution.py:132
  185.8 2.3 pad_maximum_fusion.1
  197.2 5.2 collective-permute-done.13
  202.3 17.2 %project.1 = (bf16[1280,768]{1,0:T(8,128)(2,1)}, bf16[1280,768]{1,0:T(8,128)(2,1)}, bf16[1280,768]{1,0:T(8,128)(2,1)}, bf16[3,16,768]{2,1,0:T(8,128)(2,1)}) custom-call(bf16[768,1280]{1,0:T(8,128)(2,1)} %bitcast.320, f32[1,1280]{1,0:T(1,128)} %broadcast_in_dim.89.gain_ref, bf16[3,1280,128]{2,1,0:T(8,128)(2,1)} %copy.233.a_ref, ...), custom_call_target="tpu_custom_call" | custom-call | flops 7549747200 | bytes 9830400 | tf_op jit(solution)/shard_map/project/pallas_call | solution.py:426
  220.3 4.9 all-to-all-start.3
  231.4 35.0 %attend_forward.1 = (bf16[1280,768]{1,0:T(8,128)(2,1)}, bf16[16,1536,768]{2,1,0:T(8,128)(2,1)}, f32[16,1,768]{2,1,0:T(1,128)}) custom-call(bf16[1280,768]{1,0:T(8,128)(2,1)} %get-tuple-element.72.refs_0_, bf16[1280,768]{1,0:T(8,128)(2,1)} %get-tuple-element.73.refs_1_, bf16[1280,768]{1,0:T(8,128)(2,1)} %collective-permute-done.14.refs_2_, ...), custom_call_target="tpu_custom_call" | custom-call | flops 19327352832 | bytes 5898240 | tf_op jit(solution)/shard_map/attend_forward/pallas_call | solution.py:239
  266.4 11.6 %leave_attention.1 = (f32[768,1280]{1,0:T(8,128)}, bf16[768,1408]{1,0:T(8,128)(2,1)}, bf16[2,16,768]{2,1,0:T(8,128)(2,1)}) custom-call(bf16[1280,768]{1,0:T(8,128)(2,1)} %get-tuple-element.75.mixed_ref.refs_7_, bf16[768,1280]{1,0:T(8,128)(2,1)} %bitcast.321, bf16[128,1280]{1,0:T(8,128)(2,1)} %bitcast.340, bf16[1280,128]{1,0:T(8,128)(2,1)} %copy.234.a1_ref, ...), custom_call_target="tpu_custom_call" | custom-call | flops 5033164800 | bytes 3276800 | tf_op jit(solution)/shard_map/leave_attention/pallas_call | solution.py:483
  278.0 19.8 %all-to-all-done.3 = bf16[8,96,1280]{2,1,0:T(8,128)(2,1)} async-done(((bf16[8,96,1280]{2,1,0:T(8,128)(2,1)}), bf16[8,96,1280]{2,1,0:T(8,128)(2,1)}, u32[]{:S(2)}, u32[]{:S(2)}) %all-to-all-start.3) | async-done | bytes 1966112 | tf_op jit(solution)/shard_map/all_to_all | solution.py:73
  297.9 59.5 %feed_forward.1 = (f32[768,1408]{1,0:T(8,128)}, f32[768,1408]{1,0:T(8,128)}, bf16[16,5120]{1,0:T(8,128)(2,1)}, bf16[16,5120]{1,0:T(8,128)(2,1)}) custom-call(bf16[768,1408]{1,0:T(8,128)(2,1)} %get-tuple-element.80.x_ref.n2_ref, bf16[768,1280]{1,0:T(8,128)(2,1)} %bitcast.61.up_ref, f32[768,1]{1,0:T(8,128)} %reshape.793.live_ref, bf16[128,1280]{1,0:T(8,128)(2,1)} %bitcast.356, ...), custom_call_target="tpu_custom_call" | custom-call | flops 44291850240 | bytes 28835840 | tf_op jit(solution)/shard_map/feed_forward/pallas_call | solution.py:556
  357.4 17.2 %turn.1 = (bf16[768,1280]{1,0:T(8,128)(2,1)}, f32[768,1280]{1,0:T(8,128)}, bf16[1280,768]{1,0:T(8,128)(2,1)}, bf16[4,16,1280]{2,1,0:T(8,128)(2,1)}) custom-call(f32[768,1408]{1,0:T(8,128)} %get-tuple-element.84.acc1_ref, f32[768,1408]{1,0:T(8,128)} %get-tuple-element.85.acc2_ref, f32[768,1280]{1,0:T(8,128)} %get-tuple-element.86.hidden_ref, ...), custom_call_target="tpu_custom_call" | custom-call | flops 5033164800 | bytes 15728640 | tf_op jit(solution)/shard_map/turn/pallas_call | solution.py:627
  379.8 3.6 all-to-all-start.4
  383.4 44.6 %attend_backward.1 = (bf16[1280,768]{1,0:T(8,128)(2,1)}, bf16[1280,768]{1,0:T(8,128)(2,1)}, bf16[1280,768]{1,0:T(8,128)(2,1)}, bf16[1280,768]{1,0:T(8,128)(2,1)}, bf16[1280,768]{1,0:T(8,128)(2,1)}) custom-call(bf16[1280,768]{1,0:T(8,128)(2,1)} %get-tuple-element.72.refs_0_, bf16[1280,768]{1,0:T(8,128)(2,1)} %get-tuple-element.73.refs_1_, ...), custom_call_target="tpu_custom_call" | custom-call | flops 38654705664 | bytes 11796480 | tf_op jit(solution)/shard_map/attend_backward/pallas_call | solution.py:306
  428.6 11.4 %all-to-all-done.4 = bf16[8,120,1280]{2,1,0:T(8,128)(2,1)S(1)} async-done(((bf16[8,120,1280]{2,1,0:T(8,128)(2,1)}), bf16[8,120,1280]{2,1,0:T(8,128)(2,1)S(1)}, u32[]{:S(2)}, u32[]{:S(2)}) %all-to-all-start.4) | async-done | bytes 2457632 | tf_op jit(solution)/shard_map/all_to_all | solution.py:80
  440.0 25.1 %finish.1 = (bf16[768,1280]{1,0:T(8,128)(2,1)}, bf16[2,3,16,1280]{3,2,1,0:T(8,128)(2,1)}) custom-call(bf16[768,1280]{1,0:T(8,128)(2,1)} %bitcast.322, f32[768,1280]{1,0:T(8,128)} %get-tuple-element.87.dhidden_ref, f32[1,1280]{1,0:T(1,128)} %broadcast_in_dim.89.gain_ref, bf16[3,1280,128]{2,1,0:T(8,128)(2,1)} %copy.233.a_ref, f32[3,1,128]{2,1,0:T(1,128)} %slice.190.mark_ref, ...), custom_call_target="tpu_custom_call" | custom-call | flops 7549747200 | bytes 9830400 | tf_op jit(solution)/shard_map/finish/pallas_call | solution.py:715
  469.8 3.1 pad_maximum_fusion.4
  472.9 4.6 all-to-all-start.5
  483.4 3.7 collective-permute-done.24
  495.7 34.2 %all-to-all-done.5 = bf16[8,108,1280]{2,1,0:T(8,128)(2,1)} async-done(((bf16[8,108,1280]{2,1,0:T(8,128)(2,1)}), bf16[8,108,1280]{2,1,0:T(8,128)(2,1)}, u32[]{:S(2)}, u32[]{:S(2)}) %all-to-all-start.5) | async-done | bytes 2211872 | tf_op jit(solution)/shard_map/all_to_all | solution.py:80
  (266 shorter events, 83.1 us)
Async XLA Ops:
  9.2 12.7 %all-to-all-start = ((bf16[4,160,320]{2,1,0:T(8,128)(2,1)}), bf16[4,160,320]{2,1,0:T(8,128)(2,1)S(1)}, u32[]{:S(2)}, u32[]{:S(2)}) async-start(bf16[4,160,320]{2,1,0:T(8,128)(2,1)} %pad_maximum_fusion.13), calls=%async_computation | async-start | bytes 983040 | tf_op jit(solution)/shard_map/all_to_all | solution.py:780
  22.0 25.2 %all-to-all-start.1 = ((bf16[2,640,320]{2,0,1:T(2,128)(2,1)}), bf16[2,640,320]{2,0,1:T(2,128)(2,1)S(1)}, u32[]{:S(2)}, u32[]{:S(2)}) async-start(bf16[2,640,320]{2,0,1:T(2,128)(2,1)} %copy.221), calls=%async_computation.1 | async-start | bytes 1966080 | tf_op jit(solution)/shard_map/all_to_all | solution.py:786
  25.5 272.4 %all-gather.5.cloned.1.call-start = ((), (), s32[]{:S(2)}) async-start(), calls=%async_computation.6 | async-start | bytes 27033600 | tf_op jit(solution)/shard_map/all_gather | solution.py:803
  26.3 10.8 %collective-permute-start = (bf16[80,1408]{1,0:T(8,128)(2,1)S(1)}, bf16[80,1408]{1,0:T(8,128)(2,1)}, u32[]{:S(2)}, u32[]{:S(2)}) collective-permute-start(bf16[80,1408]{1,0:T(8,128)(2,1)S(1)} %get-tuple-element.59), channel_id=1, source_target_pairs={{0,2},{1,3},{2,4},{3,5},{4,6},{5,7},{6,0},{7,1},{8,10},{9,11},{10,... | collective-permute-start | bytes 675848 | tf_op jit(solution)/shard_map/ppermute | solution.py:124
  28.5 13.3 %collective-permute-start.2 = (bf16[80,1408]{1,0:T(8,128)(2,1)S(1)}, bf16[80,1408]{1,0:T(8,128)(2,1)}, u32[]{:S(2)}, u32[]{:S(2)}) collective-permute-start(bf16[80,1408]{1,0:T(8,128)(2,1)S(1)} %get-tuple-element.62), channel_id=1, source_target_pairs={{0,2},{1,3},{2,4},{3,5},{4,6},{5,7},{6,0},{7,1},{8,10},{9,11},{10,... | collective-permute-start | bytes 675848 | tf_op jit(solution)/shard_map/ppermute | solution.py:124
  37.0 12.5 %collective-permute-start.1 = (bf16[80,1408]{1,0:T(8,128)(2,1)}, bf16[80,1408]{1,0:T(8,128)(2,1)}, u32[]{:S(2)}, u32[]{:S(2)}) collective-permute-start(bf16[80,1408]{1,0:T(8,128)(2,1)} %collective-permute-done), channel_id=1, source_target_pairs={{0,2},{1,3},{2,4},{3,5},{4,6},{5,7},{6,0},{7,1},{8,10},{9,11},{10,... | collective-permute-start | bytes 675848 | tf_op jit(solution)/shard_map/ppermute | solution.py:124
  41.9 9.4 %collective-permute-start.3 = (bf16[80,1408]{1,0:T(8,128)(2,1)}, bf16[80,1408]{1,0:T(8,128)(2,1)}, u32[]{:S(2)}, u32[]{:S(2)}) collective-permute-start(bf16[80,1408]{1,0:T(8,128)(2,1)} %collective-permute-done.2), channel_id=1, source_target_pairs={{0,2},{1,3},{2,4},{3,5},{4,6},{5,7},{6,0},{7,1},{8,10},{9,11},{10,... | collective-permute-start | bytes 675848 | tf_op jit(solution)/shard_map/ppermute | solution.py:124
  52.4 17.9 %collective-permute-start.6 = (bf16[4,1,96,1280]{3,2,0,1:T(8,128)(2,1)}, bf16[4,1,96,1280]{3,2,0,1:T(8,128)(2,1)}, u32[]{:S(2)}, u32[]{:S(2)}) collective-permute-start(bf16[4,1,96,1280]{3,2,0,1:T(8,128)(2,1)} %select_bitcast_fusion.3), channel_id=1, source_target_pairs={{0,8},{8,0},{16,24},{24,16},{1,9},{9,1},{17,25},{25,17},{2,10},{10... | collective-permute-start | bytes 2949128 | tf_op jit(solution)/shard_map/ppermute | solution.py:53
  52.4 10.3 %collective-permute-start.5 = (bf16[80,1408]{1,0:T(8,128)(2,1)}, bf16[80,1408]{1,0:T(8,128)(2,1)S(1)}, u32[]{:S(2)}, u32[]{:S(2)}) collective-permute-start(bf16[80,1408]{1,0:T(8,128)(2,1)} %collective-permute-done.3), channel_id=1, source_target_pairs={{0,2},{1,3},{2,4},{3,5},{4,6},{5,7},{6,0},{7,1},{8,10},{9,11},{10,... | collective-permute-start | bytes 675848 | tf_op jit(solution)/shard_map/ppermute | solution.py:124
  53.4 15.6 %collective-permute-start.4 = (bf16[80,1408]{1,0:T(8,128)(2,1)}, bf16[80,1408]{1,0:T(8,128)(2,1)S(1)}, u32[]{:S(2)}, u32[]{:S(2)}) collective-permute-start(bf16[80,1408]{1,0:T(8,128)(2,1)} %collective-permute-done.1), channel_id=1, source_target_pairs={{0,2},{1,3},{2,4},{3,5},{4,6},{5,7},{6,0},{7,1},{8,10},{9,11},{10,... | collective-permute-start | bytes 675848 | tf_op jit(solution)/shard_map/ppermute | solution.py:124
  73.4 116.9 %all-to-all-start.2 = ((bf16[8,112,1280]{2,1,0:T(8,128)(2,1)}), bf16[8,112,1280]{2,1,0:T(8,128)(2,1)S(1)}, u32[]{:S(2)}, u32[]{:S(2)}) async-start(bf16[8,112,1280]{2,1,0:T(8,128)(2,1)} %pad_maximum_fusion.3), calls=%async_computation.2 | async-start | bytes 4587520 | tf_op jit(solution)/shard_map/all_to_all | solution.py:804
  78.9 19.4 %collective-permute-start.9 = (bf16[4,80,1408]{2,1,0:T(8,128)(2,1)}, bf16[4,80,1408]{2,1,0:T(8,128)(2,1)S(1)}, u32[]{:S(2)}, u32[]{:S(2)}) collective-permute-start(bf16[4,80,1408]{2,1,0:T(8,128)(2,1)} %pad_maximum_fusion.11), channel_id=1, source_target_pairs={{0,16},{8,24},{16,0},{24,8},{1,17},{9,25},{17,1},{25,9},{2,18},{10... | collective-permute-start | bytes 2703368 | tf_op jit(solution)/shard_map/ppermute | solution.py:109
  81.9 55.1 %collective-permute-start.7 = (bf16[4,80,1408]{2,1,0:T(8,128)(2,1)S(1)}, bf16[4,80,1408]{2,1,0:T(8,128)(2,1)S(1)}, u32[]{:S(2)}, u32[]{:S(2)}) collective-permute-start(bf16[4,80,1408]{2,1,0:T(8,128)(2,1)S(1)} %pad_maximum_fusion.10), channel_id=1, source_target_pairs={{0,1},{1,0},{2,3},{3,2},{4,5},{5,4},{6,7},{7,6},{8,9},{9,8},{10,11... | collective-permute-start | bytes 2703368 | tf_op jit(solution)/shard_map/ppermute | solution.py:132
  85.4 56.0 %collective-permute-start.11 = (bf16[4,1,96,1280]{3,2,0,1:T(8,128)(2,1)S(1)}, bf16[4,1,96,1280]{3,2,0,1:T(8,128)(2,1)S(1)}, u32[]{:S(2)}, u32[]{:S(2)}) collective-permute-start(bf16[4,1,96,1280]{3,2,0,1:T(8,128)(2,1)S(1)} %select_bitcast_fusion.2), channel_id=1, source_target_pairs={{0,8},{8,0},{16,24},{24,16},{1,9},{9,1},{17,25},{25,17},{2,10},{10... | collective-permute-start | bytes 2949128 | tf_op jit(solution)/shard_map/ppermute | solution.py:53
  98.5 87.3 %collective-permute-start.10 = (bf16[2,4,80,1408]{3,2,1,0:T(8,128)(2,1)S(1)}, bf16[2,4,80,1408]{3,2,1,0:T(8,128)(2,1)S(1)}, u32[]{:S(2)}, u32[]{:S(2)}) collective-permute-start(bf16[2,4,80,1408]{3,2,1,0:T(8,128)(2,1)S(1)} %get-tuple-element.170), channel_id=1, source_target_pairs={{0,1},{1,0},{2,3},{3,2},{4,5},{5,4},{6,7},{7,6},{8,9},{9,8},{10,11... | collective-permute-start | bytes 5406728 | tf_op jit(solution)/shard_map/ppermute | solution.py:132
  137.2 50.9 %collective-permute-start.8 = (bf16[2,4,80,1408]{3,2,1,0:T(8,128)(2,1)S(1)}, bf16[2,4,80,1408]{3,2,1,0:T(8,128)(2,1)S(1)}, u32[]{:S(2)}, u32[]{:S(2)}) collective-permute-start(bf16[2,4,80,1408]{3,2,1,0:T(8,128)(2,1)S(1)} %get-tuple-element.172), channel_id=1, source_target_pairs={{0,16},{8,24},{16,0},{24,8},{1,17},{9,25},{17,1},{25,9},{2,18},{10... | collective-permute-start | bytes 5406728 | tf_op jit(solution)/shard_map/ppermute | solution.py:109
  190.3 6.9 %collective-permute-start.12 = (bf16[2,2,4,80,1408]{4,3,2,1,0:T(8,128)(2,1)}, bf16[2,2,4,80,1408]{4,3,2,1,0:T(8,128)(2,1)}, u32[]{:S(2)}, u32[]{:S(2)}) collective-permute-start(bf16[2,2,4,80,1408]{4,3,2,1,0:T(8,128)(2,1)} %pad_maximum_fusion), channel_id=1, source_target_pairs={{0,8},{8,0},{16,24},{24,16},{1,9},{9,1},{17,25},{25,17},{2,10},{10... | collective-permute-start | bytes 10813448 | tf_op jit(solution)/shard_map/ppermute | solution.py:53
  190.3 12.0 %collective-permute-start.13 = (bf16[2,2,4,80,1408]{4,3,2,1,0:T(8,128)(2,1)}, bf16[2,2,4,80,1408]{4,3,2,1,0:T(8,128)(2,1)}, u32[]{:S(2)}, u32[]{:S(2)}) collective-permute-start(bf16[2,2,4,80,1408]{4,3,2,1,0:T(8,128)(2,1)} %pad_maximum_fusion.1), channel_id=1, source_target_pairs={{0,8},{8,0},{16,24},{24,16},{1,9},{9,1},{17,25},{25,17},{2,10},{10... | collective-permute-start | bytes 10813448 | tf_op jit(solution)/shard_map/ppermute | solution.py:53
  219.6 11.8 %collective-permute-start.14 = (bf16[1280,768]{1,0:T(8,128)(2,1)}, bf16[1280,768]{1,0:T(8,128)(2,1)}, u32[]{:S(2)}, u32[]{:S(2)}) collective-permute-start(bf16[1280,768]{1,0:T(8,128)(2,1)} %get-tuple-element.73.refs_1_), channel_id=1, source_target_pairs={{0,8},{8,0},{16,24},{24,16},{1,9},{9,1},{17,25},{25,17},{2,10},{10... | collective-permute-start | bytes 5898248 | tf_op jit(solution)/shard_map/ppermute | solution.py:53
  219.8 11.6 %collective-permute-start.15 = (bf16[1280,768]{1,0:T(8,128)(2,1)}, bf16[1280,768]{1,0:T(8,128)(2,1)}, u32[]{:S(2)}, u32[]{:S(2)}) collective-permute-start(bf16[1280,768]{1,0:T(8,128)(2,1)} %get-tuple-element.74.refs_3_), channel_id=1, source_target_pairs={{0,8},{8,0},{16,24},{24,16},{1,9},{9,1},{17,25},{25,17},{2,10},{10... | collective-permute-start | bytes 5898248 | tf_op jit(solution)/shard_map/ppermute | solution.py:53
  220.3 77.5 %all-to-all-start.3 = ((bf16[8,96,1280]{2,1,0:T(8,128)(2,1)}), bf16[8,96,1280]{2,1,0:T(8,128)(2,1)}, u32[]{:S(2)}, u32[]{:S(2)}) async-start(bf16[8,96,1280]{2,1,0:T(8,128)(2,1)} %bitcast.327), calls=%async_computation.3 | async-start | bytes 3932160 | tf_op jit(solution)/shard_map/all_to_all | solution.py:73
  379.8 60.2 %all-to-all-start.4 = ((bf16[8,120,1280]{2,1,0:T(8,128)(2,1)}), bf16[8,120,1280]{2,1,0:T(8,128)(2,1)S(1)}, u32[]{:S(2)}, u32[]{:S(2)}) async-start(bf16[8,120,1280]{2,1,0:T(8,128)(2,1)} %pad_maximum_fusion.2), calls=%async_computation.4 | async-start | bytes 4915200 | tf_op jit(solution)/shard_map/all_to_all | solution.py:80
  428.0 12.0 %collective-permute-start.16 = (bf16[1280,768]{1,0:T(8,128)(2,1)}, bf16[1280,768]{1,0:T(8,128)(2,1)}, u32[]{:S(2)}, u32[]{:S(2)}) collective-permute-start(bf16[1280,768]{1,0:T(8,128)(2,1)} %get-tuple-element.99), channel_id=1, source_target_pairs={{0,8},{8,0},{16,24},{24,16},{1,9},{9,1},{17,25},{25,17},{2,10},{10... | collective-permute-start | bytes 5898248 | tf_op jit(solution)/shard_map/ppermute | solution.py:53
  428.3 11.7 %collective-permute-start.17 = (bf16[1280,768]{1,0:T(8,128)(2,1)}, bf16[1280,768]{1,0:T(8,128)(2,1)}, u32[]{:S(2)}, u32[]{:S(2)}) collective-permute-start(bf16[1280,768]{1,0:T(8,128)(2,1)} %get-tuple-element.101), channel_id=1, source_target_pairs={{0,8},{8,0},{16,24},{24,16},{1,9},{9,1},{17,25},{25,17},{2,10},{10... | collective-permute-start | bytes 5898248 | tf_op jit(solution)/shard_map/ppermute | solution.py:53
  472.9 56.9 %all-to-all-start.5 = ((bf16[8,108,1280]{2,1,0:T(8,128)(2,1)}), bf16[8,108,1280]{2,1,0:T(8,128)(2,1)}, u32[]{:S(2)}, u32[]{:S(2)}) async-start(bf16[8,108,1280]{2,1,0:T(8,128)(2,1)} %pad_maximum_fusion.4), calls=%async_computation.5 | async-start | bytes 4587520 | tf_op jit(solution)/shard_map/all_to_all | solution.py:80
  480.9 6.2 %collective-permute-start.24 = (bf16[8,4,1920]{2,0,1:T(8,128)(2,1)S(1)}, bf16[8,4,1920]{2,0,1:T(8,128)(2,1)S(1)}, u32[]{:S(2)}, u32[]{:S(2)}) collective-permute-start(bf16[8,4,1920]{2,0,1:T(8,128)(2,1)S(1)} %bitcast.373), channel_id=1, source_target_pairs={{0,16},{8,24},{16,0},{24,8},{1,17},{9,25},{17,1},{25,9},{2,18},{10... | collective-permute-start | bytes 368648 | tf_op jit(solution)/shard_map/ppermute | solution.py:101
  482.5 6.5 %collective-permute-start.25 = (bf16[8,4,1920]{2,0,1:T(8,128)(2,1)S(1)}, bf16[8,4,1920]{2,0,1:T(8,128)(2,1)S(1)}, u32[]{:S(2)}, u32[]{:S(2)}) collective-permute-start(bf16[8,4,1920]{2,0,1:T(8,128)(2,1)S(1)} %bitcast.375), channel_id=1, source_target_pairs={{0,24},{8,16},{16,8},{24,0},{1,25},{9,17},{17,9},{25,1},{2,26},{10... | collective-permute-start | bytes 368648 | tf_op jit(solution)/shard_map/ppermute | solution.py:101
  483.1 10.8 %collective-permute-start.18 = (bf16[4,1,96,1280]{3,2,0,1:T(8,128)(2,1)S(1)}, bf16[4,1,96,1280]{3,2,0,1:T(8,128)(2,1)S(1)}, u32[]{:S(2)}, u32[]{:S(2)}) collective-permute-start(bf16[4,1,96,1280]{3,2,0,1:T(8,128)(2,1)S(1)} %select_bitcast_fusion.1), channel_id=1, source_target_pairs={{0,8},{8,0},{16,24},{24,16},{1,9},{9,1},{17,25},{25,17},{2,10},{10... | collective-permute-start | bytes 2949128 | tf_op jit(solution)/shard_map/ppermute | solution.py:53
  531.3 4.3 collective-permute-start.21
  532.9 4.2 collective-permute-start.22
  533.0 4.1 collective-permute-start.20
  535.4 4.2 collective-permute-start.19
  (24 other events, 254.6 us)
Sparse Core Ops, SparseCore 0:
  51.4 246.4 all-gather.4
